TPU v7x, 32 devices: a whole 2x2x4 slice. The times are simulated.
32 devices in a mesh: dp: 16 (over z, y, core), blk: 2 (over x).
Axes of the slice: x: 2, y: 2, z: 4, core: 2. Of those that a mesh axis runs over, the one named last changes fastest.
Arguments:
- queries: bfloat16 [2, 64, 32, 128], P('blk', 'dp'), may hold values from -6 to 6
- passages: bfloat16 [2, 256, 192, 128], P('blk', 'dp'), may hold values from -6 to 6
- passage_lengths: int32 [2, 256], P('blk', 'dp'), may hold values from 32 to 192
- positives: bfloat16 [2, 64, 192, 128], P('blk', 'dp'), may hold values from -6 to 6
- positive_lengths: int32 [2, 64], P('blk', 'dp'), may hold values from 32 to 192
- owners: int32 [2, 64, 32, 1], P('blk', 'dp'), may hold values from 0 to 15; in each aligned block of 128 rows (0 to 127, 128 to 255, ..., all dimensions but the last counted through in order) at most 16 rows name the same one
- local_ids: int32 [2, 64, 32], P('blk', 'dp'), may hold values from 0 to 15
- teacher: float32 [2, 64, 32], P('blk', 'dp'), may hold values from -12 to 12
Outputs:
- student: float32 [2, 64, 32], P('blk', 'dp')
- distill: float32 [2, 64], P('blk', 'dp')
- contrast: float32 [2, 64], P('blk', 'dp')
Inputs may be any that keep to these rules, and one draw needn't show every extreme that they name: `owners`: among the 128 candidate pairs of the queries of one device, no owner is named more than 16 times, a bound that some block reaches.
All inputs are finite; a program needn't handle non-finite values.
Results may differ from a plain program's by a relative error of at most 0.00062.
Values may be sent and summed in bfloat16 or wider, within the bound.
No kernel may reach another device: no remote copies, remote signals or barrier semaphores. Data moves between devices by JAX's collectives and lax.ppermute only.
A program may use at most 64 MiB of HBM per device.

v0:
```python
import math

import jax
import jax.numpy as jnp
from jax import lax
from jax.sharding import PartitionSpec as P


def unit_rows(values):
    wide = values.astype(jnp.float32)
    total = jnp.sum(wide * wide, axis=-1, keepdims=True) + 1e-06
    return (wide * lax.rsqrt(total)).astype(jnp.bfloat16)


def slot_ranks(destination, peer_count):
    onehot = (destination[:, None] == jnp.arange(peer_count, dtype=jnp.int32)[None, :]).astype(
        jnp.int32
    )
    before = jnp.cumsum(onehot, axis=0) - onehot
    return jnp.sum(before * onehot, axis=1)


def slot_scores(slot_queries, slot_ids, passage_unit, kept_lengths):
    row_count = slot_queries.shape[0]
    block_rows = math.gcd(row_count, 64)
    query_blocks = slot_queries.reshape(
        row_count // block_rows, block_rows, slot_queries.shape[1], slot_queries.shape[2]
    )
    id_blocks = slot_ids.reshape(row_count // block_rows, block_rows)

    def slot_block_relevance(inputs):
        query_tile_rows, id_block = inputs
        document_rows = passage_unit[id_block]
        similarity_matrix = jnp.einsum(
            "uhv,uyv->uhy", query_tile_rows, document_rows, preferred_element_type=jnp.float32
        )
        usable = (
            lax.broadcasted_iota(jnp.int32, (1, 1, document_rows.shape[1]), 2)
            < kept_lengths[id_block][:, None, None]
        )
        return jnp.sum(jnp.max(jnp.where(usable, similarity_matrix, -1000000000.0), axis=2), axis=1)

    return lax.map(slot_block_relevance, (query_blocks, id_blocks)).reshape(row_count)


def cross_scores(query_tile, document_rows, lengths):
    doc_count = document_rows.shape[0]
    block_docs = math.gcd(doc_count, 8)
    doc_blocks = document_rows.reshape(
        doc_count // block_docs, block_docs, document_rows.shape[1], document_rows.shape[2]
    )
    length_blocks = lengths.reshape(doc_count // block_docs, block_docs)

    def cross_block_relevance(inputs):
        document_tile_rows, length_block = inputs
        similarity_matrix = jnp.einsum(
            "aqd,kld->akql", query_tile, document_tile_rows, preferred_element_type=jnp.float32
        )
        usable = (
            lax.broadcasted_iota(jnp.int32, (1, 1, 1, document_tile_rows.shape[1]), 3)
            < length_block[None, :, None, None]
        )
        return jnp.sum(jnp.max(jnp.where(usable, similarity_matrix, -1000000000.0), axis=3), axis=2)

    scored = lax.map(cross_block_relevance, (doc_blocks, length_blocks))
    return jnp.moveaxis(scored, 0, 1).reshape(query_tile.shape[0], doc_count)


def send_back(scored):
    return lax.all_to_all(scored, "dp", split_axis=0, concat_axis=0, tiled=True)


def per_device(
    queries, passages, passage_lengths, positives, positive_lengths, owners, local_ids, teacher
):
    peer_count = lax.axis_size("dp")
    query_unit = unit_rows(queries[0])
    passage_unit = unit_rows(passages[0])
    kept_lengths = passage_lengths[0]
    query_count = query_unit.shape[0]
    cand_count = owners.shape[2]
    capacity = 2 * query_count * cand_count // peer_count
    destination = owners[0, :, :, 0].reshape(-1)
    passage_ids = local_ids[0].reshape(-1)
    slot_rank = slot_ranks(destination, peer_count)
    slot_index = destination * capacity + slot_rank
    pair_rows = query_unit[jnp.arange(destination.shape[0], dtype=jnp.int32) // cand_count]
    send_queries = (
        jnp.zeros((peer_count * capacity,) + query_unit.shape[1:], jnp.bfloat16)
        .at[slot_index]
        .set(pair_rows)
    )
    send_queries = send_queries.reshape((peer_count, capacity) + query_unit.shape[1:])
    send_ids = (
        jnp.zeros((peer_count * capacity,), jnp.int32)
        .at[slot_index]
        .set(passage_ids)
        .reshape(peer_count, capacity)
    )
    got_queries = lax.all_to_all(send_queries, "dp", split_axis=0, concat_axis=0, tiled=True)
    received_token_ids = lax.all_to_all(send_ids, "dp", split_axis=0, concat_axis=0, tiled=True)
    sources, items = received_token_ids.shape
    flat_queries = got_queries.reshape((sources * items,) + got_queries.shape[2:])
    scored = slot_scores(
        flat_queries, received_token_ids.reshape(-1), passage_unit, kept_lengths
    ).reshape(sources, items)
    returned = send_back(scored)
    student = returned.reshape(-1)[slot_index].reshape(query_count, cand_count)
    teacher_score_rows = teacher[0]
    log_teacher = teacher_score_rows - jnp.log(
        jnp.sum(jnp.exp(teacher_score_rows), axis=-1, keepdims=True)
    )
    log_student = student - jnp.log(jnp.sum(jnp.exp(student), axis=-1, keepdims=True))
    distill = jnp.sum(jnp.exp(log_teacher) * (log_teacher - log_student), axis=-1)
    positive_unit = unit_rows(positives[0])
    positive_kept = positive_lengths[0]
    doc_piece = lax.all_gather(positive_unit, "blk", axis=0, tiled=True)
    length_piece = lax.all_gather(positive_kept, "blk", axis=0, tiled=True)
    scored = cross_scores(query_unit, doc_piece, length_piece)
    own_column = lax.axis_index("blk") * query_count + jnp.arange(query_count, dtype=jnp.int32)
    own_logit = jnp.take_along_axis(scored, own_column[:, None], axis=1)[:, 0]
    contrast = jnp.log(jnp.sum(jnp.exp(scored), axis=-1)) - own_logit
    return (student[None], distill[None], contrast[None])


def solution(mesh):
    in_specs = (
        P("blk", "dp", None, None),
        P("blk", "dp", None, None),
        P("blk", "dp"),
        P("blk", "dp", None, None),
        P("blk", "dp"),
        P("blk", "dp", None, None),
        P("blk", "dp", None),
        P("blk", "dp", None),
    )
    out_specs = (P("blk", "dp", None), P("blk", "dp"), P("blk", "dp"))
    return jax.shard_map(
        per_device, mesh=mesh, in_specs=in_specs, out_specs=out_specs, check_vma=False
    )
```

profile of v0, /device:TPU:0, one launch (start us, length us, event | category | flops | bytes accessed | tf_op | source)
XLA Modules:
  0.0 131.4 jit_solution(10572305742999214558)
XLA Ops:
  0.6 0.5 broadcast.336
  1.1 1.3 %fusion.25 = (s32[4,32]{1,0:T(4,128)S(1)}, s32[4,32]{1,0:T(4,128)S(1)}) fusion(s32[1,4,32,1]{2,3,1,0:T(1,128)} %param.15, s32[]{:T(128)} %broadcast.336), kind=kLoop, calls=%fused_computation.69 | loop fusion | flops 128 | bytes 1540 | tf_op args[5]
  2.5 0.1 eq.15
  2.6 0.1 fusion.15
  2.7 0.2 reduce_window_sum.11
  2.8 0.2 select_reduce_fusion.1
  3.0 0.1 mul.65
  3.1 0.8 reshape.338
  3.9 1.0 scatter_custom_fusion
  4.9 0.7 all_to_all.15
  5.5 7.4 %all-to-all-start = ((s32[16,1,16]{2,1,0:T(1,128)}), s32[16,1,16]{2,1,0:T(1,128)S(1)}, u32[]{:S(2)}, u32[]{:S(2)}) async-start(s32[16,1,16]{2,1,0:T(1,128)} %all_to_all.15), calls=%async_computation | async-start | bytes 16384 | tf_op jit(solution)/shard_map/all_to_all | solution.py:101
  13.0 0.8 fusion.12
  13.8 0.8 fusion.13
  14.7 0.8 gather_fusion.2
  15.5 1.6 %broadcast_in_dim.67 = bf16[256,32,128]{2,1,0:T(8,128)(2,1)} broadcast(bf16[]{:T(256)} %constant.61.clone.1), dimensions={} | broadcast | bytes 2097154 | tf_op jit(solution)/shard_map/broadcast_in_dim | solution.py:89
  17.1 13.7 %scatter_fusion = bf16[256,32,128]{2,1,0:T(8,128)(2,1)} fusion(bf16[256,32,128]{2,1,0:T(8,128)(2,1)} %broadcast_in_dim.67, s32[128]{0:T(128)S(1)} %fusion.22, bf16[128,32,128]{2,1,0:T(8,128)(2,1)S(1)} %gather_fusion.2), kind=kCustom, calls=%fused_computation.6 | custom fusion | bytes 3146240 | tf_op jit(solution)/shard_map/scatter | solution.py:91
  30.8 6.1 %all-to-all-start.1 = ((bf16[16,16,32,128]{3,2,1,0:T(8,128)(2,1)}), bf16[16,16,32,128]{3,2,1,0:T(8,128)(2,1)S(1)}, u32[]{:S(2)}, u32[]{:S(2)}) async-start(bf16[16,16,32,128]{3,2,1,0:T(8,128)(2,1)} %bitcast.9), calls=%async_computation.1 | async-start | bytes 4194304 | tf_op jit(solution)/shard_map/all_to_all | solution.py:100
  37.0 0.6 dynamic-slice.2
  38.2 0.1 bitcast_dynamic-update-slice_fusion
  38.3 4.3 %all-reduce = s32[8]{0:T(128)S(1)} all-reduce(s32[8]{0:T(128)S(1)} %bitcast_dynamic-update-slice_fusion), channel_id=2, replica_groups=mesh['dp'=16,'blk'=2] {'blk'}, use_global_device_ids=true, to_apply=%add | all-reduce | flops 8 | bytes 64
  42.6 0.2 fusion.7
  42.8 0.2 fusion.8
  43.0 7.1 %all_gather.7 = bf16[8,192,128]{2,1,0:T(8,128)(2,1)S(1)} all-gather(bf16[4,192,128]{2,1,0:T(8,128)(2,1)S(1)} %fusion.8), channel_id=1, replica_groups=mesh['dp'=16,'blk'=2] {'blk'}, dimensions={0}, use_global_device_ids=true | all-gather | bytes 589824 | tf_op jit(solution)/shard_map/all_gather | solution.py:117
  50.1 0.5 fusion.6
  50.7 0.1 reduce_sum.103
  50.8 0.6 gather_fusion.4
  51.5 0.6 fusion.4
  52.1 0.5 fusion.21
  52.6 1.6 %fusion.5 = bf16[16,192,128]{2,1,0:T(8,128)(2,1)S(1)} fusion(bf16[1,16,192,128]{3,2,1,0:T(8,128)(2,1)} %param.11, f32[16,192]{1,0:T(8,128)S(1)} %add_rsqrt_fusion), kind=kLoop, calls=%fused_computation.18 | loop fusion | flops 1179648 | bytes 1585152 | tf_op jit(solution)/shard_map/convert_element_type | solution.py:12
  54.2 0.7 reduce.16
  55.0 23.1 %all-to-all-done.1 = bf16[16,16,32,128]{3,2,1,0:T(8,128)(2,1)S(1)} async-done(((bf16[16,16,32,128]{3,2,1,0:T(8,128)(2,1)}), bf16[16,16,32,128]{3,2,1,0:T(8,128)(2,1)S(1)}, u32[]{:S(2)}, u32[]{:S(2)}) %all-to-all-start.1) | async-done | bytes 2097184 | tf_op jit(solution)/shard_map/all_to_all | solution.py:100
  78.1 30.9 %while.2 = (s32[]{:T(128)}, f32[4,64]{1,0:T(4,128)S(1)}, s32[4,64]{1,0:T(4,128)S(1)}, s32[16]{0:T(128)S(1)}, bf16[4,64,32,128]{3,2,1,0:T(8,128)(2,1)S(1)}, /*ind...) while((s32[]{:T(128)}, f32[4,64]{1,0:T(4,128)S(1)}, s32[4,64]{1,0:T(4,128)S(1)}, ...), condition=%wide.region_9.10_spmd, body=%wide.region_6.9_spmd.sunk | while | flops 101463168 | bytes 10013549 | solution.py:43
  78.1 2.6 %gather_fusion = bf16[64,192,128]{2,1,0:T(8,128)(2,1)} fusion(bf16[16,192,128]{2,1,0:T(8,128)(2,1)S(1)} %get-tuple-element.125, s32[1024]{0:T(1024)S(1)} %pad_clamp_fusion.4), kind=kCustom, calls=%fused_computation.1.clone.1 | custom fusion | bytes 6291712 | tf_op jit(solution)/shard_map/while/body/eval_jaxpr/gather | solution.py:33
  80.7 0.8 gather_fusion.1
  81.5 0.1 iota_compare_fusion.4
  81.6 4.0 %select_reduce_fusion.3 = f32[64,32]{1,0:T(8,128)S(1)} fusion(bf16[64,192,128]{2,1,0:T(8,128)(2,1)} %gather_fusion, pred[64,192]{1,0:T(8,128)(4,1)S(1)} %iota_compare_fusion.4, bf16[4,64,32,128]{3,2,1,0:T(8,128)(2,1)S(1)} %get-tuple-element.124, s32[]{:T(128)} %get-tuple-element.111), kind=kOutput, calls=%fused_computation.7.clone.1 | convolution fusion | flops 101447680 | bytes 3694596 | tf_op jit(solution)/shard_map/while/body/eval_jaxpr/uhv,uyv->uhy/dot_general | solution.py:34
  85.6 0.1 reduce_sum.115
  85.8 2.6 %gather_fusion = bf16[64,192,128]{2,1,0:T(8,128)(2,1)} fusion(bf16[16,192,128]{2,1,0:T(8,128)(2,1)S(1)} %get-tuple-element.125, s32[1024]{0:T(1024)S(1)} %pad_clamp_fusion.4), kind=kCustom, calls=%fused_computation.1.clone.1 | custom fusion | bytes 6291712 | tf_op jit(solution)/shard_map/while/body/eval_jaxpr/gather | solution.py:33
  88.4 0.8 gather_fusion.1
  89.2 0.1 iota_compare_fusion.4
  89.3 4.0 %select_reduce_fusion.3 = f32[64,32]{1,0:T(8,128)S(1)} fusion(bf16[64,192,128]{2,1,0:T(8,128)(2,1)} %gather_fusion, pred[64,192]{1,0:T(8,128)(4,1)S(1)} %iota_compare_fusion.4, bf16[4,64,32,128]{3,2,1,0:T(8,128)(2,1)S(1)} %get-tuple-element.124, s32[]{:T(128)} %get-tuple-element.111), kind=kOutput, calls=%fused_computation.7.clone.1 | convolution fusion | flops 101447680 | bytes 3694596 | tf_op jit(solution)/shard_map/while/body/eval_jaxpr/uhv,uyv->uhy/dot_general | solution.py:34
  93.3 0.1 reduce_sum.115
  93.5 2.6 %gather_fusion = bf16[64,192,128]{2,1,0:T(8,128)(2,1)} fusion(bf16[16,192,128]{2,1,0:T(8,128)(2,1)S(1)} %get-tuple-element.125, s32[1024]{0:T(1024)S(1)} %pad_clamp_fusion.4), kind=kCustom, calls=%fused_computation.1.clone.1 | custom fusion | bytes 6291712 | tf_op jit(solution)/shard_map/while/body/eval_jaxpr/gather | solution.py:33
  96.1 0.8 gather_fusion.1
  96.9 0.1 iota_compare_fusion.4
  97.0 4.0 %select_reduce_fusion.3 = f32[64,32]{1,0:T(8,128)S(1)} fusion(bf16[64,192,128]{2,1,0:T(8,128)(2,1)} %gather_fusion, pred[64,192]{1,0:T(8,128)(4,1)S(1)} %iota_compare_fusion.4, bf16[4,64,32,128]{3,2,1,0:T(8,128)(2,1)S(1)} %get-tuple-element.124, s32[]{:T(128)} %get-tuple-element.111), kind=kOutput, calls=%fused_computation.7.clone.1 | convolution fusion | flops 101447680 | bytes 3694596 | tf_op jit(solution)/shard_map/while/body/eval_jaxpr/uhv,uyv->uhy/dot_general | solution.py:34
  101.1 0.1 reduce_sum.115
  101.3 2.6 %gather_fusion = bf16[64,192,128]{2,1,0:T(8,128)(2,1)} fusion(bf16[16,192,128]{2,1,0:T(8,128)(2,1)S(1)} %get-tuple-element.125, s32[1024]{0:T(1024)S(1)} %pad_clamp_fusion.4), kind=kCustom, calls=%fused_computation.1.clone.1 | custom fusion | bytes 6291712 | tf_op jit(solution)/shard_map/while/body/eval_jaxpr/gather | solution.py:33
  103.9 0.8 gather_fusion.1
  104.6 0.1 iota_compare_fusion.4
  104.7 4.0 %select_reduce_fusion.3 = f32[64,32]{1,0:T(8,128)S(1)} fusion(bf16[64,192,128]{2,1,0:T(8,128)(2,1)} %gather_fusion, pred[64,192]{1,0:T(8,128)(4,1)S(1)} %iota_compare_fusion.4, bf16[4,64,32,128]{3,2,1,0:T(8,128)(2,1)S(1)} %get-tuple-element.124, s32[]{:T(128)} %get-tuple-element.111), kind=kOutput, calls=%fused_computation.7.clone.1 | convolution fusion | flops 101447680 | bytes 3694596 | tf_op jit(solution)/shard_map/while/body/eval_jaxpr/uhv,uyv->uhy/dot_general | solution.py:34
  108.8 0.1 reduce_sum.115
  108.9 0.7 all_to_all.18
  109.6 11.2 %all-to-all-start.2 = ((f32[16,1,16]{2,1,0:T(1,128)}), f32[16,1,16]{2,1,0:T(1,128)S(1)}, u32[]{:S(2)}, u32[]{:S(2)}) async-start(f32[16,1,16]{2,1,0:T(1,128)} %all_to_all.18), calls=%async_computation.2 | async-start | bytes 16384 | tf_op jit(solution)/shard_map/all_to_all | solution.py:70
  120.9 0.1 fusion.19
  121.0 6.3 %all-to-all-done.2 = f32[16,1,16]{2,1,0:T(1,128)S(1)} async-done(((f32[16,1,16]{2,1,0:T(1,128)}), f32[16,1,16]{2,1,0:T(1,128)S(1)}, u32[]{:S(2)}, u32[]{:S(2)}) %all-to-all-start.2) | async-done | bytes 1056 | tf_op jit(solution)/shard_map/all_to_all | solution.py:70
  127.3 0.5 broadcast.338
  127.8 0.7 reduce.17
  128.4 0.1 reshape.289
  128.5 1.3 gather_fusion.3
  129.8 0.1 reshape.290
  129.9 0.7 broadcast_in_dim_reshape.3
  130.5 0.1 exponential_reduce_fusion.1
  130.7 0.7 multiply_reduce_fusion
  (45 shorter events, 0.5 us)
Async XLA Ops:
  5.5 25.2 %all-to-all-start = ((s32[16,1,16]{2,1,0:T(1,128)}), s32[16,1,16]{2,1,0:T(1,128)S(1)}, u32[]{:S(2)}, u32[]{:S(2)}) async-start(s32[16,1,16]{2,1,0:T(1,128)} %all_to_all.15), calls=%async_computation | async-start | bytes 16384 | tf_op jit(solution)/shard_map/all_to_all | solution.py:101
  30.8 6.2 %copy-start.6 = (u32[32]{0:T(128)S(1)}, u32[32]{0:T(128)}, u32[]{:S(2)}) copy-start(u32[32]{0:T(128)} %constant.122) | copy-start | bytes 388
  30.8 7.5 %copy-start.5 = (s32[1,4]{1,0:T(1,128)S(1)}, s32[1,4]{1,0:T(1,128)}, u32[]{:S(2)}) copy-start(s32[1,4]{1,0:T(1,128)} %param.14) | copy-start | bytes 52
  30.8 11.8 %copy-start.2 = (bf16[1,4,192,128]{3,2,1,0:T(8,128)(2,1)S(1)}, bf16[1,4,192,128]{3,2,1,0:T(8,128)(2,1)}, u32[]{:S(2)}) copy-start(bf16[1,4,192,128]{3,2,1,0:T(8,128)(2,1)} %param.13) | copy-start | bytes 589828
  30.8 19.4 %copy-start.3 = (bf16[1,4,32,128]{3,2,1,0:T(8,128)(2,1)S(1)}, bf16[1,4,32,128]{3,2,1,0:T(8,128)(2,1)}, u32[]{:S(2)}) copy-start(bf16[1,4,32,128]{3,2,1,0:T(8,128)(2,1)} %param.10) | copy-start | bytes 98308
  30.8 47.3 %all-to-all-start.1 = ((bf16[16,16,32,128]{3,2,1,0:T(8,128)(2,1)}), bf16[16,16,32,128]{3,2,1,0:T(8,128)(2,1)S(1)}, u32[]{:S(2)}, u32[]{:S(2)}) async-start(bf16[16,16,32,128]{3,2,1,0:T(8,128)(2,1)} %bitcast.9), calls=%async_computation.1 | async-start | bytes 4194304 | tf_op jit(solution)/shard_map/all_to_all | solution.py:100
  36.9 14.5 %copy-start.1 = (bf16[1,16,192,128]{3,2,1,0:T(8,128)(2,1)S(1)}, bf16[1,16,192,128]{3,2,1,0:T(8,128)(2,1)}, u32[]{:S(2)}) copy-start(bf16[1,16,192,128]{3,2,1,0:T(8,128)(2,1)} %param.11) | copy-start | bytes 2359300
  50.1 28.0 %copy-start = (s32[1,16]{1,0:T(1,128)S(1)}, s32[1,16]{1,0:T(1,128)}, u32[]{:S(2)}) copy-start(s32[1,16]{1,0:T(1,128)} %param.12) | copy-start | bytes 196
  78.1 42.8 %copy-start.4 = (f32[1,4,32]{2,1,0:T(4,128)S(1)}, f32[1,4,32]{2,1,0:T(4,128)}, u32[]{:S(2)}) copy-start(f32[1,4,32]{2,1,0:T(4,128)} %param.17) | copy-start | bytes 1540
  109.6 17.6 %all-to-all-start.2 = ((f32[16,1,16]{2,1,0:T(1,128)}), f32[16,1,16]{2,1,0:T(1,128)S(1)}, u32[]{:S(2)}, u32[]{:S(2)}) async-start(f32[16,1,16]{2,1,0:T(1,128)} %all_to_all.18), calls=%async_computation.2 | async-start | bytes 16384 | tf_op jit(solution)/shard_map/all_to_all | solution.py:70
where the time goes:
time: 132 us; the launch traced here: 131 us
  local copies, waits for them, and re-layouts  37.6 us (28%)
  waiting for transfers between devices  29.3 us (22%)
  starting transfers between devices  24.7 us (19%)
  matrix products  16.7 us (13%)
  blocking collectives  11.3 us (9%)
  other arithmetic  9.97 us (8%)
  between operations  1.53 us (1%)
    all_to_all x1, waiting for transfers between devices, per_device(): lax.all_to_all(send_queries, 'dp', split_axis=0, concat_axis=0, tiled=True)  23.1 us
    dot_general x4, matrix products, slot_block_relevance(): jnp.einsum('uhv,uyv->uhy', query_tile_rows, document_rows, preferred_elem...  16.2 us
    scatter x1, local copies, waits for them, and re-layouts, per_device(): send_queries = jnp.zeros((peer_count * capacity,) + query_unit.shape[1:],...  13.7 us
    all_to_all x1, starting transfers between devices, send_back(): return lax.all_to_all(scored, 'dp', split_axis=0, concat_axis=0, tiled=True)  11.2 us
    gather x4, local copies, waits for them, and re-layouts, slot_block_relevance(): document_rows = passage_unit[id_block]  10.5 us
    all_to_all x1, starting transfers between devices, per_device(): lax.all_to_all(send_ids, 'dp', split_axis=0, concat_axis=0, tiled=True)  7.39 us
    all_gather x1, blocking collectives, per_device(): doc_piece = lax.all_gather(positive_unit, 'blk', axis=0, tiled=True)  7.06 us
    all_to_all x1, waiting for transfers between devices, send_back(): return lax.all_to_all(scored, 'dp', split_axis=0, concat_axis=0, tiled=True)  6.27 us
  transfers between devices with their start and end apart: 3, of which 2 were waited for; matrix products, arithmetic and copies ran while one was open for 18% of the time, Pallas kernels for 0%

commit v1 on v0

v1 whole, which is shorter than its diff:
```python
import functools

import jax
import jax.numpy as jnp
from jax import lax
from jax.experimental import pallas as pl
from jax.experimental.pallas import tpu as pltpu
from jax.sharding import PartitionSpec as P

VMEM = pl.BlockSpec(memory_space=pltpu.VMEM)
SMEM = pl.BlockSpec(memory_space=pltpu.SMEM)
LIMIT = 32 * 1024 * 1024


def unit(values):
    wide = values.astype(jnp.float32)
    total = jnp.sum(wide * wide, axis=-1, keepdims=True) + 1e-06
    return (wide * lax.rsqrt(total)).astype(jnp.bfloat16)


def kept_unit(rows, kept):
    place = lax.broadcasted_iota(jnp.int32, (rows.shape[0], 1), 0)
    wide = rows.astype(jnp.float32)
    return unit(jnp.where(place < kept, wide, wide[0:1]))


def group_sum(values, width):
    lanes = values.shape[1]
    row = lax.broadcasted_iota(jnp.int32, (lanes, lanes), 0) // width
    column = lax.broadcasted_iota(jnp.int32, (lanes, lanes), 1) // width
    same = (row == column).astype(jnp.bfloat16)
    high = values.astype(jnp.bfloat16)
    rest = values - high.astype(jnp.float32)
    middle = rest.astype(jnp.bfloat16)
    low = (rest - middle.astype(jnp.float32)).astype(jnp.bfloat16)
    parts = [jnp.dot(part, same, preferred_element_type=jnp.float32) for part in (high, middle, low)]
    return parts[0] + (parts[1] + parts[2])


def best_match(tokens, query_rows):
    similar = lax.dot_general(
        tokens, query_rows, (((1,), (1,)), ((), ())), preferred_element_type=jnp.float32
    )
    return jnp.max(similar, axis=0, keepdims=True)


def prepare_kernel(kept_ref, rows_ref, out_ref):
    def one(i, carry):
        out_ref[i] = kept_unit(rows_ref[i], kept_ref[0, i])
        return carry

    lax.fori_loop(0, rows_ref.shape[0], one, 0, unroll=4)


def prepare(rows, kept):
    return pl.pallas_call(
        prepare_kernel,
        out_shape=jax.ShapeDtypeStruct(rows.shape, rows.dtype),
        in_specs=[SMEM, VMEM],
        out_specs=VMEM,
        compiler_params=pltpu.CompilerParams(vmem_limit_bytes=LIMIT),
        cost_estimate=pl.CostEstimate(flops=16 * rows.size, bytes_accessed=4 * rows.size, transcendentals=0),
    )(kept, rows)


def score_kernel(qlen, count, *refs):
    query_refs, (near_ref, far_ref, out_ref, best_ref) = refs[:count], refs[count:]
    near = near_ref.shape[0]
    total = near + far_ref.shape[0]
    lanes = query_refs[0].shape[1]
    row = lax.broadcasted_iota(jnp.int32, (total, lanes), 0)
    column = lax.broadcasted_iota(jnp.int32, (total, lanes), 1) % qlen
    start = 0
    queries = [ref[i] for ref in query_refs for i in range(ref.shape[0])]
    while start < len(queries):
        block = [unit(q) for q in queries[start : start + 2]]
        joined = jnp.concatenate(block, axis=0)
        width = joined.shape[0]
        for i in range(total):
            tokens = near_ref[i] if i < near else far_ref[i - near]
            best_ref[i : i + 1, :width] = best_match(tokens, joined)
        for s in range(len(block)):
            summed = group_sum(best_ref[:, s * lanes : (s + 1) * lanes], qlen)
            out_ref[start + s : start + s + 1, :] = jnp.sum(
                jnp.where(row == column, summed, 0.0), axis=0, keepdims=True
            )
        start += 2


def score(query_list, near, far, qlen):
    lanes = query_list[0].shape[1]
    sources = sum(q.shape[0] for q in query_list)
    total = near.shape[0] + far.shape[0]
    return pl.pallas_call(
        functools.partial(score_kernel, qlen, len(query_list)),
        out_shape=jax.ShapeDtypeStruct((sources, lanes), jnp.float32),
        in_specs=[VMEM] * (len(query_list) + 2),
        out_specs=VMEM,
        scratch_shapes=[pltpu.VMEM((total, 2 * lanes), jnp.float32)],
        compiler_params=pltpu.CompilerParams(vmem_limit_bytes=LIMIT),
        cost_estimate=pl.CostEstimate(
            flops=2 * sources * lanes * near.shape[2] * total * near.shape[1],
            bytes_accessed=2 * (near.size + far.size),
            transcendentals=0,
        ),
    )(*query_list, near, far)


def contrast_kernel(qlen, query_ref, own_ref, other_ref, out_ref, best_ref):
    queries = unit(query_ref[...])
    lanes = queries.shape[0]
    docs = own_ref.shape[0]
    total = docs + other_ref.shape[0]
    for i in range(total):
        tokens = own_ref[i] if i < docs else other_ref[i - docs]
        best_ref[i : i + 1, :] = best_match(tokens, queries)
    logits = group_sum(best_ref[...], qlen)
    row = lax.broadcasted_iota(jnp.int32, (total, lanes), 0)
    query = lax.broadcasted_iota(jnp.int32, (total, lanes), 1) // qlen
    own = jnp.sum(jnp.where(row == query, logits, 0.0), axis=0, keepdims=True)
    loss = jnp.log(jnp.sum(jnp.exp(logits), axis=0, keepdims=True)) - own
    place = (lax.broadcasted_iota(jnp.int32, (8, lanes), 1) * qlen) % lanes
    spread = jnp.take_along_axis(jnp.broadcast_to(loss, (8, lanes)), place, axis=1)
    out_ref[...] = spread[0:1, : lanes // qlen]


def contrast_loss(query_rows, own, other, qlen):
    lanes = query_rows.shape[0]
    total = own.shape[0] + other.shape[0]
    return pl.pallas_call(
        functools.partial(contrast_kernel, qlen),
        out_shape=jax.ShapeDtypeStruct((1, lanes // qlen), jnp.float32),
        in_specs=[VMEM, VMEM, VMEM],
        out_specs=VMEM,
        scratch_shapes=[pltpu.VMEM((total, lanes), jnp.float32)],
        compiler_params=pltpu.CompilerParams(vmem_limit_bytes=LIMIT),
        cost_estimate=pl.CostEstimate(
            flops=2 * lanes * own.shape[2] * total * own.shape[1], bytes_accessed=4 * own.size, transcendentals=0
        ),
    )(query_rows, own, other)


def flat_lanes(rows, pad_ref, lanes):
    queries, width = rows.shape
    pad_ref[:queries, :width] = rows
    place = lax.broadcasted_iota(jnp.int32, (8, lanes), 1)
    spread = jnp.take_along_axis(pad_ref[...], place % width, axis=1)
    row = lax.broadcasted_iota(jnp.int32, (8, lanes), 0)
    return jnp.sum(jnp.where(row == place // width, spread, 0), axis=0, keepdims=True)


def distill_kernel(returned_ref, where_ref, lane_ref, teacher_ref, student_ref, distill_ref, pad_ref, ints_ref):
    queries, width = teacher_ref.shape[1:]
    scorers, lanes = returned_ref.shape
    teacher = flat_lanes(teacher_ref[0], pad_ref, lanes)
    whose = flat_lanes(where_ref[...], ints_ref, lanes)
    lane = flat_lanes(lane_ref[...], ints_ref, lanes)
    lane = lane + lax.broadcasted_iota(jnp.int32, (1, lanes), 1) // width * (lanes // queries)
    returned = returned_ref[...]
    picked = jnp.take_along_axis(returned, jnp.broadcast_to(lane, (scorers, lanes)), axis=1)
    row = lax.broadcasted_iota(jnp.int32, (scorers, lanes), 0)
    student = jnp.sum(jnp.where(row == whose, picked, 0.0), axis=0, keepdims=True)
    log_teacher = teacher - jnp.log(group_sum(jnp.exp(teacher), width))
    log_student = student - jnp.log(group_sum(jnp.exp(student), width))
    loss = group_sum(jnp.exp(log_teacher) * (log_teacher - log_student), width)
    first = lax.broadcasted_iota(jnp.int32, (8, lanes), 0)
    place = lax.broadcasted_iota(jnp.int32, (8, lanes), 1)
    spread = jnp.take_along_axis(jnp.broadcast_to(student, (8, lanes)), (first * width + place) % lanes, axis=1)
    student_ref[0] = spread[:queries, :width]
    spread = jnp.take_along_axis(jnp.broadcast_to(loss, (8, lanes)), (place * width) % lanes, axis=1)
    distill_ref[...] = spread[0:1, :queries]


def distill_loss(returned, whose, lane, teacher):
    lanes = returned.shape[1]
    return pl.pallas_call(
        distill_kernel,
        out_shape=(
            jax.ShapeDtypeStruct(teacher.shape, jnp.float32),
            jax.ShapeDtypeStruct(teacher.shape[:2], jnp.float32),
        ),
        in_specs=[VMEM] * 4,
        out_specs=(VMEM, VMEM),
        scratch_shapes=[pltpu.VMEM((8, lanes), jnp.float32), pltpu.VMEM((8, lanes), jnp.int32)],
        compiler_params=pltpu.CompilerParams(vmem_limit_bytes=LIMIT),
    )(returned, whose, lane, teacher)


def swap(values, axis, bit):
    return lax.ppermute(values, axis, [(i, i ^ bit) for i in range(lax.axis_size(axis))])


def per_device(
    queries, passages, passage_lengths, positives, positive_lengths, owners, local_ids, teacher
):
    peers = lax.axis_size("dp")
    groups = lax.axis_size("blk")
    me = lax.axis_index("dp")
    query_count, qlen = queries.shape[1:3]
    pass_count = passages.shape[1]
    own_rows = queries.reshape(1, query_count * qlen, queries.shape[3])
    bits = [1 << n for n in range(1, peers.bit_length() - 1)]

    first = swap(own_rows, "dp", bits[-1])
    near = prepare(passages[0], passage_lengths)
    far = swap(near, "dp", 1)
    own_docs = prepare(positives[0], positive_lengths)
    other_docs = jnp.concatenate(
        [
            lax.ppermute(own_docs, "blk", [(i, (i + k) % groups) for i in range(groups)])
            for k in range(1, groups)
        ],
        axis=0,
    )

    held = jnp.concatenate([own_rows, first], axis=0)
    scored = [score([own_rows, first], near, far, qlen)]
    for bit in reversed(bits[:-1]):
        got = swap(held, "dp", bit)
        scored.append(score([got], near, far, qlen))
        held = jnp.concatenate([held, got], axis=0)
    contrast = contrast_loss(own_rows[0], own_docs, other_docs, qlen)

    back = jnp.concatenate(scored, axis=0)[None]
    for bit in bits:
        half = back.shape[1] // 2
        back = jnp.concatenate([back[:, :half], swap(back[:, half:], "dp", bit)], axis=0)
    returned = back.reshape(peers // 2, query_count * qlen)

    apart = owners[0, :, :, 0] ^ me
    student, distill = distill_loss(returned, apart >> 1, (apart & 1) * pass_count + local_ids[0], teacher)
    return (student, distill, contrast)


def solution(mesh):
    in_specs = (
        P("blk", "dp", None, None),
        P("blk", "dp", None, None),
        P("blk", "dp"),
        P("blk", "dp", None, None),
        P("blk", "dp"),
        P("blk", "dp", None, None),
        P("blk", "dp", None),
        P("blk", "dp", None),
    )
    out_specs = (P("blk", "dp", None), P("blk", "dp"), P("blk", "dp"))
    return jax.shard_map(
        per_device, mesh=mesh, in_specs=in_specs, out_specs=out_specs, check_vma=False
    )
```

time: 132 us -> 37 us (0.28)
  local copies, waits for them, and re-layouts: 37.6 us -> 2.49 us
  waiting for transfers between devices: 29.3 us -> 10.2 us
  matrix products: 16.7 us -> 0 us
  blocking collectives: 11.3 us -> 0 us
  starting transfers between devices: 24.7 us -> 14.4 us
  other arithmetic: 9.97 us -> 0.07 us
  Pallas kernels: 0 us -> 9.03 us
    all_to_all x3 -> x0, waiting for transfers between devices: 29.3 us -> none  [the longest x1 23.1 us: per_device(): lax.all_to_all(send_queries, 'dp', split_axis=0, concat_axis=0, tiled=True)]
    all_to_all x3 -> x0, starting transfers between devices: 24.7 us -> none  [the longest x1 11.2 us: send_back(): return lax.all_to_all(scored, 'dp', split_axis=0, concat_axis=0, tiled=True)]
    dot_general x5 -> x0, matrix products: 16.7 us -> none  [the longest x4 16.2 us: slot_block_relevance(): jnp.einsum('uhv,uyv->uhy', query_tile_rows, document_rows, preferred_elem...]
    gather x11 -> x0, local copies, waits for them, and re-layouts: 16.2 us -> none  [the longest x4 10.5 us: slot_block_relevance(): document_rows = passage_unit[id_block]]
    scatter x2 -> x0, local copies, waits for them, and re-layouts: 14.7 us -> none  [the longest x1 13.7 us: per_device(): send_queries = jnp.zeros((peer_count * capacity,) + query_unit.shape[1:],...]
    ppermute x0 -> x8, starting transfers between devices: none -> 14.4 us  [the longest x7 12.8 us: swap(): lax.ppermute(values, axis, [(i, i ^ bit) for i in range(lax.axis_size(axi...]
    ppermute x0 -> x8, waiting for transfers between devices: none -> 10.2 us  [the longest x7 10.2 us: swap(): lax.ppermute(values, axis, [(i, i ^ bit) for i in range(lax.axis_size(axi...]
    pallas_call x0 -> x7, Pallas kernels: none -> 9.03 us  [the longest x3 4.8 us: score(): pl.pallas_call(functools.partial(score_kernel, qlen, len(query_list)), ou...]
  transfers between devices with their start and end apart: 3 -> 8, of which waited for: 2 -> 5; matrix products, arithmetic and copies ran while one was open for 18% -> 0% of each run, Pallas kernels for 0% -> 18%
where the time goes in v1:
time: 37 us; the launch traced here: 36.9 us
  starting transfers between devices  14.4 us (39%)
  waiting for transfers between devices  10.2 us (28%)
  Pallas kernels  9.03 us (24%)
  local copies, waits for them, and re-layouts  2.49 us (7%)
  between operations  0.75 us (2%)
    ppermute x7, starting transfers between devices, swap(): lax.ppermute(values, axis, [(i, i ^ bit) for i in range(lax.axis_size(axi...  12.8 us
    ppermute x7, waiting for transfers between devices, swap(): lax.ppermute(values, axis, [(i, i ^ bit) for i in range(lax.axis_size(axi...  10.2 us
    pallas_call x3, Pallas kernels, score(): pl.pallas_call(functools.partial(score_kernel, qlen, len(query_list)), ou...  4.8 us
    unnamed x16, local copies, waits for them, and re-layouts  2.49 us
    pallas_call x2, Pallas kernels, prepare(): pl.pallas_call(prepare_kernel, out_shape=jax.ShapeDtypeStruct(rows.shape,...  2.02 us
    ppermute x1, starting transfers between devices, per_device(): lax.ppermute(own_docs, 'blk', [(i, (i + k) % groups) for i in range(group...  1.56 us
    pallas_call x1, Pallas kernels, contrast_loss(): pl.pallas_call(functools.partial(contrast_kernel, qlen), out_shape=jax.Sh...  1.14 us
    pallas_call x1, Pallas kernels, distill_loss(): pl.pallas_call(distill_kernel, out_shape=(jax.ShapeDtypeStruct(teacher.sh...  1.07 us
  transfers between devices with their start and end apart: 8, of which 5 were waited for; matrix products, arithmetic and copies ran while one was open for 0% of the time, Pallas kernels for 18%

profile of v1, /device:TPU:0, one launch (start us, length us, event | category | flops | bytes accessed | tf_op | source)
XLA Modules:
  0.0 36.9 jit_solution(8870814144321933059)
XLA Ops:
  0.6 0.0 copy-start.4
  0.6 0.6 %copy-done.4 = s32[1,16]{1,0:T(1,128)S(1)} copy-done((s32[1,16]{1,0:T(1,128)S(1)}, s32[1,16]{1,0:T(1,128)}, u32[]{:S(2)}) %copy-start.4) | copy-done | bytes 88
  1.3 0.0 copy-start
  1.3 1.1 %copy-done = bf16[1,16,192,128]{3,2,1,0:T(8,128)(2,1)S(1)} copy-done((bf16[1,16,192,128]{3,2,1,0:T(8,128)(2,1)S(1)}, bf16[1,16,192,128]{3,2,1,0:T(8,128)(2,1)}, u32[]{:S(2)}) %copy-start) | copy-done | bytes 786456
  2.4 0.0 copy-start.1
  2.4 1.3 %shard_map.103.refs_2_.refs_1_ = bf16[16,192,128]{2,1,0:T(8,128)(2,1)S(1)} custom-call(s32[1,16]{1,0:T(1,128)S(1)} %copy-done.4, bf16[16,192,128]{2,1,0:T(8,128)(2,1)S(1)} %bitcast.11), custom_call_target="tpu_custom_call" | custom-call | flops 6291456 | bytes 1572864 | tf_op jit(solution)/shard_map/pallas_call | solution.py:56
  3.7 0.5 %collective-permute-start.1 = (bf16[16,192,128]{2,1,0:T(8,128)(2,1)S(1)}, bf16[16,192,128]{2,1,0:T(8,128)(2,1)S(1)}, u32[]{:S(2)}, u32[]{:S(2)}) collective-permute-start(bf16[16,192,128]{2,1,0:T(8,128)(2,1)S(1)} %shard_map.103.refs_2_.refs_1_), channel_id=1, source_target_pairs={{0,2},{2,0},{4,6},{6,4},{8,10},{10,8},{12,14},{14,12},{16,18},{18,... | collective-permute-start | bytes 2359304 | tf_op jit(solution)/shard_map/ppermute | solution.py:190
  4.2 0.0 copy-done.1
  4.2 0.0 copy-start.2
  4.2 3.7 %collective-permute-start = (bf16[1,128,128]{2,1,0:T(8,128)(2,1)S(1)}, bf16[1,128,128]{2,1,0:T(8,128)(2,1)S(1)}, u32[]{:S(2)}, u32[]{:S(2)}) collective-permute-start(bf16[1,128,128]{2,1,0:T(8,128)(2,1)S(1)} %bitcast.12), channel_id=1, source_target_pairs={{0,16},{2,18},{4,20},{6,22},{8,24},{10,26},{12,28},{14,30},{16,0},... | collective-permute-start | bytes 98312 | tf_op jit(solution)/shard_map/ppermute | solution.py:190
  7.9 2.0 %collective-permute-done.refs_1_ = bf16[1,128,128]{2,1,0:T(8,128)(2,1)S(1)} collective-permute-done((bf16[1,128,128]{2,1,0:T(8,128)(2,1)S(1)}, bf16[1,128,128]{2,1,0:T(8,128)(2,1)S(1)}, u32[]{:S(2)}, u32[]{:S(2)}) %collective-permute-start) | collective-permute-done | bytes 32800 | tf_op jit(solution)/shard_map/ppermute | solution.py:190
  9.9 1.9 %collective-permute-start.2 = (bf16[2,128,128]{2,1,0:T(8,128)(2,1)S(1)}, bf16[2,128,128]{2,1,0:T(8,128)(2,1)S(1)}, u32[]{:S(2)}, u32[]{:S(2)}) collective-permute-start(bf16[2,128,128]{2,1,0:T(8,128)(2,1)S(1)} %pad_maximum_fusion.1), channel_id=1, source_target_pairs={{0,8},{2,10},{4,12},{6,14},{8,0},{10,2},{12,4},{14,6},{16,24},{18,... | collective-permute-start | bytes 196616 | tf_op jit(solution)/shard_map/ppermute | solution.py:190
  11.8 2.4 %collective-permute-done.2.refs_0_ = bf16[2,128,128]{2,1,0:T(8,128)(2,1)S(1)} collective-permute-done((bf16[2,128,128]{2,1,0:T(8,128)(2,1)S(1)}, bf16[2,128,128]{2,1,0:T(8,128)(2,1)S(1)}, u32[]{:S(2)}, u32[]{:S(2)}) %collective-permute-start.2) | collective-permute-done | bytes 65568 | tf_op jit(solution)/shard_map/ppermute | solution.py:190
  14.3 0.0 copy-start.5
  14.3 1.8 %collective-permute-start.3 = (bf16[4,128,128]{2,1,0:T(8,128)(2,1)S(1)}, bf16[4,128,128]{2,1,0:T(8,128)(2,1)S(1)}, u32[]{:S(2)}, u32[]{:S(2)}) collective-permute-start(bf16[4,128,128]{2,1,0:T(8,128)(2,1)S(1)} %pad_maximum_fusion), channel_id=1, source_target_pairs={{0,4},{2,6},{4,0},{6,2},{8,12},{10,14},{12,8},{14,10},{16,20},{18,... | collective-permute-start | bytes 393224 | tf_op jit(solution)/shard_map/ppermute | solution.py:190
  16.1 0.0 copy-done.2
  16.1 0.0 copy-done.5
  16.1 0.7 %shard_map.108.own_ref = bf16[4,192,128]{2,1,0:T(8,128)(2,1)S(1)} custom-call(s32[1,4]{1,0:T(1,128)S(1)} %copy-done.5, bf16[4,192,128]{2,1,0:T(8,128)(2,1)S(1)} %bitcast.17), custom_call_target="tpu_custom_call" | custom-call | flops 1572864 | bytes 393216 | tf_op jit(solution)/shard_map/pallas_call | solution.py:56
  16.8 1.6 %collective-permute-start.7 = (bf16[4,192,128]{2,1,0:T(8,128)(2,1)S(1)}, bf16[4,192,128]{2,1,0:T(8,128)(2,1)S(1)}, u32[]{:S(2)}, u32[]{:S(2)}) collective-permute-start(bf16[4,192,128]{2,1,0:T(8,128)(2,1)S(1)} %shard_map.108.own_ref), channel_id=1, source_target_pairs={{0,1},{1,0},{2,3},{3,2},{4,5},{5,4},{6,7},{7,6},{8,9},{9,8},{10,11... | collective-permute-start | bytes 589832 | tf_op jit(solution)/shard_map/ppermute | solution.py:210
  18.4 0.0 collective-permute-done.1.refs_3_.refs_2_
  18.4 1.3 %shard_map.105 = f32[2,128]{1,0:T(2,128)S(1)} custom-call(bf16[2,128,128]{2,1,0:T(8,128)(2,1)S(1)} %collective-permute-done.2.refs_0_, bf16[16,192,128]{2,1,0:T(8,128)(2,1)S(1)} %shard_map.103.refs_2_.refs_1_, bf16[16,192,128]{2,1,0:T(8,128)(2,1)S(1)} %collective-permute-done.1.refs_3_.refs_2_), custom_call_target="tpu_custom_call" | custom-call | flops 402653184 | bytes 1572864 | tf_op jit(solution)/shard_map/pallas_call | solution.py:94
  19.7 1.3 %shard_map.104 = f32[2,128]{1,0:T(2,128)S(1)} custom-call(bf16[1,128,128]{2,1,0:T(8,128)(2,1)S(1)} %bitcast.15, bf16[1,128,128]{2,1,0:T(8,128)(2,1)S(1)} %collective-permute-done.refs_1_, bf16[16,192,128]{2,1,0:T(8,128)(2,1)S(1)} %shard_map.103.refs_2_.refs_1_, bf16[16,192,128]{2,1,0:T(8,128)(2,1)S(1)} %collective-permute-done.1.refs_3_.refs_2_), custom_call_target="tpu_custom_call" | custom-call | flops 402653184 | bytes 1572864 | tf_op jit(solution)/shard_map/pallas_call | solution.py:94
  20.9 0.0 collective-permute-done.3.refs_0_
  20.9 0.0 copy-start.7
  21.0 2.3 %shard_map.106 = f32[4,128]{1,0:T(4,128)S(1)} custom-call(bf16[4,128,128]{2,1,0:T(8,128)(2,1)S(1)} %collective-permute-done.3.refs_0_, bf16[16,192,128]{2,1,0:T(8,128)(2,1)S(1)} %shard_map.103.refs_2_.refs_1_, bf16[16,192,128]{2,1,0:T(8,128)(2,1)S(1)} %collective-permute-done.1.refs_3_.refs_2_), custom_call_target="tpu_custom_call" | custom-call | flops 805306368 | bytes 1572864 | tf_op jit(solution)/shard_map/pallas_call | solution.py:94
  23.3 0.6 %collective-permute-start.4 = (f32[1,4,128]{2,0,1:T(1,128)S(1)}, f32[1,4,128]{2,0,1:T(1,128)S(1)}, u32[]{:S(2)}, u32[]{:S(2)}) collective-permute-start(f32[1,4,128]{2,0,1:T(1,128)S(1)} %get-tuple-element.12), channel_id=1, source_target_pairs={{0,4},{2,6},{4,0},{6,2},{8,12},{10,14},{12,8},{14,10},{16,20},{18,... | collective-permute-start | bytes 6152 | tf_op jit(solution)/shard_map/ppermute | solution.py:190
  23.9 0.0 copy-done.7
  23.9 3.0 %collective-permute-done.4 = f32[1,4,128]{2,0,1:T(1,128)S(1)} collective-permute-done((f32[1,4,128]{2,0,1:T(1,128)S(1)}, f32[1,4,128]{2,0,1:T(1,128)S(1)}, u32[]{:S(2)}, u32[]{:S(2)}) %collective-permute-start.4) | collective-permute-done | bytes 2080 | tf_op jit(solution)/shard_map/ppermute | solution.py:190
  26.9 0.0 copy-start.6
  27.0 1.6 %collective-permute-start.5 = (f32[2,2,128]{2,0,1:T(2,128)S(1)}, f32[2,2,128]{2,0,1:T(2,128)S(1)}, u32[]{:S(2)}, u32[]{:S(2)}) collective-permute-start(f32[2,2,128]{2,0,1:T(2,128)S(1)} %get-tuple-element.10), channel_id=1, source_target_pairs={{0,8},{2,10},{4,12},{6,14},{8,0},{10,2},{12,4},{14,6},{16,24},{18,... | collective-permute-start | bytes 6152 | tf_op jit(solution)/shard_map/ppermute | solution.py:190
  28.6 0.0 copy-done.6
  28.6 2.0 %collective-permute-done.5 = f32[2,2,128]{2,0,1:T(2,128)S(1)} collective-permute-done((f32[2,2,128]{2,0,1:T(2,128)S(1)}, f32[2,2,128]{2,0,1:T(2,128)S(1)}, u32[]{:S(2)}, u32[]{:S(2)}) %collective-permute-start.5) | collective-permute-done | bytes 2080 | tf_op jit(solution)/shard_map/ppermute | solution.py:190
  30.6 2.6 %collective-permute-start.6 = (f32[4,1,128]{2,0,1:T(4,128)S(1)}, f32[4,1,128]{2,0,1:T(4,128)S(1)}, u32[]{:S(2)}, u32[]{:S(2)}) collective-permute-start(f32[4,1,128]{2,0,1:T(4,128)S(1)} %get-tuple-element.8), channel_id=1, source_target_pairs={{0,16},{2,18},{4,20},{6,22},{8,24},{10,26},{12,28},{14,30},{16,0},... | collective-permute-start | bytes 6152 | tf_op jit(solution)/shard_map/ppermute | solution.py:190
  33.2 0.0 collective-permute-done.7.other_ref
  33.2 1.1 %shard_map.109 = f32[1,4]{1,0:T(1,128)} custom-call(bf16[128,128]{1,0:T(8,128)(2,1)S(1)} %bitcast.16, bf16[4,192,128]{2,1,0:T(8,128)(2,1)S(1)} %shard_map.108.own_ref, bf16[4,192,128]{2,1,0:T(8,128)(2,1)S(1)} %collective-permute-done.7.other_ref), custom_call_target="tpu_custom_call" | custom-call | flops 50331648 | bytes 393216 | tf_op jit(solution)/shard_map/pallas_call | solution.py:130
  34.3 0.7 %collective-permute-done.6 = f32[4,1,128]{2,0,1:T(4,128)S(1)} collective-permute-done((f32[4,1,128]{2,0,1:T(4,128)S(1)}, f32[4,1,128]{2,0,1:T(4,128)S(1)}, u32[]{:S(2)}, u32[]{:S(2)}) %collective-permute-start.6) | collective-permute-done | bytes 2080 | tf_op jit(solution)/shard_map/ppermute | solution.py:190
  35.1 0.0 copy-start.3
  35.1 0.7 %copy-done.3 = f32[1,4,32]{2,1,0:T(4,128)S(1)} copy-done((f32[1,4,32]{2,1,0:T(4,128)S(1)}, f32[1,4,32]{2,1,0:T(4,128)}, u32[]{:S(2)}) %copy-start.3) | copy-done | bytes 536
  35.8 1.1 %shard_map.107 = (f32[1,4,32]{2,1,0:T(4,128)}, f32[1,4]{1,0:T(1,128)}) custom-call(f32[8,128]{1,0:T(8,128)S(1)} %maximum_bitcast_fusion.returned_ref, s32[4,32]{1,0:T(4,128)S(1)} %bitcast.18, s32[4,32]{1,0:T(4,128)S(1)} %bitcast_add_fusion.lane_ref, f32[1,4,32]{2,1,0:T(4,128)S(1)} %copy-done.3), custom_call_target="tpu_custom_call" | custom-call | tf_op jit(solution)/shard_map/pallas_call | solution.py:176
  (9 shorter events, 0.1 us)
Async XLA Ops:
  0.6 0.7 %copy-start.4 = (s32[1,16]{1,0:T(1,128)S(1)}, s32[1,16]{1,0:T(1,128)}, u32[]{:S(2)}) copy-start(s32[1,16]{1,0:T(1,128)} %kept_ref.2) | copy-start | bytes 196
  1.3 1.1 %copy-start = (bf16[1,16,192,128]{3,2,1,0:T(8,128)(2,1)S(1)}, bf16[1,16,192,128]{3,2,1,0:T(8,128)(2,1)}, u32[]{:S(2)}) copy-start(bf16[1,16,192,128]{3,2,1,0:T(8,128)(2,1)} %param.9) | copy-start | bytes 2359300
  2.4 1.8 %copy-start.1 = (bf16[1,4,32,128]{3,2,1,0:T(8,128)(2,1)S(1)}, bf16[1,4,32,128]{3,2,1,0:T(8,128)(2,1)}, u32[]{:S(2)}) copy-start(bf16[1,4,32,128]{3,2,1,0:T(8,128)(2,1)} %param.8) | copy-start | bytes 98308
  3.7 14.7 %collective-permute-start.1 = (bf16[16,192,128]{2,1,0:T(8,128)(2,1)S(1)}, bf16[16,192,128]{2,1,0:T(8,128)(2,1)S(1)}, u32[]{:S(2)}, u32[]{:S(2)}) collective-permute-start(bf16[16,192,128]{2,1,0:T(8,128)(2,1)S(1)} %shard_map.103.refs_2_.refs_1_), channel_id=1, source_target_pairs={{0,2},{2,0},{4,6},{6,4},{8,10},{10,8},{12,14},{14,12},{16,18},{18,... | collective-permute-start | bytes 2359304 | tf_op jit(solution)/shard_map/ppermute | solution.py:190
  4.2 11.9 %copy-start.2 = (bf16[1,4,192,128]{3,2,1,0:T(8,128)(2,1)S(1)}, bf16[1,4,192,128]{3,2,1,0:T(8,128)(2,1)}, u32[]{:S(2)}) copy-start(bf16[1,4,192,128]{3,2,1,0:T(8,128)(2,1)} %param.11) | copy-start | bytes 589828
  4.2 5.6 %collective-permute-start = (bf16[1,128,128]{2,1,0:T(8,128)(2,1)S(1)}, bf16[1,128,128]{2,1,0:T(8,128)(2,1)S(1)}, u32[]{:S(2)}, u32[]{:S(2)}) collective-permute-start(bf16[1,128,128]{2,1,0:T(8,128)(2,1)S(1)} %bitcast.12), channel_id=1, source_target_pairs={{0,16},{2,18},{4,20},{6,22},{8,24},{10,26},{12,28},{14,30},{16,0},... | collective-permute-start | bytes 98312 | tf_op jit(solution)/shard_map/ppermute | solution.py:190
  9.9 4.3 %collective-permute-start.2 = (bf16[2,128,128]{2,1,0:T(8,128)(2,1)S(1)}, bf16[2,128,128]{2,1,0:T(8,128)(2,1)S(1)}, u32[]{:S(2)}, u32[]{:S(2)}) collective-permute-start(bf16[2,128,128]{2,1,0:T(8,128)(2,1)S(1)} %pad_maximum_fusion.1), channel_id=1, source_target_pairs={{0,8},{2,10},{4,12},{6,14},{8,0},{10,2},{12,4},{14,6},{16,24},{18,... | collective-permute-start | bytes 196616 | tf_op jit(solution)/shard_map/ppermute | solution.py:190
  14.3 1.9 %copy-start.5 = (s32[1,4]{1,0:T(1,128)S(1)}, s32[1,4]{1,0:T(1,128)}, u32[]{:S(2)}) copy-start(s32[1,4]{1,0:T(1,128)} %kept_ref.3) | copy-start | bytes 52
  14.3 6.7 %collective-permute-start.3 = (bf16[4,128,128]{2,1,0:T(8,128)(2,1)S(1)}, bf16[4,128,128]{2,1,0:T(8,128)(2,1)S(1)}, u32[]{:S(2)}, u32[]{:S(2)}) collective-permute-start(bf16[4,128,128]{2,1,0:T(8,128)(2,1)S(1)} %pad_maximum_fusion), channel_id=1, source_target_pairs={{0,4},{2,6},{4,0},{6,2},{8,12},{10,14},{12,8},{14,10},{16,20},{18,... | collective-permute-start | bytes 393224 | tf_op jit(solution)/shard_map/ppermute | solution.py:190
  16.8 16.4 %collective-permute-start.7 = (bf16[4,192,128]{2,1,0:T(8,128)(2,1)S(1)}, bf16[4,192,128]{2,1,0:T(8,128)(2,1)S(1)}, u32[]{:S(2)}, u32[]{:S(2)}) collective-permute-start(bf16[4,192,128]{2,1,0:T(8,128)(2,1)S(1)} %shard_map.108.own_ref), channel_id=1, source_target_pairs={{0,1},{1,0},{2,3},{3,2},{4,5},{5,4},{6,7},{7,6},{8,9},{9,8},{10,11... | collective-permute-start | bytes 589832 | tf_op jit(solution)/shard_map/ppermute | solution.py:210
  20.9 3.0 %copy-start.7 = (s32[1,4,32,1]{2,3,1,0:T(1,128)S(1)}, s32[1,4,32,1]{2,3,1,0:T(1,128)}, u32[]{:S(2)}) copy-start(s32[1,4,32,1]{2,3,1,0:T(1,128)} %param.13) | copy-start | bytes 1540
  23.3 3.7 %collective-permute-start.4 = (f32[1,4,128]{2,0,1:T(1,128)S(1)}, f32[1,4,128]{2,0,1:T(1,128)S(1)}, u32[]{:S(2)}, u32[]{:S(2)}) collective-permute-start(f32[1,4,128]{2,0,1:T(1,128)S(1)} %get-tuple-element.12), channel_id=1, source_target_pairs={{0,4},{2,6},{4,0},{6,2},{8,12},{10,14},{12,8},{14,10},{16,20},{18,... | collective-permute-start | bytes 6152 | tf_op jit(solution)/shard_map/ppermute | solution.py:190
  26.9 1.6 %copy-start.6 = (s32[1,4,32]{2,1,0:T(4,128)S(1)}, s32[1,4,32]{2,1,0:T(4,128)}, u32[]{:S(2)}) copy-start(s32[1,4,32]{2,1,0:T(4,128)} %param.14) | copy-start | bytes 1540
  27.0 3.7 %collective-permute-start.5 = (f32[2,2,128]{2,0,1:T(2,128)S(1)}, f32[2,2,128]{2,0,1:T(2,128)S(1)}, u32[]{:S(2)}, u32[]{:S(2)}) collective-permute-start(f32[2,2,128]{2,0,1:T(2,128)S(1)} %get-tuple-element.10), channel_id=1, source_target_pairs={{0,8},{2,10},{4,12},{6,14},{8,0},{10,2},{12,4},{14,6},{16,24},{18,... | collective-permute-start | bytes 6152 | tf_op jit(solution)/shard_map/ppermute | solution.py:190
  30.6 4.5 %collective-permute-start.6 = (f32[4,1,128]{2,0,1:T(4,128)S(1)}, f32[4,1,128]{2,0,1:T(4,128)S(1)}, u32[]{:S(2)}, u32[]{:S(2)}) collective-permute-start(f32[4,1,128]{2,0,1:T(4,128)S(1)} %get-tuple-element.8), channel_id=1, source_target_pairs={{0,16},{2,18},{4,20},{6,22},{8,24},{10,26},{12,28},{14,30},{16,0},... | collective-permute-start | bytes 6152 | tf_op jit(solution)/shard_map/ppermute | solution.py:190
  35.1 0.7 %copy-start.3 = (f32[1,4,32]{2,1,0:T(4,128)S(1)}, f32[1,4,32]{2,1,0:T(4,128)}, u32[]{:S(2)}) copy-start(f32[1,4,32]{2,1,0:T(4,128)} %teacher_ref.1) | copy-start | bytes 1540

commit v2 on v1

--- a/solution.py
+++ b/solution.py
@@ -106,7 +106,19 @@
     )(*query_list, near, far)
 
 
-def contrast_kernel(qlen, query_ref, own_ref, other_ref, out_ref, best_ref):
+def flat_lanes(rows, pad_ref, lanes):
+    queries, width = rows.shape
+    pad_ref[:queries, :width] = rows
+    place = lax.broadcasted_iota(jnp.int32, (8, lanes), 1)
+    spread = jnp.take_along_axis(pad_ref[...], place % width, axis=1)
+    row = lax.broadcasted_iota(jnp.int32, (8, lanes), 0)
+    return jnp.sum(jnp.where(row == place // width, spread, 0), axis=0, keepdims=True)
+
+
+def early_kernel(
+    qlen, query_ref, own_ref, other_ref, where_ref, lane_ref, teacher_ref,
+    contrast_ref, teach_ref, index_ref, best_ref, pad_ref, ints_ref,
+):
     queries = unit(query_ref[...])
     lanes = queries.shape[0]
     docs = own_ref.shape[0]
@@ -121,69 +133,71 @@
     loss = jnp.log(jnp.sum(jnp.exp(logits), axis=0, keepdims=True)) - own
     place = (lax.broadcasted_iota(jnp.int32, (8, lanes), 1) * qlen) % lanes
     spread = jnp.take_along_axis(jnp.broadcast_to(loss, (8, lanes)), place, axis=1)
-    out_ref[...] = spread[0:1, : lanes // qlen]
-
-
-def contrast_loss(query_rows, own, other, qlen):
+    contrast_ref[...] = spread[0:1, : lanes // qlen]
+
+    count, width = teacher_ref.shape[1:]
+    teacher = flat_lanes(teacher_ref[0], pad_ref, lanes)
+    log_teacher = teacher - jnp.log(group_sum(jnp.exp(teacher), width))
+    teach_ref[0:1, :] = log_teacher
+    teach_ref[1:2, :] = jnp.exp(log_teacher)
+    index_ref[0:1, :] = flat_lanes(where_ref[...], ints_ref, lanes)
+    lane = flat_lanes(lane_ref[...], ints_ref, lanes)
+    index_ref[1:2, :] = lane + lax.broadcasted_iota(jnp.int32, (1, lanes), 1) // width * (lanes // count)
+
+
+def early(query_rows, own, other, whose, lane, teacher, qlen):
     lanes = query_rows.shape[0]
     total = own.shape[0] + other.shape[0]
     return pl.pallas_call(
-        functools.partial(contrast_kernel, qlen),
-        out_shape=jax.ShapeDtypeStruct((1, lanes // qlen), jnp.float32),
-        in_specs=[VMEM, VMEM, VMEM],
-        out_specs=VMEM,
-        scratch_shapes=[pltpu.VMEM((total, lanes), jnp.float32)],
+        functools.partial(early_kernel, qlen),
+        out_shape=(
+            jax.ShapeDtypeStruct(teacher.shape[:2], jnp.float32),
+            jax.ShapeDtypeStruct((2, lanes), jnp.float32),
+            jax.ShapeDtypeStruct((2, lanes), jnp.int32),
+        ),
+        in_specs=[VMEM] * 6,
+        out_specs=(VMEM, VMEM, VMEM),
+        scratch_shapes=[
+            pltpu.VMEM((total, lanes), jnp.float32),
+            pltpu.VMEM((8, lanes), jnp.float32),
+            pltpu.VMEM((8, lanes), jnp.int32),
+        ],
         compiler_params=pltpu.CompilerParams(vmem_limit_bytes=LIMIT),
         cost_estimate=pl.CostEstimate(
             flops=2 * lanes * own.shape[2] * total * own.shape[1], bytes_accessed=4 * own.size, transcendentals=0
         ),
-    )(query_rows, own, other)
-
-
-def flat_lanes(rows, pad_ref, lanes):
-    queries, width = rows.shape
-    pad_ref[:queries, :width] = rows
-    place = lax.broadcasted_iota(jnp.int32, (8, lanes), 1)
-    spread = jnp.take_along_axis(pad_ref[...], place % width, axis=1)
-    row = lax.broadcasted_iota(jnp.int32, (8, lanes), 0)
-    return jnp.sum(jnp.where(row == place // width, spread, 0), axis=0, keepdims=True)
-
-
-def distill_kernel(returned_ref, where_ref, lane_ref, teacher_ref, student_ref, distill_ref, pad_ref, ints_ref):
-    queries, width = teacher_ref.shape[1:]
+    )(query_rows, own, other, whose, lane, teacher)
+
+
+def distill_kernel(returned_ref, teach_ref, index_ref, student_ref, distill_ref):
+    queries, width = student_ref.shape[1:]
     scorers, lanes = returned_ref.shape
-    teacher = flat_lanes(teacher_ref[0], pad_ref, lanes)
-    whose = flat_lanes(where_ref[...], ints_ref, lanes)
-    lane = flat_lanes(lane_ref[...], ints_ref, lanes)
-    lane = lane + lax.broadcasted_iota(jnp.int32, (1, lanes), 1) // width * (lanes // queries)
-    returned = returned_ref[...]
-    picked = jnp.take_along_axis(returned, jnp.broadcast_to(lane, (scorers, lanes)), axis=1)
+    picked = jnp.take_along_axis(
+        returned_ref[...], jnp.broadcast_to(index_ref[1:2, :], (scorers, lanes)), axis=1
+    )
     row = lax.broadcasted_iota(jnp.int32, (scorers, lanes), 0)
-    student = jnp.sum(jnp.where(row == whose, picked, 0.0), axis=0, keepdims=True)
-    log_teacher = teacher - jnp.log(group_sum(jnp.exp(teacher), width))
-    log_student = student - jnp.log(group_sum(jnp.exp(student), width))
-    loss = group_sum(jnp.exp(log_teacher) * (log_teacher - log_student), width)
+    student = jnp.sum(jnp.where(row == index_ref[0:1, :], picked, 0.0), axis=0, keepdims=True)
     first = lax.broadcasted_iota(jnp.int32, (8, lanes), 0)
     place = lax.broadcasted_iota(jnp.int32, (8, lanes), 1)
     spread = jnp.take_along_axis(jnp.broadcast_to(student, (8, lanes)), (first * width + place) % lanes, axis=1)
     student_ref[0] = spread[:queries, :width]
+    log_student = student - jnp.log(group_sum(jnp.exp(student), width))
+    loss = group_sum(teach_ref[1:2, :] * (teach_ref[0:1, :] - log_student), width)
     spread = jnp.take_along_axis(jnp.broadcast_to(loss, (8, lanes)), (place * width) % lanes, axis=1)
     distill_ref[...] = spread[0:1, :queries]
 
 
-def distill_loss(returned, whose, lane, teacher):
-    lanes = returned.shape[1]
+def distill_loss(returned, teach, index, shape):
     return pl.pallas_call(
         distill_kernel,
         out_shape=(
-            jax.ShapeDtypeStruct(teacher.shape, jnp.float32),
-            jax.ShapeDtypeStruct(teacher.shape[:2], jnp.float32),
-        ),
-        in_specs=[VMEM] * 4,
+            jax.ShapeDtypeStruct(shape, jnp.float32),
+            jax.ShapeDtypeStruct(shape[:2], jnp.float32),
+        ),
+        in_specs=[VMEM] * 3,
         out_specs=(VMEM, VMEM),
-        scratch_shapes=[pltpu.VMEM((8, lanes), jnp.float32), pltpu.VMEM((8, lanes), jnp.int32)],
-        compiler_params=pltpu.CompilerParams(vmem_limit_bytes=LIMIT),
-    )(returned, whose, lane, teacher)
+        compiler_params=pltpu.CompilerParams(vmem_limit_bytes=LIMIT),
+    )(returned, teach, index)
 
 
 def swap(values, axis, bit):
@@ -199,11 +213,32 @@
     query_count, qlen = queries.shape[1:3]
     pass_count = passages.shape[1]
     own_rows = queries.reshape(1, query_count * qlen, queries.shape[3])
-    bits = [1 << n for n in range(1, peers.bit_length() - 1)]
-
-    first = swap(own_rows, "dp", bits[-1])
+    bits = [(1 << n) | 1 for n in range(1, peers.bit_length() - 1)]
+
+    tie = lax.optimization_barrier
+
+    last = bits[0]
+    held = fresh = own_rows
+    crossed = []
+    parts = []
     near = prepare(passages[0], passage_lengths)
-    far = swap(near, "dp", 1)
+    for n, bit in enumerate(reversed(bits[1:])):
+        got = swap(held, "dp", bit)
+        crossed.append(swap(fresh, "dp", last))
+        if n == 0:
+            near, got = tie((near, got))
+            far = swap(near, "dp", 1)
+            parts.append(score([own_rows, got], near, far, qlen))
+        else:
+            got, parts[-1] = tie((got, parts[-1]))
+            parts.append(score([got], near, far, qlen))
+        held, fresh = jnp.concatenate([held, got], axis=0), got
+    rest = score(crossed, near, far, qlen)
+    final = swap(fresh, "dp", last)
+    final, rest, parts[-1] = tie((final, rest, parts[-1]))
+    final = score([final], near, far, qlen)
+
+    final, positives, owners, local_ids = tie((final, positives, owners, local_ids))
     own_docs = prepare(positives[0], positive_lengths)
     other_docs = jnp.concatenate(
         [
@@ -212,23 +247,22 @@
         ],
         axis=0,
     )
-
-    held = jnp.concatenate([own_rows, first], axis=0)
-    scored = [score([own_rows, first], near, far, qlen)]
-    for bit in reversed(bits[:-1]):
-        got = swap(held, "dp", bit)
-        scored.append(score([got], near, far, qlen))
-        held = jnp.concatenate([held, got], axis=0)
-    contrast = contrast_loss(own_rows[0], own_docs, other_docs, qlen)
-
-    back = jnp.concatenate(scored, axis=0)[None]
-    for bit in bits:
+    apart = owners[0, :, :, 0] ^ me
+    odd = functools.reduce(lambda x, n: x ^ (apart >> n), range(1, peers.bit_length() - 1), apart) & 1
+    lane = odd * pass_count + local_ids[0]
+    contrast, teach, index = early(own_rows[0], own_docs, other_docs, apart >> 1, lane, teacher, qlen)
+
+    back = jnp.concatenate(parts + [rest, final], axis=0)[None]
+    for n, bit in enumerate(bits):
         half = back.shape[1] // 2
-        back = jnp.concatenate([back[:, :half], swap(back[:, half:], "dp", bit)], axis=0)
+        arrived = swap(back[:, half:], "dp", bit)
+        if n == 0:
+            arrived, own_docs = tie((arrived, own_docs))
+        if n == len(bits) - 1:
+            arrived, teach = tie((arrived, teach))
+        back = jnp.concatenate([back[:, :half], arrived], axis=0)
     returned = back.reshape(peers // 2, query_count * qlen)
-
-    apart = owners[0, :, :, 0] ^ me
-    student, distill = distill_loss(returned, apart >> 1, (apart & 1) * pass_count + local_ids[0], teacher)
+    student, distill = distill_loss(returned, teach, index, teacher.shape)
     return (student, distill, contrast)
 
 

time: 37 us -> 30.3 us (0.82)
  waiting for transfers between devices: 10.2 us -> 1.86 us
  starting transfers between devices: 14.4 us -> 16.4 us
  local copies, waits for them, and re-layouts: 2.49 us -> 1.85 us
    ppermute x7 -> x9, waiting for transfers between devices: 10.2 us -> 1.86 us  [swap(): lax.ppermute(values, axis, [(i, i ^ bit) for i in range(lax.axis_size(axi...]
    ppermute x7 -> x9, starting transfers between devices: 12.8 us -> 14.8 us  [swap(): lax.ppermute(values, axis, [(i, i ^ bit) for i in range(lax.axis_size(axi...]
    unnamed x16, local copies, waits for them, and re-layouts: 2.49 us -> 1.85 us
    pallas_call x3 -> x4, Pallas kernels: 4.8 us -> 5.01 us  [score(): pl.pallas_call(functools.partial(score_kernel, qlen, len(query_list)), ou...]
  transfers between devices with their start and end apart: 8 -> 10, of which waited for: 5 -> 1; matrix products, arithmetic and copies ran while one was open for 0% -> 0% of each run, Pallas kernels for 18% -> 23%
where the time goes in v2:
time: 30.3 us; the launch traced here: 30.1 us
  starting transfers between devices  16.4 us (54%)
  Pallas kernels  9.18 us (30%)
  waiting for transfers between devices  1.86 us (6%)
  local copies, waits for them, and re-layouts  1.85 us (6%)
  between operations  0.79 us (3%)
    ppermute x9, starting transfers between devices, swap(): lax.ppermute(values, axis, [(i, i ^ bit) for i in range(lax.axis_size(axi...  14.8 us
    pallas_call x4, Pallas kernels, score(): pl.pallas_call(functools.partial(score_kernel, qlen, len(query_list)), ou...  5.01 us
    pallas_call x2, Pallas kernels, prepare(): pl.pallas_call(prepare_kernel, out_shape=jax.ShapeDtypeStruct(rows.shape,...  2.02 us
    ppermute x9, waiting for transfers between devices, swap(): lax.ppermute(values, axis, [(i, i ^ bit) for i in range(lax.axis_size(axi...  1.86 us
    unnamed x16, local copies, waits for them, and re-layouts  1.85 us
    ppermute x1, starting transfers between devices, per_device(): lax.ppermute(own_docs, 'blk', [(i, (i + k) % groups) for i in range(group...  1.55 us
    pallas_call x1, Pallas kernels, early(): pl.pallas_call(functools.partial(early_kernel, qlen), out_shape=(jax.Shap...  1.17 us
    pallas_call x1, Pallas kernels, distill_loss(): pl.pallas_call(distill_kernel, out_shape=(jax.ShapeDtypeStruct(shape, jnp...  0.98 us
  transfers between devices with their start and end apart: 10, of which 1 were waited for; matrix products, arithmetic and copies ran while one was open for 0% of the time, Pallas kernels for 23%

profile of v2, /device:TPU:0, one launch (start us, length us, event | category | flops | bytes accessed | tf_op | source)
XLA Modules:
  0.0 30.1 jit_solution(14365982722981201329)
XLA Ops:
  0.6 0.0 copy-start.4
  0.6 3.5 %collective-permute-start = (bf16[1,128,128]{2,1,0:T(8,128)(2,1)}, bf16[1,128,128]{2,1,0:T(8,128)(2,1)S(1)}, u32[]{:S(2)}, u32[]{:S(2)}) collective-permute-start(bf16[1,128,128]{2,1,0:T(8,128)(2,1)} %bitcast.11), channel_id=1, source_target_pairs={{0,18},{2,16},{4,22},{6,20},{8,26},{10,24},{12,30},{14,28},{16,2},... | collective-permute-start | bytes 98312 | tf_op jit(solution)/shard_map/ppermute | solution.py:204
  4.2 0.0 copy-done.4
  4.2 0.0 copy-start
  4.2 1.1 %copy-done = bf16[1,16,192,128]{3,2,1,0:T(8,128)(2,1)S(1)} copy-done((bf16[1,16,192,128]{3,2,1,0:T(8,128)(2,1)S(1)}, bf16[1,16,192,128]{3,2,1,0:T(8,128)(2,1)}, u32[]{:S(2)}) %copy-start) | copy-done | bytes 786456
  5.3 0.0 copy-start.1
  5.3 1.3 %shard_map.103.refs_2_.refs_1_ = bf16[16,192,128]{2,1,0:T(8,128)(2,1)S(1)} custom-call(s32[1,16]{1,0:T(1,128)S(1)} %copy-done.4, bf16[16,192,128]{2,1,0:T(8,128)(2,1)S(1)} %bitcast.10), custom_call_target="tpu_custom_call" | custom-call | flops 6291456 | bytes 1572864 | tf_op jit(solution)/shard_map/pallas_call | solution.py:56
  6.6 0.0 collective-permute-done.refs_1_
  6.6 0.7 %collective-permute-start.2 = (bf16[16,192,128]{2,1,0:T(8,128)(2,1)S(1)}, bf16[16,192,128]{2,1,0:T(8,128)(2,1)S(1)}, u32[]{:S(2)}, u32[]{:S(2)}) collective-permute-start(bf16[16,192,128]{2,1,0:T(8,128)(2,1)S(1)} %shard_map.103.refs_2_.refs_1_), channel_id=1, source_target_pairs={{0,2},{2,0},{4,6},{6,4},{8,10},{10,8},{12,14},{14,12},{16,18},{18,... | collective-permute-start | bytes 2359304 | tf_op jit(solution)/shard_map/ppermute | solution.py:204
  7.4 0.0 copy-done.1
  7.4 1.3 %collective-permute-start.1 = (bf16[2,128,128]{2,1,0:T(8,128)(2,1)S(1)}, bf16[2,128,128]{2,1,0:T(8,128)(2,1)S(1)}, u32[]{:S(2)}, u32[]{:S(2)}) collective-permute-start(bf16[2,128,128]{2,1,0:T(8,128)(2,1)S(1)} %pad_maximum_fusion), channel_id=1, source_target_pairs={{0,10},{2,8},{4,14},{6,12},{8,2},{10,0},{12,6},{14,4},{16,26},{18,... | collective-permute-start | bytes 196616 | tf_op jit(solution)/shard_map/ppermute | solution.py:204
  8.7 1.6 %collective-permute-start.4 = (bf16[1,128,128]{2,1,0:T(8,128)(2,1)S(1)}, bf16[1,128,128]{2,1,0:T(8,128)(2,1)S(1)}, u32[]{:S(2)}, u32[]{:S(2)}) collective-permute-start(bf16[1,128,128]{2,1,0:T(8,128)(2,1)S(1)} %bitcast.13), channel_id=1, source_target_pairs={{0,6},{2,4},{4,2},{6,0},{8,14},{10,12},{12,10},{14,8},{16,22},{18,... | collective-permute-start | bytes 98312 | tf_op jit(solution)/shard_map/ppermute | solution.py:204
  10.3 0.1 collective-permute-start.5
  10.4 0.0 collective-permute-done.2.refs_3_.refs_2_
  10.4 1.3 %shard_map.104 = f32[2,128]{1,0:T(2,128)S(1)} custom-call(bf16[1,128,128]{2,1,0:T(8,128)(2,1)S(1)} %bitcast.14, bf16[1,128,128]{2,1,0:T(8,128)(2,1)S(1)} %collective-permute-done.refs_1_, bf16[16,192,128]{2,1,0:T(8,128)(2,1)S(1)} %shard_map.103.refs_2_.refs_1_, bf16[16,192,128]{2,1,0:T(8,128)(2,1)S(1)} %collective-permute-done.2.refs_3_.refs_2_), custom_call_target="tpu_custom_call" | custom-call | flops 402653184 | bytes 1572864 | tf_op jit(solution)/shard_map/pallas_call | solution.py:94
  11.7 0.0 collective-permute-done.1.refs_0_
  11.7 1.7 %collective-permute-start.3 = (bf16[2,128,128]{2,1,0:T(8,128)(2,1)S(1)}, bf16[2,128,128]{2,1,0:T(8,128)(2,1)S(1)}, u32[]{:S(2)}, u32[]{:S(2)}) collective-permute-start(bf16[2,128,128]{2,1,0:T(8,128)(2,1)S(1)} %collective-permute-done.1.refs_0_), channel_id=1, source_target_pairs={{0,6},{2,4},{4,2},{6,0},{8,14},{10,12},{12,10},{14,8},{16,22},{18,... | collective-permute-start | bytes 196616 | tf_op jit(solution)/shard_map/ppermute | solution.py:204
  13.4 1.3 %shard_map.106 = f32[2,128]{1,0:T(2,128)S(1)} custom-call(bf16[2,128,128]{2,1,0:T(8,128)(2,1)S(1)} %collective-permute-done.1.refs_0_, bf16[16,192,128]{2,1,0:T(8,128)(2,1)S(1)} %shard_map.103.refs_2_.refs_1_, bf16[16,192,128]{2,1,0:T(8,128)(2,1)S(1)} %collective-permute-done.2.refs_3_.refs_2_), custom_call_target="tpu_custom_call" | custom-call | flops 402653184 | bytes 1572864 | tf_op jit(solution)/shard_map/pallas_call | solution.py:94
  14.6 0.0 collective-permute-done.4.refs_0_
  14.6 0.0 collective-permute-done.5.refs_1_
  14.6 1.3 %shard_map.105 = f32[2,128]{1,0:T(2,128)S(1)} custom-call(bf16[1,128,128]{2,1,0:T(8,128)(2,1)S(1)} %collective-permute-done.4.refs_0_, bf16[1,128,128]{2,1,0:T(8,128)(2,1)S(1)} %collective-permute-done.5.refs_1_, bf16[16,192,128]{2,1,0:T(8,128)(2,1)S(1)} %shard_map.103.refs_2_.refs_1_, bf16[16,192,128]{2,1,0:T(8,128)(2,1)S(1)} %collective-permute-done.2.refs_3_.refs_2_), custom_call_target="tpu_custom_call" | custom-call | flops 402653184 | bytes 1572864 | tf_op jit(solution)/shard_map/pallas_call | solution.py:94
  15.9 0.0 copy-start.2
  15.9 0.0 collective-permute-done.3.refs_0_
  15.9 1.2 %shard_map.107 = f32[2,128]{1,0:T(2,128)S(1)} custom-call(bf16[2,128,128]{2,1,0:T(8,128)(2,1)S(1)} %collective-permute-done.3.refs_0_, bf16[16,192,128]{2,1,0:T(8,128)(2,1)S(1)} %shard_map.103.refs_2_.refs_1_, bf16[16,192,128]{2,1,0:T(8,128)(2,1)S(1)} %collective-permute-done.2.refs_3_.refs_2_), custom_call_target="tpu_custom_call" | custom-call | flops 402653184 | bytes 1572864 | tf_op jit(solution)/shard_map/pallas_call | solution.py:94
  17.2 0.0 copy-start.5
  17.2 1.2 %collective-permute-start.6 = (f32[1,4,128]{2,0,1:T(1,128)S(1)}, f32[1,4,128]{2,0,1:T(1,128)S(1)}, u32[]{:S(2)}, u32[]{:S(2)}) collective-permute-start(f32[1,4,128]{2,0,1:T(1,128)S(1)} %get-tuple-element.46), channel_id=1, source_target_pairs={{0,6},{2,4},{4,2},{6,0},{8,14},{10,12},{12,10},{14,8},{16,22},{18,... | collective-permute-start | bytes 6152 | tf_op jit(solution)/shard_map/ppermute | solution.py:204
  18.4 0.0 copy-done.2
  18.4 0.0 copy-done.5
  18.4 0.0 copy-start.6
  18.5 0.7 %shard_map.108.own_ref = bf16[4,192,128]{2,1,0:T(8,128)(2,1)S(1)} custom-call(s32[1,4]{1,0:T(1,128)S(1)} %copy-done.5, bf16[4,192,128]{2,1,0:T(8,128)(2,1)S(1)} %bitcast.16), custom_call_target="tpu_custom_call" | custom-call | flops 1572864 | bytes 393216 | tf_op jit(solution)/shard_map/pallas_call | solution.py:56
  19.2 1.6 %collective-permute-start.9 = (bf16[4,192,128]{2,1,0:T(8,128)(2,1)S(1)}, bf16[4,192,128]{2,1,0:T(8,128)(2,1)S(1)}, u32[]{:S(2)}, u32[]{:S(2)}) collective-permute-start(bf16[4,192,128]{2,1,0:T(8,128)(2,1)S(1)} %shard_map.108.own_ref), channel_id=1, source_target_pairs={{0,1},{1,0},{2,3},{3,2},{4,5},{5,4},{6,7},{7,6},{8,9},{9,8},{10,11... | collective-permute-start | bytes 589832 | tf_op jit(solution)/shard_map/ppermute | solution.py:245
  20.7 0.0 copy-done.6
  20.7 0.0 collective-permute-done.6
  20.8 0.0 copy-start.7
  20.8 1.2 %collective-permute-start.7 = (f32[2,2,128]{2,0,1:T(2,128)S(1)}, f32[2,2,128]{2,0,1:T(2,128)S(1)}, u32[]{:S(2)}, u32[]{:S(2)}) collective-permute-start(f32[2,2,128]{2,0,1:T(2,128)S(1)} %get-tuple-element.44), channel_id=1, source_target_pairs={{0,10},{2,8},{4,14},{6,12},{8,2},{10,0},{12,6},{14,4},{16,26},{18,... | collective-permute-start | bytes 6152 | tf_op jit(solution)/shard_map/ppermute | solution.py:204
  22.0 0.0 copy-done.7
  22.0 1.8 %collective-permute-done.7 = f32[2,2,128]{2,0,1:T(2,128)S(1)} collective-permute-done((f32[2,2,128]{2,0,1:T(2,128)S(1)}, f32[2,2,128]{2,0,1:T(2,128)S(1)}, u32[]{:S(2)}, u32[]{:S(2)}) %collective-permute-start.7) | collective-permute-done | bytes 2080 | tf_op jit(solution)/shard_map/ppermute | solution.py:204
  23.9 3.4 %collective-permute-start.8 = (f32[4,1,128]{2,0,1:T(4,128)S(1)}, f32[4,1,128]{2,0,1:T(4,128)S(1)}, u32[]{:S(2)}, u32[]{:S(2)}) collective-permute-start(f32[4,1,128]{2,0,1:T(4,128)S(1)} %get-tuple-element.42), channel_id=1, source_target_pairs={{0,18},{2,16},{4,22},{6,20},{8,26},{10,24},{12,30},{14,28},{16,2},... | collective-permute-start | bytes 6152 | tf_op jit(solution)/shard_map/ppermute | solution.py:204
  27.3 0.0 collective-permute-done.9.other_ref
  27.3 0.0 copy-start.3
  27.3 0.7 %copy-done.3 = f32[1,4,32]{2,1,0:T(4,128)S(1)} copy-done((f32[1,4,32]{2,1,0:T(4,128)S(1)}, f32[1,4,32]{2,1,0:T(4,128)}, u32[]{:S(2)}) %copy-start.3) | copy-done | bytes 536
  27.9 1.2 %shard_map.109 = (f32[1,4]{1,0:T(1,128)}, f32[2,128]{1,0:T(2,128)S(1)}, s32[2,128]{1,0:T(2,128)S(1)}) custom-call(bf16[128,128]{1,0:T(8,128)(2,1)S(1)} %bitcast.15, bf16[4,192,128]{2,1,0:T(8,128)(2,1)S(1)} %shard_map.108.own_ref, bf16[4,192,128]{2,1,0:T(8,128)(2,1)S(1)} %collective-permute-done.9.other_ref, s32[4,32]{1,0:T(4,128)S(1)} %get-tuple-element.48.where_ref, ...), custom_call_target="tpu_custom_call" | custom-call | flops 50331648 | bytes 393216 | tf_op jit(solution)/shard_map/pallas_call | solution.py:151
  29.1 0.0 collective-permute-done.8
  29.1 1.0 %shard_map.110 = (f32[1,4,32]{2,1,0:T(4,128)}, f32[1,4]{1,0:T(1,128)}) custom-call(f32[8,128]{1,0:T(8,128)S(1)} %maximum_bitcast_fusion.returned_ref, f32[2,128]{1,0:T(2,128)S(1)} %get-tuple-element.36.teach_ref, s32[2,128]{1,0:T(2,128)S(1)} %get-tuple-element.37.index_ref), custom_call_target="tpu_custom_call" | custom-call | tf_op jit(solution)/shard_map/pallas_call | solution.py:191
  (8 shorter events, 0.1 us)
Async XLA Ops:
  0.6 3.6 %copy-start.4 = (s32[1,16]{1,0:T(1,128)S(1)}, s32[1,16]{1,0:T(1,128)}, u32[]{:S(2)}) copy-start(s32[1,16]{1,0:T(1,128)} %kept_ref.2) | copy-start | bytes 196
  0.6 6.0 %collective-permute-start = (bf16[1,128,128]{2,1,0:T(8,128)(2,1)}, bf16[1,128,128]{2,1,0:T(8,128)(2,1)S(1)}, u32[]{:S(2)}, u32[]{:S(2)}) collective-permute-start(bf16[1,128,128]{2,1,0:T(8,128)(2,1)} %bitcast.11), channel_id=1, source_target_pairs={{0,18},{2,16},{4,22},{6,20},{8,26},{10,24},{12,30},{14,28},{16,2},... | collective-permute-start | bytes 98312 | tf_op jit(solution)/shard_map/ppermute | solution.py:204
  4.2 1.1 %copy-start = (bf16[1,16,192,128]{3,2,1,0:T(8,128)(2,1)S(1)}, bf16[1,16,192,128]{3,2,1,0:T(8,128)(2,1)}, u32[]{:S(2)}) copy-start(bf16[1,16,192,128]{3,2,1,0:T(8,128)(2,1)} %param.9) | copy-start | bytes 2359300
  5.3 2.1 %copy-start.1 = (bf16[1,4,32,128]{3,2,1,0:T(8,128)(2,1)S(1)}, bf16[1,4,32,128]{3,2,1,0:T(8,128)(2,1)}, u32[]{:S(2)}) copy-start(bf16[1,4,32,128]{3,2,1,0:T(8,128)(2,1)} %param.8) | copy-start | bytes 98308
  6.6 3.8 %collective-permute-start.2 = (bf16[16,192,128]{2,1,0:T(8,128)(2,1)S(1)}, bf16[16,192,128]{2,1,0:T(8,128)(2,1)S(1)}, u32[]{:S(2)}, u32[]{:S(2)}) collective-permute-start(bf16[16,192,128]{2,1,0:T(8,128)(2,1)S(1)} %shard_map.103.refs_2_.refs_1_), channel_id=1, source_target_pairs={{0,2},{2,0},{4,6},{6,4},{8,10},{10,8},{12,14},{14,12},{16,18},{18,... | collective-permute-start | bytes 2359304 | tf_op jit(solution)/shard_map/ppermute | solution.py:204
  7.4 4.3 %collective-permute-start.1 = (bf16[2,128,128]{2,1,0:T(8,128)(2,1)S(1)}, bf16[2,128,128]{2,1,0:T(8,128)(2,1)S(1)}, u32[]{:S(2)}, u32[]{:S(2)}) collective-permute-start(bf16[2,128,128]{2,1,0:T(8,128)(2,1)S(1)} %pad_maximum_fusion), channel_id=1, source_target_pairs={{0,10},{2,8},{4,14},{6,12},{8,2},{10,0},{12,6},{14,4},{16,26},{18,... | collective-permute-start | bytes 196616 | tf_op jit(solution)/shard_map/ppermute | solution.py:204
  8.7 6.0 %collective-permute-start.4 = (bf16[1,128,128]{2,1,0:T(8,128)(2,1)S(1)}, bf16[1,128,128]{2,1,0:T(8,128)(2,1)S(1)}, u32[]{:S(2)}, u32[]{:S(2)}) collective-permute-start(bf16[1,128,128]{2,1,0:T(8,128)(2,1)S(1)} %bitcast.13), channel_id=1, source_target_pairs={{0,6},{2,4},{4,2},{6,0},{8,14},{10,12},{12,10},{14,8},{16,22},{18,... | collective-permute-start | bytes 98312 | tf_op jit(solution)/shard_map/ppermute | solution.py:204
  10.3 4.4 %collective-permute-start.5 = (bf16[1,128,128]{2,1,0:T(8,128)(2,1)S(1)}, bf16[1,128,128]{2,1,0:T(8,128)(2,1)S(1)}, u32[]{:S(2)}, u32[]{:S(2)}) collective-permute-start(bf16[1,128,128]{2,1,0:T(8,128)(2,1)S(1)} %collective-permute-done.refs_1_), channel_id=1, source_target_pairs={{0,6},{2,4},{4,2},{6,0},{8,14},{10,12},{12,10},{14,8},{16,22},{18,... | collective-permute-start | bytes 98312 | tf_op jit(solution)/shard_map/ppermute | solution.py:204
  11.7 4.2 %collective-permute-start.3 = (bf16[2,128,128]{2,1,0:T(8,128)(2,1)S(1)}, bf16[2,128,128]{2,1,0:T(8,128)(2,1)S(1)}, u32[]{:S(2)}, u32[]{:S(2)}) collective-permute-start(bf16[2,128,128]{2,1,0:T(8,128)(2,1)S(1)} %collective-permute-done.1.refs_0_), channel_id=1, source_target_pairs={{0,6},{2,4},{4,2},{6,0},{8,14},{10,12},{12,10},{14,8},{16,22},{18,... | collective-permute-start | bytes 196616 | tf_op jit(solution)/shard_map/ppermute | solution.py:204
  15.9 2.6 %copy-start.2 = (bf16[1,4,192,128]{3,2,1,0:T(8,128)(2,1)S(1)}, bf16[1,4,192,128]{3,2,1,0:T(8,128)(2,1)}, u32[]{:S(2)}) copy-start(bf16[1,4,192,128]{3,2,1,0:T(8,128)(2,1)} %param.11) | copy-start | bytes 589828
  17.2 1.2 %copy-start.5 = (s32[1,4]{1,0:T(1,128)S(1)}, s32[1,4]{1,0:T(1,128)}, u32[]{:S(2)}) copy-start(s32[1,4]{1,0:T(1,128)} %kept_ref.3) | copy-start | bytes 52
  17.2 3.5 %collective-permute-start.6 = (f32[1,4,128]{2,0,1:T(1,128)S(1)}, f32[1,4,128]{2,0,1:T(1,128)S(1)}, u32[]{:S(2)}, u32[]{:S(2)}) collective-permute-start(f32[1,4,128]{2,0,1:T(1,128)S(1)} %get-tuple-element.46), channel_id=1, source_target_pairs={{0,6},{2,4},{4,2},{6,0},{8,14},{10,12},{12,10},{14,8},{16,22},{18,... | collective-permute-start | bytes 6152 | tf_op jit(solution)/shard_map/ppermute | solution.py:204
  18.4 2.3 %copy-start.6 = (s32[1,4,32,1]{2,3,1,0:T(1,128)S(1)}, s32[1,4,32,1]{2,3,1,0:T(1,128)}, u32[]{:S(2)}) copy-start(s32[1,4,32,1]{2,3,1,0:T(1,128)} %param.13) | copy-start | bytes 1540
  19.2 8.1 %collective-permute-start.9 = (bf16[4,192,128]{2,1,0:T(8,128)(2,1)S(1)}, bf16[4,192,128]{2,1,0:T(8,128)(2,1)S(1)}, u32[]{:S(2)}, u32[]{:S(2)}) collective-permute-start(bf16[4,192,128]{2,1,0:T(8,128)(2,1)S(1)} %shard_map.108.own_ref), channel_id=1, source_target_pairs={{0,1},{1,0},{2,3},{3,2},{4,5},{5,4},{6,7},{7,6},{8,9},{9,8},{10,11... | collective-permute-start | bytes 589832 | tf_op jit(solution)/shard_map/ppermute | solution.py:245
  20.8 1.2 %copy-start.7 = (s32[1,4,32]{2,1,0:T(4,128)S(1)}, s32[1,4,32]{2,1,0:T(4,128)}, u32[]{:S(2)}) copy-start(s32[1,4,32]{2,1,0:T(4,128)} %param.14) | copy-start | bytes 1540
  20.8 3.1 %collective-permute-start.7 = (f32[2,2,128]{2,0,1:T(2,128)S(1)}, f32[2,2,128]{2,0,1:T(2,128)S(1)}, u32[]{:S(2)}, u32[]{:S(2)}) collective-permute-start(f32[2,2,128]{2,0,1:T(2,128)S(1)} %get-tuple-element.44), channel_id=1, source_target_pairs={{0,10},{2,8},{4,14},{6,12},{8,2},{10,0},{12,6},{14,4},{16,26},{18,... | collective-permute-start | bytes 6152 | tf_op jit(solution)/shard_map/ppermute | solution.py:204
  23.9 5.3 %collective-permute-start.8 = (f32[4,1,128]{2,0,1:T(4,128)S(1)}, f32[4,1,128]{2,0,1:T(4,128)S(1)}, u32[]{:S(2)}, u32[]{:S(2)}) collective-permute-start(f32[4,1,128]{2,0,1:T(4,128)S(1)} %get-tuple-element.42), channel_id=1, source_target_pairs={{0,18},{2,16},{4,22},{6,20},{8,26},{10,24},{12,30},{14,28},{16,2},... | collective-permute-start | bytes 6152 | tf_op jit(solution)/shard_map/ppermute | solution.py:204
  27.3 0.7 %copy-start.3 = (f32[1,4,32]{2,1,0:T(4,128)S(1)}, f32[1,4,32]{2,1,0:T(4,128)}, u32[]{:S(2)}) copy-start(f32[1,4,32]{2,1,0:T(4,128)} %teacher_ref.1) | copy-start | bytes 1540

commit v3 on v2

--- a/solution.py
+++ b/solution.py
@@ -33,8 +33,10 @@
     rest = values - high.astype(jnp.float32)
     middle = rest.astype(jnp.bfloat16)
     low = (rest - middle.astype(jnp.float32)).astype(jnp.bfloat16)
-    parts = [jnp.dot(part, same, preferred_element_type=jnp.float32) for part in (high, middle, low)]
-    return parts[0] + (parts[1] + parts[2])
+    stacked = jnp.concatenate([high, middle, low], axis=0)
+    sums = jnp.dot(stacked, same, preferred_element_type=jnp.float32)
+    count = values.shape[0]
+    return sums[:count] + (sums[count : 2 * count] + sums[2 * count :])
 
 
 def best_match(tokens, query_rows):
@@ -115,10 +117,7 @@
     return jnp.sum(jnp.where(row == place // width, spread, 0), axis=0, keepdims=True)
 
 
-def early_kernel(
-    qlen, query_ref, own_ref, other_ref, where_ref, lane_ref, teacher_ref,
-    contrast_ref, teach_ref, index_ref, best_ref, pad_ref, ints_ref,
-):
+def contrast_kernel(qlen, query_ref, own_ref, other_ref, contrast_ref, best_ref):
     queries = unit(query_ref[...])
     lanes = queries.shape[0]
     docs = own_ref.shape[0]
@@ -135,7 +134,26 @@
     spread = jnp.take_along_axis(jnp.broadcast_to(loss, (8, lanes)), place, axis=1)
     contrast_ref[...] = spread[0:1, : lanes // qlen]
 
+
+def contrast_loss(query_rows, own, other, qlen):
+    lanes = query_rows.shape[0]
+    total = own.shape[0] + other.shape[0]
+    return pl.pallas_call(
+        functools.partial(contrast_kernel, qlen),
+        out_shape=jax.ShapeDtypeStruct((1, lanes // qlen), jnp.float32),
+        in_specs=[VMEM] * 3,
+        out_specs=VMEM,
+        scratch_shapes=[pltpu.VMEM((total, lanes), jnp.float32)],
+        compiler_params=pltpu.CompilerParams(vmem_limit_bytes=LIMIT),
+        cost_estimate=pl.CostEstimate(
+            flops=2 * lanes * own.shape[2] * total * own.shape[1], bytes_accessed=4 * own.size, transcendentals=0
+        ),
+    )(query_rows, own, other)
+
+
+def teach_kernel(where_ref, lane_ref, teacher_ref, teach_ref, index_ref, pad_ref, ints_ref):
     count, width = teacher_ref.shape[1:]
+    lanes = teach_ref.shape[1]
     teacher = flat_lanes(teacher_ref[0], pad_ref, lanes)
     log_teacher = teacher - jnp.log(group_sum(jnp.exp(teacher), width))
     teach_ref[0:1, :] = log_teacher
@@ -145,28 +163,18 @@
     index_ref[1:2, :] = lane + lax.broadcasted_iota(jnp.int32, (1, lanes), 1) // width * (lanes // count)
 
 
-def early(query_rows, own, other, whose, lane, teacher, qlen):
-    lanes = query_rows.shape[0]
-    total = own.shape[0] + other.shape[0]
-    return pl.pallas_call(
-        functools.partial(early_kernel, qlen),
+def teach_rows(whose, lane, teacher, lanes):
+    return pl.pallas_call(
+        teach_kernel,
         out_shape=(
-            jax.ShapeDtypeStruct(teacher.shape[:2], jnp.float32),
             jax.ShapeDtypeStruct((2, lanes), jnp.float32),
             jax.ShapeDtypeStruct((2, lanes), jnp.int32),
         ),
-        in_specs=[VMEM] * 6,
-        out_specs=(VMEM, VMEM, VMEM),
-        scratch_shapes=[
-            pltpu.VMEM((total, lanes), jnp.float32),
-            pltpu.VMEM((8, lanes), jnp.float32),
-            pltpu.VMEM((8, lanes), jnp.int32),
-        ],
-        compiler_params=pltpu.CompilerParams(vmem_limit_bytes=LIMIT),
-        cost_estimate=pl.CostEstimate(
-            flops=2 * lanes * own.shape[2] * total * own.shape[1], bytes_accessed=4 * own.size, transcendentals=0
-        ),
-    )(query_rows, own, other, whose, lane, teacher)
+        in_specs=[VMEM] * 3,
+        out_specs=(VMEM, VMEM),
+        scratch_shapes=[pltpu.VMEM((8, lanes), jnp.float32), pltpu.VMEM((8, lanes), jnp.int32)],
+        compiler_params=pltpu.CompilerParams(vmem_limit_bytes=LIMIT),
+    )(whose, lane, teacher)
 
 
 def distill_kernel(returned_ref, teach_ref, index_ref, student_ref, distill_ref):
@@ -218,28 +226,21 @@
     tie = lax.optimization_barrier
 
     last = bits[0]
-    held = fresh = own_rows
+    near = prepare(passages[0], passage_lengths)
+    got = swap(own_rows, "dp", bits[-1])
+    near, positives, got = tie((near, positives, got))
+    far = swap(near, "dp", 1)
+    own_docs = prepare(positives[0], positive_lengths)
+    parts = [got]
+    held = jnp.concatenate([own_rows, got], axis=0)
     crossed = []
-    parts = []
-    near = prepare(passages[0], passage_lengths)
-    for n, bit in enumerate(reversed(bits[1:])):
+    for n, bit in enumerate(reversed(bits[1:-1])):
         got = swap(held, "dp", bit)
-        crossed.append(swap(fresh, "dp", last))
+        crossed.append(swap(held if n == 0 else parts[-1], "dp", last))
         if n == 0:
-            near, got = tie((near, got))
-            far = swap(near, "dp", 1)
-            parts.append(score([own_rows, got], near, far, qlen))
-        else:
-            got, parts[-1] = tie((got, parts[-1]))
-            parts.append(score([got], near, far, qlen))
-        held, fresh = jnp.concatenate([held, got], axis=0), got
-    rest = score(crossed, near, far, qlen)
-    final = swap(fresh, "dp", last)
-    final, rest, parts[-1] = tie((final, rest, parts[-1]))
-    final = score([final], near, far, qlen)
-
-    final, positives, owners, local_ids = tie((final, positives, owners, local_ids))
-    own_docs = prepare(positives[0], positive_lengths)
+            got, own_docs = tie((got, own_docs))
+        parts.append(got)
+        held = jnp.concatenate([held, got], axis=0)
     other_docs = jnp.concatenate(
         [
             lax.ppermute(own_docs, "blk", [(i, (i + k) % groups) for i in range(groups)])
@@ -247,21 +248,36 @@
         ],
         axis=0,
     )
-    apart = owners[0, :, :, 0] ^ me
-    odd = functools.reduce(lambda x, n: x ^ (apart >> n), range(1, peers.bit_length() - 1), apart) & 1
-    lane = odd * pass_count + local_ids[0]
-    contrast, teach, index = early(own_rows[0], own_docs, other_docs, apart >> 1, lane, teacher, qlen)
-
-    back = jnp.concatenate(parts + [rest, final], axis=0)[None]
-    for n, bit in enumerate(bits):
+    early_cross = score(crossed, near, far, qlen)
+    late_cross = swap(parts[-1], "dp", last)
+    late_cross, early_cross = tie((late_cross, early_cross))
+    late_cross = score([late_cross], near, far, qlen)
+
+    gate = jnp.concatenate([early_cross, late_cross], axis=0)
+    arrived = swap(gate[None], "dp", last)
+    back = arrived
+    for n, bit in enumerate(bits[1:]):
         half = back.shape[1] // 2
-        arrived = swap(back[:, half:], "dp", bit)
+        rows = [parts[-1 - n]] if n < len(bits) - 2 else [own_rows, parts[0]]
+        rows, gate = tie((rows, gate))
+        mine = score(rows, near, far, qlen)
+        arrived, mine = tie((arrived, mine))
         if n == 0:
-            arrived, own_docs = tie((arrived, own_docs))
-        if n == len(bits) - 1:
-            arrived, teach = tie((arrived, teach))
+            back = arrived
+        gate = arrived
+        leaving = jnp.concatenate([mine[None, -half:], back[:, half:]], axis=0)
+        if n == len(bits) - 2:
+            leaving, other_docs, owners = tie((leaving, other_docs, owners))
+            apart = owners[0, :, :, 0] ^ me
+            odd = functools.reduce(lambda x, m: x ^ (apart >> m), range(1, peers.bit_length() - 1), apart) & 1
+            lane = odd * pass_count + local_ids[0]
+            teach, index = teach_rows(apart >> 1, lane, teacher, query_count * qlen)
+            contrast = contrast_loss(own_rows[0], own_docs, other_docs, qlen)
+        arrived = swap(leaving, "dp", bit)
+        if n == len(bits) - 2:
+            arrived, contrast, teach = tie((arrived, contrast, teach))
         back = jnp.concatenate([back[:, :half], arrived], axis=0)
-    returned = back.reshape(peers // 2, query_count * qlen)
+    returned = jnp.concatenate([mine[:1], back[:, 0]], axis=0)
     student, distill = distill_loss(returned, teach, index, teacher.shape)
     return (student, distill, contrast)
 

time: 30.3 us -> 28.9 us (0.954)
  starting transfers between devices: 16.4 us -> 15.3 us
  waiting for transfers between devices: 1.86 us -> 1.52 us
    ppermute x9 -> x8, starting transfers between devices: 14.8 us -> 13.9 us  [swap(): lax.ppermute(values, axis, [(i, i ^ bit) for i in range(lax.axis_size(axi...]
    ppermute x9 -> x8, waiting for transfers between devices: 1.86 us -> 1.52 us  [swap(): lax.ppermute(values, axis, [(i, i ^ bit) for i in range(lax.axis_size(axi...]
    pallas_call x1 -> x2, Pallas kernels: 1.17 us -> 1.35 us  [the longest x1 1.13 us: contrast_loss(): pl.pallas_call(functools.partial(contrast_kernel, qlen), out_shape=jax.Sh...]
  transfers between devices with their start and end apart: 10 -> 9, of which waited for: 1 -> 3; matrix products, arithmetic and copies ran while one was open for 0% -> 0% of each run, Pallas kernels for 23% -> 29%
where the time goes in v3:
time: 28.9 us; the launch traced here: 28.7 us
  starting transfers between devices  15.3 us (53%)
  Pallas kernels  9.15 us (32%)
  local copies, waits for them, and re-layouts  1.84 us (6%)
  waiting for transfers between devices  1.52 us (5%)
  between operations  0.75 us (3%)
    ppermute x8, starting transfers between devices, swap(): lax.ppermute(values, axis, [(i, i ^ bit) for i in range(lax.axis_size(axi...  13.9 us
    pallas_call x4, Pallas kernels, score(): pl.pallas_call(functools.partial(score_kernel, qlen, len(query_list)), ou...  4.85 us
    pallas_call x2, Pallas kernels, prepare(): pl.pallas_call(prepare_kernel, out_shape=jax.ShapeDtypeStruct(rows.shape,...  2.02 us
    unnamed x16, local copies, waits for them, and re-layouts  1.84 us
    ppermute x8, waiting for transfers between devices, swap(): lax.ppermute(values, axis, [(i, i ^ bit) for i in range(lax.axis_size(axi...  1.52 us
    ppermute x1, starting transfers between devices, per_device(): lax.ppermute(own_docs, 'blk', [(i, (i + k) % groups) for i in range(group...  1.49 us
    pallas_call x1, Pallas kernels, contrast_loss(): pl.pallas_call(functools.partial(contrast_kernel, qlen), out_shape=jax.Sh...  1.13 us
    pallas_call x1, Pallas kernels, distill_loss(): pl.pallas_call(distill_kernel, out_shape=(jax.ShapeDtypeStruct(shape, jnp...  0.93 us
  transfers between devices with their start and end apart: 9, of which 3 were waited for; matrix products, arithmetic and copies ran while one was open for 0% of the time, Pallas kernels for 29%

profile of v3, /device:TPU:0, one launch (start us, length us, event | category | flops | bytes accessed | tf_op | source)
XLA Modules:
  0.0 28.7 jit_solution(10166785658424115094)
XLA Ops:
  0.6 0.0 copy-start.4
  0.6 3.5 %collective-permute-start = (bf16[1,128,128]{2,1,0:T(8,128)(2,1)}, bf16[1,128,128]{2,1,0:T(8,128)(2,1)S(1)}, u32[]{:S(2)}, u32[]{:S(2)}) collective-permute-start(bf16[1,128,128]{2,1,0:T(8,128)(2,1)} %bitcast.16), channel_id=1, source_target_pairs={{0,18},{2,16},{4,22},{6,20},{8,26},{10,24},{12,30},{14,28},{16,2},... | collective-permute-start | bytes 98312 | tf_op jit(solution)/shard_map/ppermute | solution.py:212
  4.2 0.0 copy-done.4
  4.2 0.0 copy-start
  4.2 1.1 %copy-done = bf16[1,16,192,128]{3,2,1,0:T(8,128)(2,1)S(1)} copy-done((bf16[1,16,192,128]{3,2,1,0:T(8,128)(2,1)S(1)}, bf16[1,16,192,128]{3,2,1,0:T(8,128)(2,1)}, u32[]{:S(2)}) %copy-start) | copy-done | bytes 786456
  5.3 0.0 copy-start.1
  5.3 0.0 copy-start.2
  5.3 1.3 %shard_map.103.refs_1_.refs_2_ = bf16[16,192,128]{2,1,0:T(8,128)(2,1)S(1)} custom-call(s32[1,16]{1,0:T(1,128)S(1)} %copy-done.4, bf16[16,192,128]{2,1,0:T(8,128)(2,1)S(1)} %bitcast.15), custom_call_target="tpu_custom_call" | custom-call | flops 6291456 | bytes 1572864 | tf_op jit(solution)/shard_map/pallas_call | solution.py:58
  6.6 0.0 collective-permute-done.refs_1_
  6.6 0.7 %collective-permute-start.4 = (bf16[16,192,128]{2,1,0:T(8,128)(2,1)S(1)}, bf16[16,192,128]{2,1,0:T(8,128)(2,1)S(1)}, u32[]{:S(2)}, u32[]{:S(2)}) collective-permute-start(bf16[16,192,128]{2,1,0:T(8,128)(2,1)S(1)} %shard_map.103.refs_1_.refs_2_), channel_id=1, source_target_pairs={{0,2},{2,0},{4,6},{6,4},{8,10},{10,8},{12,14},{14,12},{16,18},{18,... | collective-permute-start | bytes 2359304 | tf_op jit(solution)/shard_map/ppermute | solution.py:212
  7.4 0.0 copy-done.1
  7.4 0.0 copy-start.5
  7.4 1.3 %collective-permute-start.1 = (bf16[2,128,128]{2,1,0:T(8,128)(2,1)S(1)}, bf16[2,128,128]{2,1,0:T(8,128)(2,1)S(1)}, u32[]{:S(2)}, u32[]{:S(2)}) collective-permute-start(bf16[2,128,128]{2,1,0:T(8,128)(2,1)S(1)} %pad_maximum_fusion), channel_id=1, source_target_pairs={{0,10},{2,8},{4,14},{6,12},{8,2},{10,0},{12,6},{14,4},{16,26},{18,... | collective-permute-start | bytes 196616 | tf_op jit(solution)/shard_map/ppermute | solution.py:212
  8.7 1.6 %collective-permute-start.3 = (bf16[2,128,128]{2,1,0:T(8,128)(2,1)S(1)}, bf16[2,128,128]{2,1,0:T(8,128)(2,1)S(1)}, u32[]{:S(2)}, u32[]{:S(2)}) collective-permute-start(bf16[2,128,128]{2,1,0:T(8,128)(2,1)S(1)} %pad_maximum_fusion), channel_id=1, source_target_pairs={{0,6},{2,4},{4,2},{6,0},{8,14},{10,12},{12,10},{14,8},{16,22},{18,... | collective-permute-start | bytes 196616 | tf_op jit(solution)/shard_map/ppermute | solution.py:212
  10.3 0.0 copy-done.2
  10.3 0.0 copy-done.5
  10.3 0.7 %shard_map.104.own_ref = bf16[4,192,128]{2,1,0:T(8,128)(2,1)S(1)} custom-call(s32[1,4]{1,0:T(1,128)S(1)} %copy-done.5, bf16[4,192,128]{2,1,0:T(8,128)(2,1)S(1)} %bitcast.20), custom_call_target="tpu_custom_call" | custom-call | flops 1572864 | bytes 393216 | tf_op jit(solution)/shard_map/pallas_call | solution.py:58
  11.0 0.6 %collective-permute-done.1.refs_0_ = bf16[2,128,128]{2,1,0:T(8,128)(2,1)S(1)} collective-permute-done((bf16[2,128,128]{2,1,0:T(8,128)(2,1)S(1)}, bf16[2,128,128]{2,1,0:T(8,128)(2,1)S(1)}, u32[]{:S(2)}, u32[]{:S(2)}) %collective-permute-start.1) | collective-permute-done | bytes 65568 | tf_op jit(solution)/shard_map/ppermute | solution.py:212
  11.7 1.4 %collective-permute-start.2 = (bf16[2,128,128]{2,1,0:T(8,128)(2,1)S(1)}, bf16[2,128,128]{2,1,0:T(8,128)(2,1)S(1)}, u32[]{:S(2)}, u32[]{:S(2)}) collective-permute-start(bf16[2,128,128]{2,1,0:T(8,128)(2,1)S(1)} %collective-permute-done.1.refs_0_), channel_id=1, source_target_pairs={{0,6},{2,4},{4,2},{6,0},{8,14},{10,12},{12,10},{14,8},{16,22},{18,... | collective-permute-start | bytes 196616 | tf_op jit(solution)/shard_map/ppermute | solution.py:212
  13.1 1.5 %collective-permute-start.7 = (bf16[4,192,128]{2,1,0:T(8,128)(2,1)S(1)}, bf16[4,192,128]{2,1,0:T(8,128)(2,1)S(1)}, u32[]{:S(2)}, u32[]{:S(2)}) collective-permute-start(bf16[4,192,128]{2,1,0:T(8,128)(2,1)S(1)} %shard_map.104.own_ref), channel_id=1, source_target_pairs={{0,1},{1,0},{2,3},{3,2},{4,5},{5,4},{6,7},{7,6},{8,9},{9,8},{10,11... | collective-permute-start | bytes 589832 | tf_op jit(solution)/shard_map/ppermute | solution.py:246
  14.6 0.0 collective-permute-done.3.refs_0_
  14.6 0.0 collective-permute-done.4.refs_2_.refs_3_
  14.6 1.2 %shard_map.105 = f32[2,128]{1,0:T(2,128)S(1)} custom-call(bf16[2,128,128]{2,1,0:T(8,128)(2,1)S(1)} %collective-permute-done.3.refs_0_, bf16[16,192,128]{2,1,0:T(8,128)(2,1)S(1)} %shard_map.103.refs_1_.refs_2_, bf16[16,192,128]{2,1,0:T(8,128)(2,1)S(1)} %collective-permute-done.4.refs_2_.refs_3_), custom_call_target="tpu_custom_call" | custom-call | flops 402653184 | bytes 1572864 | tf_op jit(solution)/shard_map/pallas_call | solution.py:96
  15.8 0.0 collective-permute-done.2.refs_0_
  15.8 1.2 %shard_map.106 = f32[2,128]{1,0:T(2,128)S(1)} custom-call(bf16[2,128,128]{2,1,0:T(8,128)(2,1)S(1)} %collective-permute-done.2.refs_0_, bf16[16,192,128]{2,1,0:T(8,128)(2,1)S(1)} %shard_map.103.refs_1_.refs_2_, bf16[16,192,128]{2,1,0:T(8,128)(2,1)S(1)} %collective-permute-done.4.refs_2_.refs_3_), custom_call_target="tpu_custom_call" | custom-call | flops 402653184 | bytes 1572864 | tf_op jit(solution)/shard_map/pallas_call | solution.py:96
  17.1 1.5 %collective-permute-start.5 = (f32[1,4,128]{2,0,1:T(1,128)S(1)}, f32[1,4,128]{2,0,1:T(1,128)S(1)}, u32[]{:S(2)}, u32[]{:S(2)}) collective-permute-start(f32[1,4,128]{2,0,1:T(1,128)S(1)} %bitcast.23), channel_id=1, source_target_pairs={{0,6},{2,4},{4,2},{6,0},{8,14},{10,12},{12,10},{14,8},{16,22},{18,... | collective-permute-start | bytes 6152 | tf_op jit(solution)/shard_map/ppermute | solution.py:212
  18.6 1.2 %shard_map.107 = f32[2,128]{1,0:T(2,128)S(1)} custom-call(bf16[2,128,128]{2,1,0:T(8,128)(2,1)S(1)} %collective-permute-done.1.refs_0_, bf16[16,192,128]{2,1,0:T(8,128)(2,1)S(1)} %shard_map.103.refs_1_.refs_2_, bf16[16,192,128]{2,1,0:T(8,128)(2,1)S(1)} %collective-permute-done.4.refs_2_.refs_3_), custom_call_target="tpu_custom_call" | custom-call | flops 402653184 | bytes 1572864 | tf_op jit(solution)/shard_map/pallas_call | solution.py:96
  19.8 0.4 %collective-permute-done.5 = f32[1,4,128]{2,0,1:T(1,128)S(1)} collective-permute-done((f32[1,4,128]{2,0,1:T(1,128)S(1)}, f32[1,4,128]{2,0,1:T(1,128)S(1)}, u32[]{:S(2)}, u32[]{:S(2)}) %collective-permute-start.5) | collective-permute-done | bytes 2080 | tf_op jit(solution)/shard_map/ppermute | solution.py:212
  20.2 1.3 %collective-permute-start.6 = (f32[2,2,128]{2,0,1:T(2,128)S(1)}, f32[2,2,128]{2,0,1:T(2,128)S(1)}, u32[]{:S(2)}, u32[]{:S(2)}) collective-permute-start(f32[2,2,128]{2,0,1:T(2,128)S(1)} %pad_maximum_fusion.4), channel_id=1, source_target_pairs={{0,10},{2,8},{4,14},{6,12},{8,2},{10,0},{12,6},{14,4},{16,26},{18,... | collective-permute-start | bytes 6152 | tf_op jit(solution)/shard_map/ppermute | solution.py:212
  21.5 0.0 copy-start.7
  21.5 1.2 %shard_map.108 = f32[2,128]{1,0:T(2,128)S(1)} custom-call(bf16[1,128,128]{2,1,0:T(8,128)(2,1)S(1)} %bitcast.18, bf16[1,128,128]{2,1,0:T(8,128)(2,1)S(1)} %collective-permute-done.refs_1_, bf16[16,192,128]{2,1,0:T(8,128)(2,1)S(1)} %shard_map.103.refs_1_.refs_2_, bf16[16,192,128]{2,1,0:T(8,128)(2,1)S(1)} %collective-permute-done.4.refs_2_.refs_3_), custom_call_target="tpu_custom_call" | custom-call | flops 402653184 | bytes 1572864 | tf_op jit(solution)/shard_map/pallas_call | solution.py:96
  22.7 0.5 %collective-permute-done.6 = f32[2,2,128]{2,0,1:T(2,128)S(1)} collective-permute-done((f32[2,2,128]{2,0,1:T(2,128)S(1)}, f32[2,2,128]{2,0,1:T(2,128)S(1)}, u32[]{:S(2)}, u32[]{:S(2)}) %collective-permute-start.6) | collective-permute-done | bytes 2080 | tf_op jit(solution)/shard_map/ppermute | solution.py:212
  23.2 0.0 copy-start.6
  23.3 0.0 collective-permute-done.7.other_ref
  23.3 2.4 %collective-permute-start.8 = (f32[4,1,128]{2,0,1:T(4,128)S(1)}, f32[4,1,128]{2,0,1:T(4,128)S(1)}, u32[]{:S(2)}, u32[]{:S(2)}) collective-permute-start(f32[4,1,128]{2,0,1:T(4,128)S(1)} %fusion.1), channel_id=1, source_target_pairs={{0,18},{2,16},{4,22},{6,20},{8,26},{10,24},{12,30},{14,28},{16,2},... | collective-permute-start | bytes 6152 | tf_op jit(solution)/shard_map/ppermute | solution.py:212
  25.7 0.0 copy-done.6
  25.7 0.0 copy-done.7
  25.7 1.1 %shard_map.109 = f32[1,4]{1,0:T(1,128)} custom-call(bf16[128,128]{1,0:T(8,128)(2,1)S(1)} %bitcast.19, bf16[4,192,128]{2,1,0:T(8,128)(2,1)S(1)} %shard_map.104.own_ref, bf16[4,192,128]{2,1,0:T(8,128)(2,1)S(1)} %collective-permute-done.7.other_ref), custom_call_target="tpu_custom_call" | custom-call | flops 50331648 | bytes 393216 | tf_op jit(solution)/shard_map/pallas_call | solution.py:141
  26.8 0.0 copy-start.3
  26.8 0.7 %copy-done.3 = f32[1,4,32]{2,1,0:T(4,128)S(1)} copy-done((f32[1,4,32]{2,1,0:T(4,128)S(1)}, f32[1,4,32]{2,1,0:T(4,128)}, u32[]{:S(2)}) %copy-start.3) | copy-done | bytes 536
  27.5 0.2 shard_map.110
  27.7 0.0 collective-permute-done.8
  27.8 0.9 %shard_map.111 = (f32[1,4,32]{2,1,0:T(4,128)}, f32[1,4]{1,0:T(1,128)}) custom-call(f32[8,128]{1,0:T(8,128)S(1)} %pad_maximum_fusion.1.returned_ref, f32[2,128]{1,0:T(2,128)S(1)} %get-tuple-element.44.teach_ref, s32[2,128]{1,0:T(2,128)S(1)} %get-tuple-element.45.index_ref), custom_call_target="tpu_custom_call" | custom-call | tf_op jit(solution)/shard_map/pallas_call | solution.py:199
  (11 shorter events, 0.1 us)
Async XLA Ops:
  0.6 3.6 %copy-start.4 = (s32[1,16]{1,0:T(1,128)S(1)}, s32[1,16]{1,0:T(1,128)}, u32[]{:S(2)}) copy-start(s32[1,16]{1,0:T(1,128)} %kept_ref.2) | copy-start | bytes 196
  0.6 6.0 %collective-permute-start = (bf16[1,128,128]{2,1,0:T(8,128)(2,1)}, bf16[1,128,128]{2,1,0:T(8,128)(2,1)S(1)}, u32[]{:S(2)}, u32[]{:S(2)}) collective-permute-start(bf16[1,128,128]{2,1,0:T(8,128)(2,1)} %bitcast.16), channel_id=1, source_target_pairs={{0,18},{2,16},{4,22},{6,20},{8,26},{10,24},{12,30},{14,28},{16,2},... | collective-permute-start | bytes 98312 | tf_op jit(solution)/shard_map/ppermute | solution.py:212
  4.2 1.1 %copy-start = (bf16[1,16,192,128]{3,2,1,0:T(8,128)(2,1)S(1)}, bf16[1,16,192,128]{3,2,1,0:T(8,128)(2,1)}, u32[]{:S(2)}) copy-start(bf16[1,16,192,128]{3,2,1,0:T(8,128)(2,1)} %param.9) | copy-start | bytes 2359300
  5.3 2.1 %copy-start.1 = (bf16[1,4,32,128]{3,2,1,0:T(8,128)(2,1)S(1)}, bf16[1,4,32,128]{3,2,1,0:T(8,128)(2,1)}, u32[]{:S(2)}) copy-start(bf16[1,4,32,128]{3,2,1,0:T(8,128)(2,1)} %param.8) | copy-start | bytes 98308
  5.3 5.0 %copy-start.2 = (bf16[1,4,192,128]{3,2,1,0:T(8,128)(2,1)S(1)}, bf16[1,4,192,128]{3,2,1,0:T(8,128)(2,1)}, u32[]{:S(2)}) copy-start(bf16[1,4,192,128]{3,2,1,0:T(8,128)(2,1)} %param.11) | copy-start | bytes 589828
  6.6 8.0 %collective-permute-start.4 = (bf16[16,192,128]{2,1,0:T(8,128)(2,1)S(1)}, bf16[16,192,128]{2,1,0:T(8,128)(2,1)S(1)}, u32[]{:S(2)}, u32[]{:S(2)}) collective-permute-start(bf16[16,192,128]{2,1,0:T(8,128)(2,1)S(1)} %shard_map.103.refs_1_.refs_2_), channel_id=1, source_target_pairs={{0,2},{2,0},{4,6},{6,4},{8,10},{10,8},{12,14},{14,12},{16,18},{18,... | collective-permute-start | bytes 2359304 | tf_op jit(solution)/shard_map/ppermute | solution.py:212
  7.4 2.9 %copy-start.5 = (s32[1,4]{1,0:T(1,128)S(1)}, s32[1,4]{1,0:T(1,128)}, u32[]{:S(2)}) copy-start(s32[1,4]{1,0:T(1,128)} %kept_ref.3) | copy-start | bytes 52
  7.4 4.2 %collective-permute-start.1 = (bf16[2,128,128]{2,1,0:T(8,128)(2,1)S(1)}, bf16[2,128,128]{2,1,0:T(8,128)(2,1)S(1)}, u32[]{:S(2)}, u32[]{:S(2)}) collective-permute-start(bf16[2,128,128]{2,1,0:T(8,128)(2,1)S(1)} %pad_maximum_fusion), channel_id=1, source_target_pairs={{0,10},{2,8},{4,14},{6,12},{8,2},{10,0},{12,6},{14,4},{16,26},{18,... | collective-permute-start | bytes 196616 | tf_op jit(solution)/shard_map/ppermute | solution.py:212
  8.7 5.9 %collective-permute-start.3 = (bf16[2,128,128]{2,1,0:T(8,128)(2,1)S(1)}, bf16[2,128,128]{2,1,0:T(8,128)(2,1)S(1)}, u32[]{:S(2)}, u32[]{:S(2)}) collective-permute-start(bf16[2,128,128]{2,1,0:T(8,128)(2,1)S(1)} %pad_maximum_fusion), channel_id=1, source_target_pairs={{0,6},{2,4},{4,2},{6,0},{8,14},{10,12},{12,10},{14,8},{16,22},{18,... | collective-permute-start | bytes 196616 | tf_op jit(solution)/shard_map/ppermute | solution.py:212
  11.7 4.2 %collective-permute-start.2 = (bf16[2,128,128]{2,1,0:T(8,128)(2,1)S(1)}, bf16[2,128,128]{2,1,0:T(8,128)(2,1)S(1)}, u32[]{:S(2)}, u32[]{:S(2)}) collective-permute-start(bf16[2,128,128]{2,1,0:T(8,128)(2,1)S(1)} %collective-permute-done.1.refs_0_), channel_id=1, source_target_pairs={{0,6},{2,4},{4,2},{6,0},{8,14},{10,12},{12,10},{14,8},{16,22},{18,... | collective-permute-start | bytes 196616 | tf_op jit(solution)/shard_map/ppermute | solution.py:212
  13.1 10.2 %collective-permute-start.7 = (bf16[4,192,128]{2,1,0:T(8,128)(2,1)S(1)}, bf16[4,192,128]{2,1,0:T(8,128)(2,1)S(1)}, u32[]{:S(2)}, u32[]{:S(2)}) collective-permute-start(bf16[4,192,128]{2,1,0:T(8,128)(2,1)S(1)} %shard_map.104.own_ref), channel_id=1, source_target_pairs={{0,1},{1,0},{2,3},{3,2},{4,5},{5,4},{6,7},{7,6},{8,9},{9,8},{10,11... | collective-permute-start | bytes 589832 | tf_op jit(solution)/shard_map/ppermute | solution.py:246
  17.1 3.1 %collective-permute-start.5 = (f32[1,4,128]{2,0,1:T(1,128)S(1)}, f32[1,4,128]{2,0,1:T(1,128)S(1)}, u32[]{:S(2)}, u32[]{:S(2)}) collective-permute-start(f32[1,4,128]{2,0,1:T(1,128)S(1)} %bitcast.23), channel_id=1, source_target_pairs={{0,6},{2,4},{4,2},{6,0},{8,14},{10,12},{12,10},{14,8},{16,22},{18,... | collective-permute-start | bytes 6152 | tf_op jit(solution)/shard_map/ppermute | solution.py:212
  20.2 3.1 %collective-permute-start.6 = (f32[2,2,128]{2,0,1:T(2,128)S(1)}, f32[2,2,128]{2,0,1:T(2,128)S(1)}, u32[]{:S(2)}, u32[]{:S(2)}) collective-permute-start(f32[2,2,128]{2,0,1:T(2,128)S(1)} %pad_maximum_fusion.4), channel_id=1, source_target_pairs={{0,10},{2,8},{4,14},{6,12},{8,2},{10,0},{12,6},{14,4},{16,26},{18,... | collective-permute-start | bytes 6152 | tf_op jit(solution)/shard_map/ppermute | solution.py:212
  21.5 4.2 %copy-start.7 = (s32[1,4,32]{2,1,0:T(4,128)S(1)}, s32[1,4,32]{2,1,0:T(4,128)}, u32[]{:S(2)}) copy-start(s32[1,4,32]{2,1,0:T(4,128)} %param.14) | copy-start | bytes 1540
  23.2 2.4 %copy-start.6 = (s32[1,4,32,1]{2,3,1,0:T(1,128)S(1)}, s32[1,4,32,1]{2,3,1,0:T(1,128)}, u32[]{:S(2)}) copy-start(s32[1,4,32,1]{2,3,1,0:T(1,128)} %param.13) | copy-start | bytes 1540
  23.3 4.5 %collective-permute-start.8 = (f32[4,1,128]{2,0,1:T(4,128)S(1)}, f32[4,1,128]{2,0,1:T(4,128)S(1)}, u32[]{:S(2)}, u32[]{:S(2)}) collective-permute-start(f32[4,1,128]{2,0,1:T(4,128)S(1)} %fusion.1), channel_id=1, source_target_pairs={{0,18},{2,16},{4,22},{6,20},{8,26},{10,24},{12,30},{14,28},{16,2},... | collective-permute-start | bytes 6152 | tf_op jit(solution)/shard_map/ppermute | solution.py:212
  26.8 0.7 %copy-start.3 = (f32[1,4,32]{2,1,0:T(4,128)S(1)}, f32[1,4,32]{2,1,0:T(4,128)}, u32[]{:S(2)}) copy-start(f32[1,4,32]{2,1,0:T(4,128)} %teacher_ref.1) | copy-start | bytes 1540

commit v4 on v3

--- a/solution.py
+++ b/solution.py
@@ -24,10 +24,11 @@
     return unit(jnp.where(place < kept, wide, wide[0:1]))
 
 
-def group_sum(values, width):
+def group_sum(values, width, packed=False):
     lanes = values.shape[1]
     row = lax.broadcasted_iota(jnp.int32, (lanes, lanes), 0) // width
-    column = lax.broadcasted_iota(jnp.int32, (lanes, lanes), 1) // width
+    column = lax.broadcasted_iota(jnp.int32, (lanes, lanes), 1)
+    column = column if packed else column // width
     same = (row == column).astype(jnp.bfloat16)
     high = values.astype(jnp.bfloat16)
     rest = values - high.astype(jnp.float32)
@@ -63,6 +64,39 @@
         compiler_params=pltpu.CompilerParams(vmem_limit_bytes=LIMIT),
         cost_estimate=pl.CostEstimate(flops=16 * rows.size, bytes_accessed=4 * rows.size, transcendentals=0),
     )(kept, rows)
+
+
+def flat_lanes(rows, pad_ref, lanes):
+    queries, width = rows.shape
+    pad_ref[:queries, :width] = rows
+    place = lax.broadcasted_iota(jnp.int32, (8, lanes), 1)
+    spread = jnp.take_along_axis(pad_ref[...], place % width, axis=1)
+    row = lax.broadcasted_iota(jnp.int32, (8, lanes), 0)
+    return jnp.sum(jnp.where(row == place // width, spread, 0), axis=0, keepdims=True)
+
+
+def prepare_docs_kernel(width, kept_ref, rows_ref, teacher_ref, out_ref, teach_ref, pad_ref):
+    prepare_kernel(kept_ref, rows_ref, out_ref)
+    teacher = flat_lanes(teacher_ref[0], pad_ref, teach_ref.shape[1])
+    log_teacher = teacher - jnp.log(group_sum(jnp.exp(teacher), width))
+    share = jnp.exp(log_teacher)
+    teach_ref[0:1, :] = share
+    teach_ref[1:3, :] = group_sum(jnp.concatenate([share * log_teacher, share], axis=0), width, packed=True)
+
+
+def prepare_docs(rows, kept, teacher, lanes):
+    return pl.pallas_call(
+        functools.partial(prepare_docs_kernel, teacher.shape[2]),
+        out_shape=(
+            jax.ShapeDtypeStruct(rows.shape, rows.dtype),
+            jax.ShapeDtypeStruct((3, lanes), jnp.float32),
+        ),
+        in_specs=[SMEM, VMEM, VMEM],
+        out_specs=(VMEM, VMEM),
+        scratch_shapes=[pltpu.VMEM((8, lanes), jnp.float32)],
+        compiler_params=pltpu.CompilerParams(vmem_limit_bytes=LIMIT),
+        cost_estimate=pl.CostEstimate(flops=16 * rows.size, bytes_accessed=4 * rows.size, transcendentals=0),
+    )(kept, rows, teacher)
 
 
 def score_kernel(qlen, count, *refs):
@@ -108,16 +142,9 @@
     )(*query_list, near, far)
 
 
-def flat_lanes(rows, pad_ref, lanes):
-    queries, width = rows.shape
-    pad_ref[:queries, :width] = rows
-    place = lax.broadcasted_iota(jnp.int32, (8, lanes), 1)
-    spread = jnp.take_along_axis(pad_ref[...], place % width, axis=1)
-    row = lax.broadcasted_iota(jnp.int32, (8, lanes), 0)
-    return jnp.sum(jnp.where(row == place // width, spread, 0), axis=0, keepdims=True)
-
-
-def contrast_kernel(qlen, query_ref, own_ref, other_ref, contrast_ref, best_ref):
+def contrast_kernel(
+    qlen, query_ref, own_ref, other_ref, where_ref, lane_ref, contrast_ref, index_ref, best_ref, ints_ref
+):
     queries = unit(query_ref[...])
     lanes = queries.shape[0]
     docs = own_ref.shape[0]
@@ -125,6 +152,10 @@
     for i in range(total):
         tokens = own_ref[i] if i < docs else other_ref[i - docs]
         best_ref[i : i + 1, :] = best_match(tokens, queries)
+    count, width = where_ref.shape
+    index_ref[0:1, :] = flat_lanes(where_ref[...], ints_ref.at[0], lanes)
+    lane = flat_lanes(lane_ref[...], ints_ref.at[1], lanes)
+    index_ref[1:2, :] = lane + lax.broadcasted_iota(jnp.int32, (1, lanes), 1) // width * (lanes // count)
     logits = group_sum(best_ref[...], qlen)
     row = lax.broadcasted_iota(jnp.int32, (total, lanes), 0)
     query = lax.broadcasted_iota(jnp.int32, (total, lanes), 1) // qlen
@@ -135,46 +166,23 @@
     contrast_ref[...] = spread[0:1, : lanes // qlen]
 
 
-def contrast_loss(query_rows, own, other, qlen):
+def contrast_loss(query_rows, own, other, whose, lane, qlen):
     lanes = query_rows.shape[0]
     total = own.shape[0] + other.shape[0]
     return pl.pallas_call(
         functools.partial(contrast_kernel, qlen),
-        out_shape=jax.ShapeDtypeStruct((1, lanes // qlen), jnp.float32),
-        in_specs=[VMEM] * 3,
-        out_specs=VMEM,
-        scratch_shapes=[pltpu.VMEM((total, lanes), jnp.float32)],
+        out_shape=(
+            jax.ShapeDtypeStruct((1, lanes // qlen), jnp.float32),
+            jax.ShapeDtypeStruct((2, lanes), jnp.int32),
+        ),
+        in_specs=[VMEM] * 5,
+        out_specs=(VMEM, VMEM),
+        scratch_shapes=[pltpu.VMEM((total, lanes), jnp.float32), pltpu.VMEM((2, 8, lanes), jnp.int32)],
         compiler_params=pltpu.CompilerParams(vmem_limit_bytes=LIMIT),
         cost_estimate=pl.CostEstimate(
             flops=2 * lanes * own.shape[2] * total * own.shape[1], bytes_accessed=4 * own.size, transcendentals=0
         ),
-    )(query_rows, own, other)
-
-
-def teach_kernel(where_ref, lane_ref, teacher_ref, teach_ref, index_ref, pad_ref, ints_ref):
-    count, width = teacher_ref.shape[1:]
-    lanes = teach_ref.shape[1]
-    teacher = flat_lanes(teacher_ref[0], pad_ref, lanes)
-    log_teacher = teacher - jnp.log(group_sum(jnp.exp(teacher), width))
-    teach_ref[0:1, :] = log_teacher
-    teach_ref[1:2, :] = jnp.exp(log_teacher)
-    index_ref[0:1, :] = flat_lanes(where_ref[...], ints_ref, lanes)
-    lane = flat_lanes(lane_ref[...], ints_ref, lanes)
-    index_ref[1:2, :] = lane + lax.broadcasted_iota(jnp.int32, (1, lanes), 1) // width * (lanes // count)
-
-
-def teach_rows(whose, lane, teacher, lanes):
-    return pl.pallas_call(
-        teach_kernel,
-        out_shape=(
-            jax.ShapeDtypeStruct((2, lanes), jnp.float32),
-            jax.ShapeDtypeStruct((2, lanes), jnp.int32),
-        ),
-        in_specs=[VMEM] * 3,
-        out_specs=(VMEM, VMEM),
-        scratch_shapes=[pltpu.VMEM((8, lanes), jnp.float32), pltpu.VMEM((8, lanes), jnp.int32)],
-        compiler_params=pltpu.CompilerParams(vmem_limit_bytes=LIMIT),
-    )(whose, lane, teacher)
+    )(query_rows, own, other, whose, lane)
 
 
 def distill_kernel(returned_ref, teach_ref, index_ref, student_ref, distill_ref):
@@ -189,10 +197,10 @@
     place = lax.broadcasted_iota(jnp.int32, (8, lanes), 1)
     spread = jnp.take_along_axis(jnp.broadcast_to(student, (8, lanes)), (first * width + place) % lanes, axis=1)
     student_ref[0] = spread[:queries, :width]
-    log_student = student - jnp.log(group_sum(jnp.exp(student), width))
-    loss = group_sum(teach_ref[1:2, :] * (teach_ref[0:1, :] - log_student), width)
-    spread = jnp.take_along_axis(jnp.broadcast_to(loss, (8, lanes)), (place * width) % lanes, axis=1)
-    distill_ref[...] = spread[0:1, :queries]
+    share = teach_ref[0:1, :]
+    sums = group_sum(jnp.concatenate([jnp.exp(student), share * student], axis=0), width, packed=True)
+    loss = teach_ref[1:2, :] - sums[1:2] + teach_ref[2:3, :] * jnp.log(sums[0:1])
+    distill_ref[...] = loss[:, :queries]
 
 
 def distill_loss(returned, teach, index, shape):
@@ -230,7 +238,7 @@
     got = swap(own_rows, "dp", bits[-1])
     near, positives, got = tie((near, positives, got))
     far = swap(near, "dp", 1)
-    own_docs = prepare(positives[0], positive_lengths)
+    own_docs, teach = prepare_docs(positives[0], positive_lengths, teacher, query_count * qlen)
     parts = [got]
     held = jnp.concatenate([own_rows, got], axis=0)
     crossed = []
@@ -238,7 +246,7 @@
         got = swap(held, "dp", bit)
         crossed.append(swap(held if n == 0 else parts[-1], "dp", last))
         if n == 0:
-            got, own_docs = tie((got, own_docs))
+            got, own_docs, teach = tie((got, own_docs, teach))
         parts.append(got)
         held = jnp.concatenate([held, got], axis=0)
     other_docs = jnp.concatenate(
@@ -271,11 +279,10 @@
             apart = owners[0, :, :, 0] ^ me
             odd = functools.reduce(lambda x, m: x ^ (apart >> m), range(1, peers.bit_length() - 1), apart) & 1
             lane = odd * pass_count + local_ids[0]
-            teach, index = teach_rows(apart >> 1, lane, teacher, query_count * qlen)
-            contrast = contrast_loss(own_rows[0], own_docs, other_docs, qlen)
+            contrast, index = contrast_loss(own_rows[0], own_docs, other_docs, apart >> 1, lane, qlen)
         arrived = swap(leaving, "dp", bit)
         if n == len(bits) - 2:
-            arrived, contrast, teach = tie((arrived, contrast, teach))
+            arrived, contrast, index = tie((arrived, contrast, index))
         back = jnp.concatenate([back[:, :half], arrived], axis=0)
     returned = jnp.concatenate([mine[:1], back[:, 0]], axis=0)
     student, distill = distill_loss(returned, teach, index, teacher.shape)

time: 28.9 us -> 28.2 us (0.976)
  local copies, waits for them, and re-layouts: 1.84 us -> 1.17 us
    pallas_call x2 -> x1, Pallas kernels: 2.02 us -> 1.29 us  [prepare(): pl.pallas_call(prepare_kernel, out_shape=jax.ShapeDtypeStruct(rows.shape,...]
    pallas_call x2, Pallas kernels: 1.35 us -> 2.03 us  [the longest x1 1.14 us: contrast_loss(): pl.pallas_call(functools.partial(contrast_kernel, qlen), out_shape=(jax.S...]
    unnamed x16, local copies, waits for them, and re-layouts: 1.84 us -> 1.16 us
  transfers between devices with their start and end apart: 9 -> 9, of which waited for: 3 -> 4; matrix products, arithmetic and copies ran while one was open for 0% -> 0% of each run, Pallas kernels for 29% -> 29%
where the time goes in v4:
time: 28.2 us; the launch traced here: 28 us
  starting transfers between devices  15.4 us (55%)
  Pallas kernels  8.91 us (32%)
  waiting for transfers between devices  1.74 us (6%)
  local copies, waits for them, and re-layouts  1.17 us (4%)
  between operations  0.72 us (3%)
    ppermute x8, starting transfers between devices, swap(): lax.ppermute(values, axis, [(i, i ^ bit) for i in range(lax.axis_size(axi...  13.9 us
    pallas_call x4, Pallas kernels, score(): pl.pallas_call(functools.partial(score_kernel, qlen, len(query_list)), ou...  4.85 us
    ppermute x8, waiting for transfers between devices, swap(): lax.ppermute(values, axis, [(i, i ^ bit) for i in range(lax.axis_size(axi...  1.74 us
    ppermute x1, starting transfers between devices, per_device(): lax.ppermute(own_docs, 'blk', [(i, (i + k) % groups) for i in range(group...  1.49 us
    pallas_call x1, Pallas kernels, prepare(): pl.pallas_call(prepare_kernel, out_shape=jax.ShapeDtypeStruct(rows.shape,...  1.29 us
    unnamed x16, local copies, waits for them, and re-layouts  1.16 us
    pallas_call x1, Pallas kernels, contrast_loss(): pl.pallas_call(functools.partial(contrast_kernel, qlen), out_shape=(jax.S...  1.14 us
    pallas_call x1, Pallas kernels, prepare_docs(): pl.pallas_call(functools.partial(prepare_docs_kernel, teacher.shape[2]),...  0.89 us
  transfers between devices with their start and end apart: 9, of which 4 were waited for; matrix products, arithmetic and copies ran while one was open for 0% of the time, Pallas kernels for 29%

profile of v4, /device:TPU:0, one launch (start us, length us, event | category | flops | bytes accessed | tf_op | source)
XLA Modules:
  0.0 28.0 jit_solution(1227610420599375190)
XLA Ops:
  0.6 0.0 copy-start.4
  0.6 3.5 %collective-permute-start = (bf16[1,128,128]{2,1,0:T(8,128)(2,1)}, bf16[1,128,128]{2,1,0:T(8,128)(2,1)S(1)}, u32[]{:S(2)}, u32[]{:S(2)}) collective-permute-start(bf16[1,128,128]{2,1,0:T(8,128)(2,1)} %bitcast.16), channel_id=1, source_target_pairs={{0,18},{2,16},{4,22},{6,20},{8,26},{10,24},{12,30},{14,28},{16,2},... | collective-permute-start | bytes 98312 | tf_op jit(solution)/shard_map/ppermute | solution.py:220
  4.2 0.0 copy-done.4
  4.2 0.0 copy-start
  4.2 1.1 %copy-done = bf16[1,16,192,128]{3,2,1,0:T(8,128)(2,1)S(1)} copy-done((bf16[1,16,192,128]{3,2,1,0:T(8,128)(2,1)S(1)}, bf16[1,16,192,128]{3,2,1,0:T(8,128)(2,1)}, u32[]{:S(2)}) %copy-start) | copy-done | bytes 786456
  5.3 0.0 copy-start.1
  5.3 0.0 copy-start.2
  5.3 1.3 %shard_map.103.refs_1_.refs_2_ = bf16[16,192,128]{2,1,0:T(8,128)(2,1)S(1)} custom-call(s32[1,16]{1,0:T(1,128)S(1)} %copy-done.4, bf16[16,192,128]{2,1,0:T(8,128)(2,1)S(1)} %bitcast.15), custom_call_target="tpu_custom_call" | custom-call | flops 6291456 | bytes 1572864 | tf_op jit(solution)/shard_map/pallas_call | solution.py:59
  6.6 0.0 collective-permute-done.refs_1_
  6.6 0.7 %collective-permute-start.4 = (bf16[16,192,128]{2,1,0:T(8,128)(2,1)S(1)}, bf16[16,192,128]{2,1,0:T(8,128)(2,1)S(1)}, u32[]{:S(2)}, u32[]{:S(2)}) collective-permute-start(bf16[16,192,128]{2,1,0:T(8,128)(2,1)S(1)} %shard_map.103.refs_1_.refs_2_), channel_id=1, source_target_pairs={{0,2},{2,0},{4,6},{6,4},{8,10},{10,8},{12,14},{14,12},{16,18},{18,... | collective-permute-start | bytes 2359304 | tf_op jit(solution)/shard_map/ppermute | solution.py:220
  7.4 0.0 copy-done.1
  7.4 0.0 copy-start.3
  7.4 0.0 copy-start.5
  7.4 1.3 %collective-permute-start.1 = (bf16[2,128,128]{2,1,0:T(8,128)(2,1)S(1)}, bf16[2,128,128]{2,1,0:T(8,128)(2,1)S(1)}, u32[]{:S(2)}, u32[]{:S(2)}) collective-permute-start(bf16[2,128,128]{2,1,0:T(8,128)(2,1)S(1)} %pad_maximum_fusion), channel_id=1, source_target_pairs={{0,10},{2,8},{4,14},{6,12},{8,2},{10,0},{12,6},{14,4},{16,26},{18,... | collective-permute-start | bytes 196616 | tf_op jit(solution)/shard_map/ppermute | solution.py:220
  8.7 1.6 %collective-permute-start.3 = (bf16[2,128,128]{2,1,0:T(8,128)(2,1)S(1)}, bf16[2,128,128]{2,1,0:T(8,128)(2,1)S(1)}, u32[]{:S(2)}, u32[]{:S(2)}) collective-permute-start(bf16[2,128,128]{2,1,0:T(8,128)(2,1)S(1)} %pad_maximum_fusion), channel_id=1, source_target_pairs={{0,6},{2,4},{4,2},{6,0},{8,14},{10,12},{12,10},{14,8},{16,22},{18,... | collective-permute-start | bytes 196616 | tf_op jit(solution)/shard_map/ppermute | solution.py:220
  10.3 0.0 copy-done.2
  10.3 0.0 copy-done.3
  10.3 0.0 copy-done.5
  10.3 0.9 %shard_map.104 = (bf16[4,192,128]{2,1,0:T(8,128)(2,1)S(1)}, f32[3,128]{1,0:T(4,128)S(1)}) custom-call(s32[1,4]{1,0:T(1,128)S(1)} %copy-done.5, bf16[4,192,128]{2,1,0:T(8,128)(2,1)S(1)} %bitcast.20, f32[1,4,32]{2,1,0:T(4,128)S(1)} %copy-done.3), custom_call_target="tpu_custom_call" | custom-call | flops 1572864 | bytes 393216 | tf_op jit(solution)/shard_map/pallas_call | solution.py:88
  11.2 0.5 %collective-permute-done.1.refs_0_ = bf16[2,128,128]{2,1,0:T(8,128)(2,1)S(1)} collective-permute-done((bf16[2,128,128]{2,1,0:T(8,128)(2,1)S(1)}, bf16[2,128,128]{2,1,0:T(8,128)(2,1)S(1)}, u32[]{:S(2)}, u32[]{:S(2)}) %collective-permute-start.1) | collective-permute-done | bytes 65568 | tf_op jit(solution)/shard_map/ppermute | solution.py:220
  11.6 1.5 %collective-permute-start.2 = (bf16[2,128,128]{2,1,0:T(8,128)(2,1)S(1)}, bf16[2,128,128]{2,1,0:T(8,128)(2,1)S(1)}, u32[]{:S(2)}, u32[]{:S(2)}) collective-permute-start(bf16[2,128,128]{2,1,0:T(8,128)(2,1)S(1)} %collective-permute-done.1.refs_0_), channel_id=1, source_target_pairs={{0,6},{2,4},{4,2},{6,0},{8,14},{10,12},{12,10},{14,8},{16,22},{18,... | collective-permute-start | bytes 196616 | tf_op jit(solution)/shard_map/ppermute | solution.py:220
  13.1 1.5 %collective-permute-start.7 = (bf16[4,192,128]{2,1,0:T(8,128)(2,1)S(1)}, bf16[4,192,128]{2,1,0:T(8,128)(2,1)S(1)}, u32[]{:S(2)}, u32[]{:S(2)}) collective-permute-start(bf16[4,192,128]{2,1,0:T(8,128)(2,1)S(1)} %get-tuple-element.43.own_ref), channel_id=1, source_target_pairs={{0,1},{1,0},{2,3},{3,2},{4,5},{5,4},{6,7},{7,6},{8,9},{9,8},{10,11... | collective-permute-start | bytes 589832 | tf_op jit(solution)/shard_map/ppermute | solution.py:254
  14.6 0.0 collective-permute-done.3.refs_0_
  14.6 0.0 collective-permute-done.4.refs_2_.refs_3_
  14.6 1.2 %shard_map.105 = f32[2,128]{1,0:T(2,128)S(1)} custom-call(bf16[2,128,128]{2,1,0:T(8,128)(2,1)S(1)} %collective-permute-done.3.refs_0_, bf16[16,192,128]{2,1,0:T(8,128)(2,1)S(1)} %shard_map.103.refs_1_.refs_2_, bf16[16,192,128]{2,1,0:T(8,128)(2,1)S(1)} %collective-permute-done.4.refs_2_.refs_3_), custom_call_target="tpu_custom_call" | custom-call | flops 402653184 | bytes 1572864 | tf_op jit(solution)/shard_map/pallas_call | solution.py:130
  15.8 0.0 collective-permute-done.2.refs_0_
  15.8 1.2 %shard_map.106 = f32[2,128]{1,0:T(2,128)S(1)} custom-call(bf16[2,128,128]{2,1,0:T(8,128)(2,1)S(1)} %collective-permute-done.2.refs_0_, bf16[16,192,128]{2,1,0:T(8,128)(2,1)S(1)} %shard_map.103.refs_1_.refs_2_, bf16[16,192,128]{2,1,0:T(8,128)(2,1)S(1)} %collective-permute-done.4.refs_2_.refs_3_), custom_call_target="tpu_custom_call" | custom-call | flops 402653184 | bytes 1572864 | tf_op jit(solution)/shard_map/pallas_call | solution.py:130
  17.1 1.5 %collective-permute-start.5 = (f32[1,4,128]{2,0,1:T(1,128)S(1)}, f32[1,4,128]{2,0,1:T(1,128)S(1)}, u32[]{:S(2)}, u32[]{:S(2)}) collective-permute-start(f32[1,4,128]{2,0,1:T(1,128)S(1)} %bitcast.23), channel_id=1, source_target_pairs={{0,6},{2,4},{4,2},{6,0},{8,14},{10,12},{12,10},{14,8},{16,22},{18,... | collective-permute-start | bytes 6152 | tf_op jit(solution)/shard_map/ppermute | solution.py:220
  18.6 1.2 %shard_map.107 = f32[2,128]{1,0:T(2,128)S(1)} custom-call(bf16[2,128,128]{2,1,0:T(8,128)(2,1)S(1)} %collective-permute-done.1.refs_0_, bf16[16,192,128]{2,1,0:T(8,128)(2,1)S(1)} %shard_map.103.refs_1_.refs_2_, bf16[16,192,128]{2,1,0:T(8,128)(2,1)S(1)} %collective-permute-done.4.refs_2_.refs_3_), custom_call_target="tpu_custom_call" | custom-call | flops 402653184 | bytes 1572864 | tf_op jit(solution)/shard_map/pallas_call | solution.py:130
  19.8 0.4 %collective-permute-done.5 = f32[1,4,128]{2,0,1:T(1,128)S(1)} collective-permute-done((f32[1,4,128]{2,0,1:T(1,128)S(1)}, f32[1,4,128]{2,0,1:T(1,128)S(1)}, u32[]{:S(2)}, u32[]{:S(2)}) %collective-permute-start.5) | collective-permute-done | bytes 2080 | tf_op jit(solution)/shard_map/ppermute | solution.py:220
  20.2 1.3 %collective-permute-start.6 = (f32[2,2,128]{2,0,1:T(2,128)S(1)}, f32[2,2,128]{2,0,1:T(2,128)S(1)}, u32[]{:S(2)}, u32[]{:S(2)}) collective-permute-start(f32[2,2,128]{2,0,1:T(2,128)S(1)} %pad_maximum_fusion.4), channel_id=1, source_target_pairs={{0,10},{2,8},{4,14},{6,12},{8,2},{10,0},{12,6},{14,4},{16,26},{18,... | collective-permute-start | bytes 6152 | tf_op jit(solution)/shard_map/ppermute | solution.py:220
  21.5 0.0 copy-start.7
  21.5 1.2 %shard_map.108 = f32[2,128]{1,0:T(2,128)S(1)} custom-call(bf16[1,128,128]{2,1,0:T(8,128)(2,1)S(1)} %bitcast.18, bf16[1,128,128]{2,1,0:T(8,128)(2,1)S(1)} %collective-permute-done.refs_1_, bf16[16,192,128]{2,1,0:T(8,128)(2,1)S(1)} %shard_map.103.refs_1_.refs_2_, bf16[16,192,128]{2,1,0:T(8,128)(2,1)S(1)} %collective-permute-done.4.refs_2_.refs_3_), custom_call_target="tpu_custom_call" | custom-call | flops 402653184 | bytes 1572864 | tf_op jit(solution)/shard_map/pallas_call | solution.py:130
  22.7 0.5 %collective-permute-done.6 = f32[2,2,128]{2,0,1:T(2,128)S(1)} collective-permute-done((f32[2,2,128]{2,0,1:T(2,128)S(1)}, f32[2,2,128]{2,0,1:T(2,128)S(1)}, u32[]{:S(2)}, u32[]{:S(2)}) %collective-permute-start.6) | collective-permute-done | bytes 2080 | tf_op jit(solution)/shard_map/ppermute | solution.py:220
  23.2 0.0 copy-start.6
  23.2 0.0 collective-permute-done.7.other_ref
  23.3 2.4 %collective-permute-start.8 = (f32[4,1,128]{2,0,1:T(4,128)S(1)}, f32[4,1,128]{2,0,1:T(4,128)S(1)}, u32[]{:S(2)}, u32[]{:S(2)}) collective-permute-start(f32[4,1,128]{2,0,1:T(4,128)S(1)} %fusion.1), channel_id=1, source_target_pairs={{0,18},{2,16},{4,22},{6,20},{8,26},{10,24},{12,30},{14,28},{16,2},... | collective-permute-start | bytes 6152 | tf_op jit(solution)/shard_map/ppermute | solution.py:220
  25.7 0.0 copy-done.6
  25.7 0.0 copy-done.7
  25.7 1.1 %shard_map.109 = (f32[1,4]{1,0:T(1,128)}, s32[2,128]{1,0:T(2,128)S(1)}) custom-call(bf16[128,128]{1,0:T(8,128)(2,1)S(1)} %bitcast.19, bf16[4,192,128]{2,1,0:T(8,128)(2,1)S(1)} %get-tuple-element.43.own_ref, bf16[4,192,128]{2,1,0:T(8,128)(2,1)S(1)} %collective-permute-done.7.other_ref, s32[4,32]{1,0:T(4,128)S(1)} %get-tuple-element.56.where_ref, ...), custom_call_target="tpu_custom_call" | custom-call | flops 50331648 | bytes 393216 | tf_op jit(solution)/shard_map/pallas_call | solution.py:172
  26.8 0.4 %collective-permute-done.8 = f32[4,1,128]{2,0,1:T(4,128)S(1)} collective-permute-done((f32[4,1,128]{2,0,1:T(4,128)S(1)}, f32[4,1,128]{2,0,1:T(4,128)S(1)}, u32[]{:S(2)}, u32[]{:S(2)}) %collective-permute-start.8) | collective-permute-done | bytes 2080 | tf_op jit(solution)/shard_map/ppermute | solution.py:220
  27.3 0.7 %shard_map.110 = (f32[1,4,32]{2,1,0:T(4,128)}, f32[1,4]{1,0:T(1,128)}) custom-call(f32[8,128]{1,0:T(8,128)S(1)} %pad_maximum_fusion.1.returned_ref, f32[3,128]{1,0:T(4,128)S(1)} %get-tuple-element.50.teach_ref, s32[2,128]{1,0:T(2,128)S(1)} %get-tuple-element.51.index_ref), custom_call_target="tpu_custom_call" | custom-call | tf_op jit(solution)/shard_map/pallas_call | solution.py:207
  (11 shorter events, 0.1 us)
Async XLA Ops:
  0.6 3.6 %copy-start.4 = (s32[1,16]{1,0:T(1,128)S(1)}, s32[1,16]{1,0:T(1,128)}, u32[]{:S(2)}) copy-start(s32[1,16]{1,0:T(1,128)} %kept_ref.2) | copy-start | bytes 196
  0.6 6.0 %collective-permute-start = (bf16[1,128,128]{2,1,0:T(8,128)(2,1)}, bf16[1,128,128]{2,1,0:T(8,128)(2,1)S(1)}, u32[]{:S(2)}, u32[]{:S(2)}) collective-permute-start(bf16[1,128,128]{2,1,0:T(8,128)(2,1)} %bitcast.16), channel_id=1, source_target_pairs={{0,18},{2,16},{4,22},{6,20},{8,26},{10,24},{12,30},{14,28},{16,2},... | collective-permute-start | bytes 98312 | tf_op jit(solution)/shard_map/ppermute | solution.py:220
  4.2 1.1 %copy-start = (bf16[1,16,192,128]{3,2,1,0:T(8,128)(2,1)S(1)}, bf16[1,16,192,128]{3,2,1,0:T(8,128)(2,1)}, u32[]{:S(2)}) copy-start(bf16[1,16,192,128]{3,2,1,0:T(8,128)(2,1)} %param.9) | copy-start | bytes 2359300
  5.3 2.1 %copy-start.1 = (bf16[1,4,32,128]{3,2,1,0:T(8,128)(2,1)S(1)}, bf16[1,4,32,128]{3,2,1,0:T(8,128)(2,1)}, u32[]{:S(2)}) copy-start(bf16[1,4,32,128]{3,2,1,0:T(8,128)(2,1)} %param.8) | copy-start | bytes 98308
  5.3 5.0 %copy-start.2 = (bf16[1,4,192,128]{3,2,1,0:T(8,128)(2,1)S(1)}, bf16[1,4,192,128]{3,2,1,0:T(8,128)(2,1)}, u32[]{:S(2)}) copy-start(bf16[1,4,192,128]{3,2,1,0:T(8,128)(2,1)} %param.11) | copy-start | bytes 589828
  6.6 8.0 %collective-permute-start.4 = (bf16[16,192,128]{2,1,0:T(8,128)(2,1)S(1)}, bf16[16,192,128]{2,1,0:T(8,128)(2,1)S(1)}, u32[]{:S(2)}, u32[]{:S(2)}) collective-permute-start(bf16[16,192,128]{2,1,0:T(8,128)(2,1)S(1)} %shard_map.103.refs_1_.refs_2_), channel_id=1, source_target_pairs={{0,2},{2,0},{4,6},{6,4},{8,10},{10,8},{12,14},{14,12},{16,18},{18,... | collective-permute-start | bytes 2359304 | tf_op jit(solution)/shard_map/ppermute | solution.py:220
  7.4 2.9 %copy-start.3 = (f32[1,4,32]{2,1,0:T(4,128)S(1)}, f32[1,4,32]{2,1,0:T(4,128)}, u32[]{:S(2)}) copy-start(f32[1,4,32]{2,1,0:T(4,128)} %teacher_ref.1) | copy-start | bytes 1540
  7.4 2.9 %copy-start.5 = (s32[1,4]{1,0:T(1,128)S(1)}, s32[1,4]{1,0:T(1,128)}, u32[]{:S(2)}) copy-start(s32[1,4]{1,0:T(1,128)} %kept_ref.3) | copy-start | bytes 52
  7.4 4.2 %collective-permute-start.1 = (bf16[2,128,128]{2,1,0:T(8,128)(2,1)S(1)}, bf16[2,128,128]{2,1,0:T(8,128)(2,1)S(1)}, u32[]{:S(2)}, u32[]{:S(2)}) collective-permute-start(bf16[2,128,128]{2,1,0:T(8,128)(2,1)S(1)} %pad_maximum_fusion), channel_id=1, source_target_pairs={{0,10},{2,8},{4,14},{6,12},{8,2},{10,0},{12,6},{14,4},{16,26},{18,... | collective-permute-start | bytes 196616 | tf_op jit(solution)/shard_map/ppermute | solution.py:220
  8.7 5.9 %collective-permute-start.3 = (bf16[2,128,128]{2,1,0:T(8,128)(2,1)S(1)}, bf16[2,128,128]{2,1,0:T(8,128)(2,1)S(1)}, u32[]{:S(2)}, u32[]{:S(2)}) collective-permute-start(bf16[2,128,128]{2,1,0:T(8,128)(2,1)S(1)} %pad_maximum_fusion), channel_id=1, source_target_pairs={{0,6},{2,4},{4,2},{6,0},{8,14},{10,12},{12,10},{14,8},{16,22},{18,... | collective-permute-start | bytes 196616 | tf_op jit(solution)/shard_map/ppermute | solution.py:220
  11.6 4.2 %collective-permute-start.2 = (bf16[2,128,128]{2,1,0:T(8,128)(2,1)S(1)}, bf16[2,128,128]{2,1,0:T(8,128)(2,1)S(1)}, u32[]{:S(2)}, u32[]{:S(2)}) collective-permute-start(bf16[2,128,128]{2,1,0:T(8,128)(2,1)S(1)} %collective-permute-done.1.refs_0_), channel_id=1, source_target_pairs={{0,6},{2,4},{4,2},{6,0},{8,14},{10,12},{12,10},{14,8},{16,22},{18,... | collective-permute-start | bytes 196616 | tf_op jit(solution)/shard_map/ppermute | solution.py:220
  13.1 10.1 %collective-permute-start.7 = (bf16[4,192,128]{2,1,0:T(8,128)(2,1)S(1)}, bf16[4,192,128]{2,1,0:T(8,128)(2,1)S(1)}, u32[]{:S(2)}, u32[]{:S(2)}) collective-permute-start(bf16[4,192,128]{2,1,0:T(8,128)(2,1)S(1)} %get-tuple-element.43.own_ref), channel_id=1, source_target_pairs={{0,1},{1,0},{2,3},{3,2},{4,5},{5,4},{6,7},{7,6},{8,9},{9,8},{10,11... | collective-permute-start | bytes 589832 | tf_op jit(solution)/shard_map/ppermute | solution.py:254
  17.1 3.1 %collective-permute-start.5 = (f32[1,4,128]{2,0,1:T(1,128)S(1)}, f32[1,4,128]{2,0,1:T(1,128)S(1)}, u32[]{:S(2)}, u32[]{:S(2)}) collective-permute-start(f32[1,4,128]{2,0,1:T(1,128)S(1)} %bitcast.23), channel_id=1, source_target_pairs={{0,6},{2,4},{4,2},{6,0},{8,14},{10,12},{12,10},{14,8},{16,22},{18,... | collective-permute-start | bytes 6152 | tf_op jit(solution)/shard_map/ppermute | solution.py:220
  20.2 3.1 %collective-permute-start.6 = (f32[2,2,128]{2,0,1:T(2,128)S(1)}, f32[2,2,128]{2,0,1:T(2,128)S(1)}, u32[]{:S(2)}, u32[]{:S(2)}) collective-permute-start(f32[2,2,128]{2,0,1:T(2,128)S(1)} %pad_maximum_fusion.4), channel_id=1, source_target_pairs={{0,10},{2,8},{4,14},{6,12},{8,2},{10,0},{12,6},{14,4},{16,26},{18,... | collective-permute-start | bytes 6152 | tf_op jit(solution)/shard_map/ppermute | solution.py:220
  21.5 4.2 %copy-start.7 = (s32[1,4,32]{2,1,0:T(4,128)S(1)}, s32[1,4,32]{2,1,0:T(4,128)}, u32[]{:S(2)}) copy-start(s32[1,4,32]{2,1,0:T(4,128)} %param.14) | copy-start | bytes 1540
  23.2 2.4 %copy-start.6 = (s32[1,4,32,1]{2,3,1,0:T(1,128)S(1)}, s32[1,4,32,1]{2,3,1,0:T(1,128)}, u32[]{:S(2)}) copy-start(s32[1,4,32,1]{2,3,1,0:T(1,128)} %param.13) | copy-start | bytes 1540
  23.3 4.0 %collective-permute-start.8 = (f32[4,1,128]{2,0,1:T(4,128)S(1)}, f32[4,1,128]{2,0,1:T(4,128)S(1)}, u32[]{:S(2)}, u32[]{:S(2)}) collective-permute-start(f32[4,1,128]{2,0,1:T(4,128)S(1)} %fusion.1), channel_id=1, source_target_pairs={{0,18},{2,16},{4,22},{6,20},{8,26},{10,24},{12,30},{14,28},{16,2},... | collective-permute-start | bytes 6152 | tf_op jit(solution)/shard_map/ppermute | solution.py:220

commit v5 on v4

--- a/solution.py
+++ b/solution.py
@@ -95,7 +95,7 @@
         out_specs=(VMEM, VMEM),
         scratch_shapes=[pltpu.VMEM((8, lanes), jnp.float32)],
         compiler_params=pltpu.CompilerParams(vmem_limit_bytes=LIMIT),
-        cost_estimate=pl.CostEstimate(flops=16 * rows.size, bytes_accessed=4 * rows.size, transcendentals=0),
+        cost_estimate=pl.CostEstimate(flops=160000 * rows.size, bytes_accessed=4 * rows.size, transcendentals=0),
     )(kept, rows, teacher)
 
 
@@ -115,10 +115,11 @@
         for i in range(total):
             tokens = near_ref[i] if i < near else far_ref[i - near]
             best_ref[i : i + 1, :width] = best_match(tokens, joined)
+        both = jnp.concatenate([best_ref[:, s * lanes : (s + 1) * lanes] for s in range(len(block))], axis=0)
+        summed = group_sum(both, qlen)
         for s in range(len(block)):
-            summed = group_sum(best_ref[:, s * lanes : (s + 1) * lanes], qlen)
             out_ref[start + s : start + s + 1, :] = jnp.sum(
-                jnp.where(row == column, summed, 0.0), axis=0, keepdims=True
+                jnp.where(row == column, summed[s * total : (s + 1) * total], 0.0), axis=0, keepdims=True
             )
         start += 2
 
@@ -236,7 +237,7 @@
     last = bits[0]
     near = prepare(passages[0], passage_lengths)
     got = swap(own_rows, "dp", bits[-1])
-    near, positives, got = tie((near, positives, got))
+    positives, got = tie((positives, got))
     far = swap(near, "dp", 1)
     own_docs, teach = prepare_docs(positives[0], positive_lengths, teacher, query_count * qlen)
     parts = [got]
@@ -244,7 +245,10 @@
     crossed = []
     for n, bit in enumerate(reversed(bits[1:-1])):
         got = swap(held, "dp", bit)
-        crossed.append(swap(held if n == 0 else parts[-1], "dp", last))
+        crossing = held if n == 0 else parts[-1]
+        if n == 0:
+            crossing, own_docs = tie((crossing, own_docs))
+        crossed.append(swap(crossing, "dp", last))
         if n == 0:
             got, own_docs, teach = tie((got, own_docs, teach))
         parts.append(got)

time: 28.2 us -> 28.1 us (level)
  transfers between devices with their start and end apart: 9 -> 9, of which waited for: 4 -> 5; matrix products, arithmetic and copies ran while one was open for 0% -> 0% of each run, Pallas kernels for 29% -> 29%
where the time goes in v5:
time: 28.1 us; the launch traced here: 27.9 us
  starting transfers between devices  15.2 us (54%)
  Pallas kernels  8.94 us (32%)
  waiting for transfers between devices  1.75 us (6%)
  local copies, waits for them, and re-layouts  1.17 us (4%)
  between operations  0.74 us (3%)
    ppermute x8, starting transfers between devices, swap(): lax.ppermute(values, axis, [(i, i ^ bit) for i in range(lax.axis_size(axi...  13.7 us
    pallas_call x4, Pallas kernels, score(): pl.pallas_call(functools.partial(score_kernel, qlen, len(query_list)), ou...  4.89 us
    ppermute x8, waiting for transfers between devices, swap(): lax.ppermute(values, axis, [(i, i ^ bit) for i in range(lax.axis_size(axi...  1.74 us
    ppermute x1, starting transfers between devices, per_device(): lax.ppermute(own_docs, 'blk', [(i, (i + k) % groups) for i in range(group...  1.49 us
    pallas_call x1, Pallas kernels, prepare(): pl.pallas_call(prepare_kernel, out_shape=jax.ShapeDtypeStruct(rows.shape,...  1.29 us
    unnamed x16, local copies, waits for them, and re-layouts  1.16 us
    pallas_call x1, Pallas kernels, contrast_loss(): pl.pallas_call(functools.partial(contrast_kernel, qlen), out_shape=(jax.S...  1.13 us
    pallas_call x1, Pallas kernels, prepare_docs(): pl.pallas_call(functools.partial(prepare_docs_kernel, teacher.shape[2]),...  0.89 us
  transfers between devices with their start and end apart: 9, of which 5 were waited for; matrix products, arithmetic and copies ran while one was open for 0% of the time, Pallas kernels for 29%

profile of v5, /device:TPU:0, one launch (start us, length us, event | category | flops | bytes accessed | tf_op | source)
XLA Modules:
  0.0 27.9 jit_solution(17776822767627281181)
XLA Ops:
  0.6 0.0 copy-start.2
  0.6 3.5 %collective-permute-start = (bf16[1,128,128]{2,1,0:T(8,128)(2,1)}, bf16[1,128,128]{2,1,0:T(8,128)(2,1)S(1)}, u32[]{:S(2)}, u32[]{:S(2)}) collective-permute-start(bf16[1,128,128]{2,1,0:T(8,128)(2,1)} %bitcast.16), channel_id=1, source_target_pairs={{0,18},{2,16},{4,22},{6,20},{8,26},{10,24},{12,30},{14,28},{16,2},... | collective-permute-start | bytes 98312 | tf_op jit(solution)/shard_map/ppermute | solution.py:221
  4.2 0.0 copy-done.2
  4.2 0.0 copy-start
  4.2 1.1 %copy-done = bf16[1,16,192,128]{3,2,1,0:T(8,128)(2,1)S(1)} copy-done((bf16[1,16,192,128]{3,2,1,0:T(8,128)(2,1)S(1)}, bf16[1,16,192,128]{3,2,1,0:T(8,128)(2,1)}, u32[]{:S(2)}) %copy-start) | copy-done | bytes 786456
  5.3 0.0 copy-start.1
  5.3 0.0 copy-start.3
  5.3 1.3 %shard_map.104.refs_1_.refs_2_ = bf16[16,192,128]{2,1,0:T(8,128)(2,1)S(1)} custom-call(s32[1,16]{1,0:T(1,128)S(1)} %copy-done.2, bf16[16,192,128]{2,1,0:T(8,128)(2,1)S(1)} %bitcast.15), custom_call_target="tpu_custom_call" | custom-call | flops 6291456 | bytes 1572864 | tf_op jit(solution)/shard_map/pallas_call | solution.py:59
  6.6 0.0 copy-start.4
  6.6 0.7 %collective-permute-start.4 = (bf16[16,192,128]{2,1,0:T(8,128)(2,1)S(1)}, bf16[16,192,128]{2,1,0:T(8,128)(2,1)S(1)}, u32[]{:S(2)}, u32[]{:S(2)}) collective-permute-start(bf16[16,192,128]{2,1,0:T(8,128)(2,1)S(1)} %shard_map.104.refs_1_.refs_2_), channel_id=1, source_target_pairs={{0,2},{2,0},{4,6},{6,4},{8,10},{10,8},{12,14},{14,12},{16,18},{18,... | collective-permute-start | bytes 2359304 | tf_op jit(solution)/shard_map/ppermute | solution.py:221
  7.4 0.0 collective-permute-done.refs_1_
  7.4 0.0 copy-done.1
  7.4 0.0 copy-start.5
  7.4 1.3 %collective-permute-start.1 = (bf16[2,128,128]{2,1,0:T(8,128)(2,1)S(1)}, bf16[2,128,128]{2,1,0:T(8,128)(2,1)S(1)}, u32[]{:S(2)}, u32[]{:S(2)}) collective-permute-start(bf16[2,128,128]{2,1,0:T(8,128)(2,1)S(1)} %pad_maximum_fusion), channel_id=1, source_target_pairs={{0,10},{2,8},{4,14},{6,12},{8,2},{10,0},{12,6},{14,4},{16,26},{18,... | collective-permute-start | bytes 196616 | tf_op jit(solution)/shard_map/ppermute | solution.py:221
  8.7 0.0 copy-done.3
  8.7 0.0 copy-done.4
  8.7 0.0 copy-done.5
  8.7 0.9 %shard_map.103 = (bf16[4,192,128]{2,1,0:T(8,128)(2,1)S(1)}, f32[3,128]{1,0:T(4,128)S(1)}) custom-call(s32[1,4]{1,0:T(1,128)S(1)} %copy-done.5, bf16[4,192,128]{2,1,0:T(8,128)(2,1)S(1)} %bitcast.21, f32[1,4,32]{2,1,0:T(4,128)S(1)} %copy-done.4), custom_call_target="tpu_custom_call" | custom-call | flops 15728640000 | bytes 393216 | tf_op jit(solution)/shard_map/pallas_call | solution.py:88
  9.6 1.6 %collective-permute-start.3 = (bf16[2,128,128]{2,1,0:T(8,128)(2,1)S(1)}, bf16[2,128,128]{2,1,0:T(8,128)(2,1)S(1)}, u32[]{:S(2)}, u32[]{:S(2)}) collective-permute-start(bf16[2,128,128]{2,1,0:T(8,128)(2,1)S(1)} %pad_maximum_fusion), channel_id=1, source_target_pairs={{0,6},{2,4},{4,2},{6,0},{8,14},{10,12},{12,10},{14,8},{16,22},{18,... | collective-permute-start | bytes 196616 | tf_op jit(solution)/shard_map/ppermute | solution.py:221
  11.2 0.5 %collective-permute-done.1.refs_0_ = bf16[2,128,128]{2,1,0:T(8,128)(2,1)S(1)} collective-permute-done((bf16[2,128,128]{2,1,0:T(8,128)(2,1)S(1)}, bf16[2,128,128]{2,1,0:T(8,128)(2,1)S(1)}, u32[]{:S(2)}, u32[]{:S(2)}) %collective-permute-start.1) | collective-permute-done | bytes 65568 | tf_op jit(solution)/shard_map/ppermute | solution.py:221
  11.7 1.2 %collective-permute-start.2 = (bf16[2,128,128]{2,1,0:T(8,128)(2,1)S(1)}, bf16[2,128,128]{2,1,0:T(8,128)(2,1)S(1)}, u32[]{:S(2)}, u32[]{:S(2)}) collective-permute-start(bf16[2,128,128]{2,1,0:T(8,128)(2,1)S(1)} %collective-permute-done.1.refs_0_), channel_id=1, source_target_pairs={{0,6},{2,4},{4,2},{6,0},{8,14},{10,12},{12,10},{14,8},{16,22},{18,... | collective-permute-start | bytes 196616 | tf_op jit(solution)/shard_map/ppermute | solution.py:221
  12.9 1.5 %collective-permute-start.7 = (bf16[4,192,128]{2,1,0:T(8,128)(2,1)S(1)}, bf16[4,192,128]{2,1,0:T(8,128)(2,1)S(1)}, u32[]{:S(2)}, u32[]{:S(2)}) collective-permute-start(bf16[4,192,128]{2,1,0:T(8,128)(2,1)S(1)} %get-tuple-element.45.own_ref), channel_id=1, source_target_pairs={{0,1},{1,0},{2,3},{3,2},{4,5},{5,4},{6,7},{7,6},{8,9},{9,8},{10,11... | collective-permute-start | bytes 589832 | tf_op jit(solution)/shard_map/ppermute | solution.py:258
  14.4 0.0 collective-permute-done.3.refs_0_
  14.4 0.0 collective-permute-done.4.refs_2_.refs_3_
  14.4 1.2 %shard_map.105 = f32[2,128]{1,0:T(2,128)S(1)} custom-call(bf16[2,128,128]{2,1,0:T(8,128)(2,1)S(1)} %collective-permute-done.3.refs_0_, bf16[16,192,128]{2,1,0:T(8,128)(2,1)S(1)} %shard_map.104.refs_1_.refs_2_, bf16[16,192,128]{2,1,0:T(8,128)(2,1)S(1)} %collective-permute-done.4.refs_2_.refs_3_), custom_call_target="tpu_custom_call" | custom-call | flops 402653184 | bytes 1572864 | tf_op jit(solution)/shard_map/pallas_call | solution.py:131
  15.6 0.1 collective-permute-done.2.refs_0_
  15.7 1.2 %shard_map.106 = f32[2,128]{1,0:T(2,128)S(1)} custom-call(bf16[2,128,128]{2,1,0:T(8,128)(2,1)S(1)} %collective-permute-done.2.refs_0_, bf16[16,192,128]{2,1,0:T(8,128)(2,1)S(1)} %shard_map.104.refs_1_.refs_2_, bf16[16,192,128]{2,1,0:T(8,128)(2,1)S(1)} %collective-permute-done.4.refs_2_.refs_3_), custom_call_target="tpu_custom_call" | custom-call | flops 402653184 | bytes 1572864 | tf_op jit(solution)/shard_map/pallas_call | solution.py:131
  17.0 1.6 %collective-permute-start.5 = (f32[1,4,128]{2,0,1:T(1,128)S(1)}, f32[1,4,128]{2,0,1:T(1,128)S(1)}, u32[]{:S(2)}, u32[]{:S(2)}) collective-permute-start(f32[1,4,128]{2,0,1:T(1,128)S(1)} %bitcast.23), channel_id=1, source_target_pairs={{0,6},{2,4},{4,2},{6,0},{8,14},{10,12},{12,10},{14,8},{16,22},{18,... | collective-permute-start | bytes 6152 | tf_op jit(solution)/shard_map/ppermute | solution.py:221
  18.6 1.2 %shard_map.107 = f32[2,128]{1,0:T(2,128)S(1)} custom-call(bf16[2,128,128]{2,1,0:T(8,128)(2,1)S(1)} %collective-permute-done.1.refs_0_, bf16[16,192,128]{2,1,0:T(8,128)(2,1)S(1)} %shard_map.104.refs_1_.refs_2_, bf16[16,192,128]{2,1,0:T(8,128)(2,1)S(1)} %collective-permute-done.4.refs_2_.refs_3_), custom_call_target="tpu_custom_call" | custom-call | flops 402653184 | bytes 1572864 | tf_op jit(solution)/shard_map/pallas_call | solution.py:131
  19.8 0.2 collective-permute-done.5
  20.1 1.4 %collective-permute-start.6 = (f32[2,2,128]{2,0,1:T(2,128)S(1)}, f32[2,2,128]{2,0,1:T(2,128)S(1)}, u32[]{:S(2)}, u32[]{:S(2)}) collective-permute-start(f32[2,2,128]{2,0,1:T(2,128)S(1)} %pad_maximum_fusion.4), channel_id=1, source_target_pairs={{0,10},{2,8},{4,14},{6,12},{8,2},{10,0},{12,6},{14,4},{16,26},{18,... | collective-permute-start | bytes 6152 | tf_op jit(solution)/shard_map/ppermute | solution.py:221
  21.5 0.0 copy-start.7
  21.5 1.2 %shard_map.108 = f32[2,128]{1,0:T(2,128)S(1)} custom-call(bf16[1,128,128]{2,1,0:T(8,128)(2,1)S(1)} %bitcast.18, bf16[1,128,128]{2,1,0:T(8,128)(2,1)S(1)} %collective-permute-done.refs_1_, bf16[16,192,128]{2,1,0:T(8,128)(2,1)S(1)} %shard_map.104.refs_1_.refs_2_, bf16[16,192,128]{2,1,0:T(8,128)(2,1)S(1)} %collective-permute-done.4.refs_2_.refs_3_), custom_call_target="tpu_custom_call" | custom-call | flops 402653184 | bytes 1572864 | tf_op jit(solution)/shard_map/pallas_call | solution.py:131
  22.7 0.4 %collective-permute-done.6 = f32[2,2,128]{2,0,1:T(2,128)S(1)} collective-permute-done((f32[2,2,128]{2,0,1:T(2,128)S(1)}, f32[2,2,128]{2,0,1:T(2,128)S(1)}, u32[]{:S(2)}, u32[]{:S(2)}) %collective-permute-start.6) | collective-permute-done | bytes 2080 | tf_op jit(solution)/shard_map/ppermute | solution.py:221
  23.2 0.0 copy-start.6
  23.2 0.0 collective-permute-done.7.other_ref
  23.2 2.3 %collective-permute-start.8 = (f32[4,1,128]{2,0,1:T(4,128)S(1)}, f32[4,1,128]{2,0,1:T(4,128)S(1)}, u32[]{:S(2)}, u32[]{:S(2)}) collective-permute-start(f32[4,1,128]{2,0,1:T(4,128)S(1)} %fusion.1), channel_id=1, source_target_pairs={{0,18},{2,16},{4,22},{6,20},{8,26},{10,24},{12,30},{14,28},{16,2},... | collective-permute-start | bytes 6152 | tf_op jit(solution)/shard_map/ppermute | solution.py:221
  25.5 0.0 copy-done.6
  25.5 0.0 copy-done.7
  25.5 1.1 %shard_map.109 = (f32[1,4]{1,0:T(1,128)}, s32[2,128]{1,0:T(2,128)S(1)}) custom-call(bf16[128,128]{1,0:T(8,128)(2,1)S(1)} %bitcast.19, bf16[4,192,128]{2,1,0:T(8,128)(2,1)S(1)} %get-tuple-element.45.own_ref, bf16[4,192,128]{2,1,0:T(8,128)(2,1)S(1)} %collective-permute-done.7.other_ref, s32[4,32]{1,0:T(4,128)S(1)} %get-tuple-element.58.where_ref, ...), custom_call_target="tpu_custom_call" | custom-call | flops 50331648 | bytes 393216 | tf_op jit(solution)/shard_map/pallas_call | solution.py:173
  26.7 0.5 %collective-permute-done.8 = f32[4,1,128]{2,0,1:T(4,128)S(1)} collective-permute-done((f32[4,1,128]{2,0,1:T(4,128)S(1)}, f32[4,1,128]{2,0,1:T(4,128)S(1)}, u32[]{:S(2)}, u32[]{:S(2)}) %collective-permute-start.8) | collective-permute-done | bytes 2080 | tf_op jit(solution)/shard_map/ppermute | solution.py:221
  27.2 0.7 %shard_map.110 = (f32[1,4,32]{2,1,0:T(4,128)}, f32[1,4]{1,0:T(1,128)}) custom-call(f32[8,128]{1,0:T(8,128)S(1)} %pad_maximum_fusion.1.returned_ref, f32[3,128]{1,0:T(4,128)S(1)} %get-tuple-element.52.teach_ref, s32[2,128]{1,0:T(2,128)S(1)} %get-tuple-element.53.index_ref), custom_call_target="tpu_custom_call" | custom-call | tf_op jit(solution)/shard_map/pallas_call | solution.py:208
  (11 shorter events, 0.1 us)
Async XLA Ops:
  0.6 3.6 %copy-start.2 = (s32[1,16]{1,0:T(1,128)S(1)}, s32[1,16]{1,0:T(1,128)}, u32[]{:S(2)}) copy-start(s32[1,16]{1,0:T(1,128)} %kept_ref.3) | copy-start | bytes 196
  0.6 6.7 %collective-permute-start = (bf16[1,128,128]{2,1,0:T(8,128)(2,1)}, bf16[1,128,128]{2,1,0:T(8,128)(2,1)S(1)}, u32[]{:S(2)}, u32[]{:S(2)}) collective-permute-start(bf16[1,128,128]{2,1,0:T(8,128)(2,1)} %bitcast.16), channel_id=1, source_target_pairs={{0,18},{2,16},{4,22},{6,20},{8,26},{10,24},{12,30},{14,28},{16,2},... | collective-permute-start | bytes 98312 | tf_op jit(solution)/shard_map/ppermute | solution.py:221
  4.2 1.1 %copy-start = (bf16[1,16,192,128]{3,2,1,0:T(8,128)(2,1)S(1)}, bf16[1,16,192,128]{3,2,1,0:T(8,128)(2,1)}, u32[]{:S(2)}) copy-start(bf16[1,16,192,128]{3,2,1,0:T(8,128)(2,1)} %param.9) | copy-start | bytes 2359300
  5.3 2.1 %copy-start.1 = (bf16[1,4,32,128]{3,2,1,0:T(8,128)(2,1)S(1)}, bf16[1,4,32,128]{3,2,1,0:T(8,128)(2,1)}, u32[]{:S(2)}) copy-start(bf16[1,4,32,128]{3,2,1,0:T(8,128)(2,1)} %param.8) | copy-start | bytes 98308
  5.3 3.4 %copy-start.3 = (bf16[1,4,192,128]{3,2,1,0:T(8,128)(2,1)S(1)}, bf16[1,4,192,128]{3,2,1,0:T(8,128)(2,1)}, u32[]{:S(2)}) copy-start(bf16[1,4,192,128]{3,2,1,0:T(8,128)(2,1)} %param.11) | copy-start | bytes 589828
  6.6 2.1 %copy-start.4 = (f32[1,4,32]{2,1,0:T(4,128)S(1)}, f32[1,4,32]{2,1,0:T(4,128)}, u32[]{:S(2)}) copy-start(f32[1,4,32]{2,1,0:T(4,128)} %teacher_ref.1) | copy-start | bytes 1540
  6.6 7.8 %collective-permute-start.4 = (bf16[16,192,128]{2,1,0:T(8,128)(2,1)S(1)}, bf16[16,192,128]{2,1,0:T(8,128)(2,1)S(1)}, u32[]{:S(2)}, u32[]{:S(2)}) collective-permute-start(bf16[16,192,128]{2,1,0:T(8,128)(2,1)S(1)} %shard_map.104.refs_1_.refs_2_), channel_id=1, source_target_pairs={{0,2},{2,0},{4,6},{6,4},{8,10},{10,8},{12,14},{14,12},{16,18},{18,... | collective-permute-start | bytes 2359304 | tf_op jit(solution)/shard_map/ppermute | solution.py:221
  7.4 1.3 %copy-start.5 = (s32[1,4]{1,0:T(1,128)S(1)}, s32[1,4]{1,0:T(1,128)}, u32[]{:S(2)}) copy-start(s32[1,4]{1,0:T(1,128)} %kept_ref.2) | copy-start | bytes 52
  7.4 4.2 %collective-permute-start.1 = (bf16[2,128,128]{2,1,0:T(8,128)(2,1)S(1)}, bf16[2,128,128]{2,1,0:T(8,128)(2,1)S(1)}, u32[]{:S(2)}, u32[]{:S(2)}) collective-permute-start(bf16[2,128,128]{2,1,0:T(8,128)(2,1)S(1)} %pad_maximum_fusion), channel_id=1, source_target_pairs={{0,10},{2,8},{4,14},{6,12},{8,2},{10,0},{12,6},{14,4},{16,26},{18,... | collective-permute-start | bytes 196616 | tf_op jit(solution)/shard_map/ppermute | solution.py:221
  9.6 4.8 %collective-permute-start.3 = (bf16[2,128,128]{2,1,0:T(8,128)(2,1)S(1)}, bf16[2,128,128]{2,1,0:T(8,128)(2,1)S(1)}, u32[]{:S(2)}, u32[]{:S(2)}) collective-permute-start(bf16[2,128,128]{2,1,0:T(8,128)(2,1)S(1)} %pad_maximum_fusion), channel_id=1, source_target_pairs={{0,6},{2,4},{4,2},{6,0},{8,14},{10,12},{12,10},{14,8},{16,22},{18,... | collective-permute-start | bytes 196616 | tf_op jit(solution)/shard_map/ppermute | solution.py:221
  11.7 4.1 %collective-permute-start.2 = (bf16[2,128,128]{2,1,0:T(8,128)(2,1)S(1)}, bf16[2,128,128]{2,1,0:T(8,128)(2,1)S(1)}, u32[]{:S(2)}, u32[]{:S(2)}) collective-permute-start(bf16[2,128,128]{2,1,0:T(8,128)(2,1)S(1)} %collective-permute-done.1.refs_0_), channel_id=1, source_target_pairs={{0,6},{2,4},{4,2},{6,0},{8,14},{10,12},{12,10},{14,8},{16,22},{18,... | collective-permute-start | bytes 196616 | tf_op jit(solution)/shard_map/ppermute | solution.py:221
  12.9 10.3 %collective-permute-start.7 = (bf16[4,192,128]{2,1,0:T(8,128)(2,1)S(1)}, bf16[4,192,128]{2,1,0:T(8,128)(2,1)S(1)}, u32[]{:S(2)}, u32[]{:S(2)}) collective-permute-start(bf16[4,192,128]{2,1,0:T(8,128)(2,1)S(1)} %get-tuple-element.45.own_ref), channel_id=1, source_target_pairs={{0,1},{1,0},{2,3},{3,2},{4,5},{5,4},{6,7},{7,6},{8,9},{9,8},{10,11... | collective-permute-start | bytes 589832 | tf_op jit(solution)/shard_map/ppermute | solution.py:258
  17.0 3.1 %collective-permute-start.5 = (f32[1,4,128]{2,0,1:T(1,128)S(1)}, f32[1,4,128]{2,0,1:T(1,128)S(1)}, u32[]{:S(2)}, u32[]{:S(2)}) collective-permute-start(f32[1,4,128]{2,0,1:T(1,128)S(1)} %bitcast.23), channel_id=1, source_target_pairs={{0,6},{2,4},{4,2},{6,0},{8,14},{10,12},{12,10},{14,8},{16,22},{18,... | collective-permute-start | bytes 6152 | tf_op jit(solution)/shard_map/ppermute | solution.py:221
  20.1 3.1 %collective-permute-start.6 = (f32[2,2,128]{2,0,1:T(2,128)S(1)}, f32[2,2,128]{2,0,1:T(2,128)S(1)}, u32[]{:S(2)}, u32[]{:S(2)}) collective-permute-start(f32[2,2,128]{2,0,1:T(2,128)S(1)} %pad_maximum_fusion.4), channel_id=1, source_target_pairs={{0,10},{2,8},{4,14},{6,12},{8,2},{10,0},{12,6},{14,4},{16,26},{18,... | collective-permute-start | bytes 6152 | tf_op jit(solution)/shard_map/ppermute | solution.py:221
  21.5 4.0 %copy-start.7 = (s32[1,4,32]{2,1,0:T(4,128)S(1)}, s32[1,4,32]{2,1,0:T(4,128)}, u32[]{:S(2)}) copy-start(s32[1,4,32]{2,1,0:T(4,128)} %param.14) | copy-start | bytes 1540
  23.2 2.3 %copy-start.6 = (s32[1,4,32,1]{2,3,1,0:T(1,128)S(1)}, s32[1,4,32,1]{2,3,1,0:T(1,128)}, u32[]{:S(2)}) copy-start(s32[1,4,32,1]{2,3,1,0:T(1,128)} %param.13) | copy-start | bytes 1540
  23.2 4.0 %collective-permute-start.8 = (f32[4,1,128]{2,0,1:T(4,128)S(1)}, f32[4,1,128]{2,0,1:T(4,128)S(1)}, u32[]{:S(2)}, u32[]{:S(2)}) collective-permute-start(f32[4,1,128]{2,0,1:T(4,128)S(1)} %fusion.1), channel_id=1, source_target_pairs={{0,18},{2,16},{4,22},{6,20},{8,26},{10,24},{12,30},{14,28},{16,2},... | collective-permute-start | bytes 6152 | tf_op jit(solution)/shard_map/ppermute | solution.py:221

commit v6 on v5

--- a/solution.py
+++ b/solution.py
@@ -52,7 +52,7 @@
         out_ref[i] = kept_unit(rows_ref[i], kept_ref[0, i])
         return carry
 
-    lax.fori_loop(0, rows_ref.shape[0], one, 0, unroll=4)
+    lax.fori_loop(0, rows_ref.shape[0], one, 0, unroll=rows_ref.shape[0])
 
 
 def prepare(rows, kept):
@@ -186,11 +186,12 @@
     )(query_rows, own, other, whose, lane)
 
 
-def distill_kernel(returned_ref, teach_ref, index_ref, student_ref, distill_ref):
+def distill_kernel(mine_ref, back_ref, teach_ref, index_ref, student_ref, distill_ref):
     queries, width = student_ref.shape[1:]
-    scorers, lanes = returned_ref.shape
+    scorers, lanes = 1 + back_ref.shape[0], back_ref.shape[1]
+    returned = jnp.concatenate([mine_ref[...], back_ref[...]], axis=0)
     picked = jnp.take_along_axis(
-        returned_ref[...], jnp.broadcast_to(index_ref[1:2, :], (scorers, lanes)), axis=1
+        returned, jnp.broadcast_to(index_ref[1:2, :], (scorers, lanes)), axis=1
     )
     row = lax.broadcasted_iota(jnp.int32, (scorers, lanes), 0)
     student = jnp.sum(jnp.where(row == index_ref[0:1, :], picked, 0.0), axis=0, keepdims=True)
@@ -211,10 +212,10 @@
             jax.ShapeDtypeStruct(shape, jnp.float32),
             jax.ShapeDtypeStruct(shape[:2], jnp.float32),
         ),
-        in_specs=[VMEM] * 3,
+        in_specs=[VMEM] * 4,
         out_specs=(VMEM, VMEM),
         compiler_params=pltpu.CompilerParams(vmem_limit_bytes=LIMIT),
-    )(returned, teach, index)
+    )(*returned, teach, index)
 
 
 def swap(values, axis, bit):
@@ -288,7 +289,7 @@
         if n == len(bits) - 2:
             arrived, contrast, index = tie((arrived, contrast, index))
         back = jnp.concatenate([back[:, :half], arrived], axis=0)
-    returned = jnp.concatenate([mine[:1], back[:, 0]], axis=0)
+    returned = [mine[:1], back[:, 0]]
     student, distill = distill_loss(returned, teach, index, teacher.shape)
     return (student, distill, contrast)
 

time: 28.1 us -> 27.8 us (0.989)
  starting transfers between devices: 15.2 us -> 15.5 us
where the time goes in v6:
time: 27.8 us; the launch traced here: 27.7 us
  starting transfers between devices  15.5 us (56%)
  Pallas kernels  8.7 us (31%)
  waiting for transfers between devices  1.49 us (5%)
  local copies, waits for them, and re-layouts  1.17 us (4%)
  between operations  0.74 us (3%)
    ppermute x8, starting transfers between devices, swap(): lax.ppermute(values, axis, [(i, i ^ bit) for i in range(lax.axis_size(axi...  14 us
    pallas_call x4, Pallas kernels, score(): pl.pallas_call(functools.partial(score_kernel, qlen, len(query_list)), ou...  4.89 us
    ppermute x1, starting transfers between devices, per_device(): lax.ppermute(own_docs, 'blk', [(i, (i + k) % groups) for i in range(group...  1.49 us
    ppermute x8, waiting for transfers between devices, swap(): lax.ppermute(values, axis, [(i, i ^ bit) for i in range(lax.axis_size(axi...  1.49 us
    unnamed x16, local copies, waits for them, and re-layouts  1.16 us
    pallas_call x1, Pallas kernels, contrast_loss(): pl.pallas_call(functools.partial(contrast_kernel, qlen), out_shape=(jax.S...  1.13 us
    pallas_call x1, Pallas kernels, prepare(): pl.pallas_call(prepare_kernel, out_shape=jax.ShapeDtypeStruct(rows.shape,...  1.05 us
    pallas_call x1, Pallas kernels, prepare_docs(): pl.pallas_call(functools.partial(prepare_docs_kernel, teacher.shape[2]),...  0.89 us
  transfers between devices with their start and end apart: 9, of which 5 were waited for; matrix products, arithmetic and copies ran while one was open for 0% of the time, Pallas kernels for 29%

profile of v6, /device:TPU:0, one launch (start us, length us, event | category | flops | bytes accessed | tf_op | source)
XLA Modules:
  0.0 27.7 jit_solution(11079323164644258683)
XLA Ops:
  0.6 0.0 copy-start.2
  0.6 3.5 %collective-permute-start = (bf16[1,128,128]{2,1,0:T(8,128)(2,1)}, bf16[1,128,128]{2,1,0:T(8,128)(2,1)S(1)}, u32[]{:S(2)}, u32[]{:S(2)}) collective-permute-start(bf16[1,128,128]{2,1,0:T(8,128)(2,1)} %bitcast.16), channel_id=1, source_target_pairs={{0,18},{2,16},{4,22},{6,20},{8,26},{10,24},{12,30},{14,28},{16,2},... | collective-permute-start | bytes 98312 | tf_op jit(solution)/shard_map/ppermute | solution.py:222
  4.2 0.0 copy-done.2
  4.2 0.0 copy-start
  4.2 1.1 %copy-done = bf16[1,16,192,128]{3,2,1,0:T(8,128)(2,1)S(1)} copy-done((bf16[1,16,192,128]{3,2,1,0:T(8,128)(2,1)S(1)}, bf16[1,16,192,128]{3,2,1,0:T(8,128)(2,1)}, u32[]{:S(2)}) %copy-start) | copy-done | bytes 786456
  5.3 0.0 copy-start.1
  5.3 0.0 copy-start.3
  5.3 1.1 %shard_map.104.refs_1_.refs_2_ = bf16[16,192,128]{2,1,0:T(8,128)(2,1)S(1)} custom-call(s32[1,16]{1,0:T(1,128)S(1)} %copy-done.2, bf16[16,192,128]{2,1,0:T(8,128)(2,1)S(1)} %bitcast.15), custom_call_target="tpu_custom_call" | custom-call | flops 6291456 | bytes 1572864 | tf_op jit(solution)/shard_map/pallas_call | solution.py:59
  6.4 0.0 copy-start.4
  6.4 0.7 %collective-permute-start.4 = (bf16[16,192,128]{2,1,0:T(8,128)(2,1)S(1)}, bf16[16,192,128]{2,1,0:T(8,128)(2,1)S(1)}, u32[]{:S(2)}, u32[]{:S(2)}) collective-permute-start(bf16[16,192,128]{2,1,0:T(8,128)(2,1)S(1)} %shard_map.104.refs_1_.refs_2_), channel_id=1, source_target_pairs={{0,2},{2,0},{4,6},{6,4},{8,10},{10,8},{12,14},{14,12},{16,18},{18,... | collective-permute-start | bytes 2359304 | tf_op jit(solution)/shard_map/ppermute | solution.py:222
  7.1 0.0 collective-permute-done.refs_1_
  7.1 0.0 copy-done.1
  7.2 0.0 copy-start.5
  7.2 1.3 %collective-permute-start.1 = (bf16[2,128,128]{2,1,0:T(8,128)(2,1)S(1)}, bf16[2,128,128]{2,1,0:T(8,128)(2,1)S(1)}, u32[]{:S(2)}, u32[]{:S(2)}) collective-permute-start(bf16[2,128,128]{2,1,0:T(8,128)(2,1)S(1)} %pad_maximum_fusion), channel_id=1, source_target_pairs={{0,10},{2,8},{4,14},{6,12},{8,2},{10,0},{12,6},{14,4},{16,26},{18,... | collective-permute-start | bytes 196616 | tf_op jit(solution)/shard_map/ppermute | solution.py:222
  8.4 0.0 copy-done.3
  8.4 0.0 copy-done.4
  8.5 0.0 copy-done.5
  8.5 0.9 %shard_map.103 = (bf16[4,192,128]{2,1,0:T(8,128)(2,1)S(1)}, f32[3,128]{1,0:T(4,128)S(1)}) custom-call(s32[1,4]{1,0:T(1,128)S(1)} %copy-done.5, bf16[4,192,128]{2,1,0:T(8,128)(2,1)S(1)} %bitcast.21, f32[1,4,32]{2,1,0:T(4,128)S(1)} %copy-done.4), custom_call_target="tpu_custom_call" | custom-call | flops 15728640000 | bytes 393216 | tf_op jit(solution)/shard_map/pallas_call | solution.py:88
  9.3 1.6 %collective-permute-start.3 = (bf16[2,128,128]{2,1,0:T(8,128)(2,1)S(1)}, bf16[2,128,128]{2,1,0:T(8,128)(2,1)S(1)}, u32[]{:S(2)}, u32[]{:S(2)}) collective-permute-start(bf16[2,128,128]{2,1,0:T(8,128)(2,1)S(1)} %pad_maximum_fusion), channel_id=1, source_target_pairs={{0,6},{2,4},{4,2},{6,0},{8,14},{10,12},{12,10},{14,8},{16,22},{18,... | collective-permute-start | bytes 196616 | tf_op jit(solution)/shard_map/ppermute | solution.py:222
  11.0 0.5 %collective-permute-done.1.refs_0_ = bf16[2,128,128]{2,1,0:T(8,128)(2,1)S(1)} collective-permute-done((bf16[2,128,128]{2,1,0:T(8,128)(2,1)S(1)}, bf16[2,128,128]{2,1,0:T(8,128)(2,1)S(1)}, u32[]{:S(2)}, u32[]{:S(2)}) %collective-permute-start.1) | collective-permute-done | bytes 65568 | tf_op jit(solution)/shard_map/ppermute | solution.py:222
  11.4 1.2 %collective-permute-start.2 = (bf16[2,128,128]{2,1,0:T(8,128)(2,1)S(1)}, bf16[2,128,128]{2,1,0:T(8,128)(2,1)S(1)}, u32[]{:S(2)}, u32[]{:S(2)}) collective-permute-start(bf16[2,128,128]{2,1,0:T(8,128)(2,1)S(1)} %collective-permute-done.1.refs_0_), channel_id=1, source_target_pairs={{0,6},{2,4},{4,2},{6,0},{8,14},{10,12},{12,10},{14,8},{16,22},{18,... | collective-permute-start | bytes 196616 | tf_op jit(solution)/shard_map/ppermute | solution.py:222
  12.7 1.5 %collective-permute-start.7 = (bf16[4,192,128]{2,1,0:T(8,128)(2,1)S(1)}, bf16[4,192,128]{2,1,0:T(8,128)(2,1)S(1)}, u32[]{:S(2)}, u32[]{:S(2)}) collective-permute-start(bf16[4,192,128]{2,1,0:T(8,128)(2,1)S(1)} %get-tuple-element.45.own_ref), channel_id=1, source_target_pairs={{0,1},{1,0},{2,3},{3,2},{4,5},{5,4},{6,7},{7,6},{8,9},{9,8},{10,11... | collective-permute-start | bytes 589832 | tf_op jit(solution)/shard_map/ppermute | solution.py:259
  14.1 0.0 collective-permute-done.3.refs_0_
  14.1 0.0 collective-permute-done.4.refs_2_.refs_3_
  14.1 1.2 %shard_map.105 = f32[2,128]{1,0:T(2,128)S(1)} custom-call(bf16[2,128,128]{2,1,0:T(8,128)(2,1)S(1)} %collective-permute-done.3.refs_0_, bf16[16,192,128]{2,1,0:T(8,128)(2,1)S(1)} %shard_map.104.refs_1_.refs_2_, bf16[16,192,128]{2,1,0:T(8,128)(2,1)S(1)} %collective-permute-done.4.refs_2_.refs_3_), custom_call_target="tpu_custom_call" | custom-call | flops 402653184 | bytes 1572864 | tf_op jit(solution)/shard_map/pallas_call | solution.py:131
  15.4 0.1 collective-permute-done.2.refs_0_
  15.5 1.2 %shard_map.106 = f32[2,128]{1,0:T(2,128)S(1)} custom-call(bf16[2,128,128]{2,1,0:T(8,128)(2,1)S(1)} %collective-permute-done.2.refs_0_, bf16[16,192,128]{2,1,0:T(8,128)(2,1)S(1)} %shard_map.104.refs_1_.refs_2_, bf16[16,192,128]{2,1,0:T(8,128)(2,1)S(1)} %collective-permute-done.4.refs_2_.refs_3_), custom_call_target="tpu_custom_call" | custom-call | flops 402653184 | bytes 1572864 | tf_op jit(solution)/shard_map/pallas_call | solution.py:131
  16.7 1.6 %collective-permute-start.5 = (f32[1,4,128]{2,0,1:T(1,128)S(1)}, f32[1,4,128]{2,0,1:T(1,128)S(1)}, u32[]{:S(2)}, u32[]{:S(2)}) collective-permute-start(f32[1,4,128]{2,0,1:T(1,128)S(1)} %bitcast.23), channel_id=1, source_target_pairs={{0,6},{2,4},{4,2},{6,0},{8,14},{10,12},{12,10},{14,8},{16,22},{18,... | collective-permute-start | bytes 6152 | tf_op jit(solution)/shard_map/ppermute | solution.py:222
  18.4 1.2 %shard_map.107 = f32[2,128]{1,0:T(2,128)S(1)} custom-call(bf16[2,128,128]{2,1,0:T(8,128)(2,1)S(1)} %collective-permute-done.1.refs_0_, bf16[16,192,128]{2,1,0:T(8,128)(2,1)S(1)} %shard_map.104.refs_1_.refs_2_, bf16[16,192,128]{2,1,0:T(8,128)(2,1)S(1)} %collective-permute-done.4.refs_2_.refs_3_), custom_call_target="tpu_custom_call" | custom-call | flops 402653184 | bytes 1572864 | tf_op jit(solution)/shard_map/pallas_call | solution.py:131
  19.6 0.2 collective-permute-done.5
  19.8 1.4 %collective-permute-start.6 = (f32[2,2,128]{2,0,1:T(2,128)S(1)}, f32[2,2,128]{2,0,1:T(2,128)S(1)}, u32[]{:S(2)}, u32[]{:S(2)}) collective-permute-start(f32[2,2,128]{2,0,1:T(2,128)S(1)} %pad_maximum_fusion.3), channel_id=1, source_target_pairs={{0,10},{2,8},{4,14},{6,12},{8,2},{10,0},{12,6},{14,4},{16,26},{18,... | collective-permute-start | bytes 6152 | tf_op jit(solution)/shard_map/ppermute | solution.py:222
  21.3 0.0 copy-start.7
  21.3 1.2 %shard_map.108 = f32[2,128]{1,0:T(2,128)S(1)} custom-call(bf16[1,128,128]{2,1,0:T(8,128)(2,1)S(1)} %bitcast.18, bf16[1,128,128]{2,1,0:T(8,128)(2,1)S(1)} %collective-permute-done.refs_1_, bf16[16,192,128]{2,1,0:T(8,128)(2,1)S(1)} %shard_map.104.refs_1_.refs_2_, bf16[16,192,128]{2,1,0:T(8,128)(2,1)S(1)} %collective-permute-done.4.refs_2_.refs_3_), custom_call_target="tpu_custom_call" | custom-call | flops 402653184 | bytes 1572864 | tf_op jit(solution)/shard_map/pallas_call | solution.py:131
  22.5 0.4 %collective-permute-done.6 = f32[2,2,128]{2,0,1:T(2,128)S(1)} collective-permute-done((f32[2,2,128]{2,0,1:T(2,128)S(1)}, f32[2,2,128]{2,0,1:T(2,128)S(1)}, u32[]{:S(2)}, u32[]{:S(2)}) %collective-permute-start.6) | collective-permute-done | bytes 2080 | tf_op jit(solution)/shard_map/ppermute | solution.py:222
  22.9 0.0 copy-start.6
  22.9 0.0 collective-permute-done.7.other_ref
  22.9 2.5 %collective-permute-start.8 = (f32[4,1,128]{2,0,1:T(4,128)S(1)}, f32[4,1,128]{2,0,1:T(4,128)S(1)}, u32[]{:S(2)}, u32[]{:S(2)}) collective-permute-start(f32[4,1,128]{2,0,1:T(4,128)S(1)} %fusion.1), channel_id=1, source_target_pairs={{0,18},{2,16},{4,22},{6,20},{8,26},{10,24},{12,30},{14,28},{16,2},... | collective-permute-start | bytes 6152 | tf_op jit(solution)/shard_map/ppermute | solution.py:222
  25.5 0.0 copy-done.6
  25.5 0.0 copy-done.7
  25.5 1.1 %shard_map.109 = (f32[1,4]{1,0:T(1,128)}, s32[2,128]{1,0:T(2,128)S(1)}) custom-call(bf16[128,128]{1,0:T(8,128)(2,1)S(1)} %bitcast.19, bf16[4,192,128]{2,1,0:T(8,128)(2,1)S(1)} %get-tuple-element.45.own_ref, bf16[4,192,128]{2,1,0:T(8,128)(2,1)S(1)} %collective-permute-done.7.other_ref, s32[4,32]{1,0:T(4,128)S(1)} %get-tuple-element.58.where_ref, ...), custom_call_target="tpu_custom_call" | custom-call | flops 50331648 | bytes 393216 | tf_op jit(solution)/shard_map/pallas_call | solution.py:173
  26.7 0.3 collective-permute-done.8
  26.9 0.7 %shard_map.110 = (f32[1,4,32]{2,1,0:T(4,128)}, f32[1,4]{1,0:T(1,128)}) custom-call(f32[1,128]{1,0:T(1,128)S(1)} %get-tuple-element.62.mine_ref, f32[7,128]{1,0:T(8,128)S(1)} %maximum_bitcast_fusion.back_ref, f32[3,128]{1,0:T(4,128)S(1)} %get-tuple-element.52.teach_ref, s32[2,128]{1,0:T(2,128)S(1)} %get-tuple-element.53.index_ref), custom_call_target="tpu_custom_call" | custom-call | tf_op jit(solution)/shard_map/pallas_call | solution.py:209
  (10 shorter events, 0.1 us)
Async XLA Ops:
  0.6 3.6 %copy-start.2 = (s32[1,16]{1,0:T(1,128)S(1)}, s32[1,16]{1,0:T(1,128)}, u32[]{:S(2)}) copy-start(s32[1,16]{1,0:T(1,128)} %kept_ref.3) | copy-start | bytes 196
  0.6 6.5 %collective-permute-start = (bf16[1,128,128]{2,1,0:T(8,128)(2,1)}, bf16[1,128,128]{2,1,0:T(8,128)(2,1)S(1)}, u32[]{:S(2)}, u32[]{:S(2)}) collective-permute-start(bf16[1,128,128]{2,1,0:T(8,128)(2,1)} %bitcast.16), channel_id=1, source_target_pairs={{0,18},{2,16},{4,22},{6,20},{8,26},{10,24},{12,30},{14,28},{16,2},... | collective-permute-start | bytes 98312 | tf_op jit(solution)/shard_map/ppermute | solution.py:222
  4.2 1.1 %copy-start = (bf16[1,16,192,128]{3,2,1,0:T(8,128)(2,1)S(1)}, bf16[1,16,192,128]{3,2,1,0:T(8,128)(2,1)}, u32[]{:S(2)}) copy-start(bf16[1,16,192,128]{3,2,1,0:T(8,128)(2,1)} %param.9) | copy-start | bytes 2359300
  5.3 1.8 %copy-start.1 = (bf16[1,4,32,128]{3,2,1,0:T(8,128)(2,1)S(1)}, bf16[1,4,32,128]{3,2,1,0:T(8,128)(2,1)}, u32[]{:S(2)}) copy-start(bf16[1,4,32,128]{3,2,1,0:T(8,128)(2,1)} %param.8) | copy-start | bytes 98308
  5.3 3.1 %copy-start.3 = (bf16[1,4,192,128]{3,2,1,0:T(8,128)(2,1)S(1)}, bf16[1,4,192,128]{3,2,1,0:T(8,128)(2,1)}, u32[]{:S(2)}) copy-start(bf16[1,4,192,128]{3,2,1,0:T(8,128)(2,1)} %param.11) | copy-start | bytes 589828
  6.4 2.1 %copy-start.4 = (f32[1,4,32]{2,1,0:T(4,128)S(1)}, f32[1,4,32]{2,1,0:T(4,128)}, u32[]{:S(2)}) copy-start(f32[1,4,32]{2,1,0:T(4,128)} %teacher_ref.1) | copy-start | bytes 1540
  6.4 7.8 %collective-permute-start.4 = (bf16[16,192,128]{2,1,0:T(8,128)(2,1)S(1)}, bf16[16,192,128]{2,1,0:T(8,128)(2,1)S(1)}, u32[]{:S(2)}, u32[]{:S(2)}) collective-permute-start(bf16[16,192,128]{2,1,0:T(8,128)(2,1)S(1)} %shard_map.104.refs_1_.refs_2_), channel_id=1, source_target_pairs={{0,2},{2,0},{4,6},{6,4},{8,10},{10,8},{12,14},{14,12},{16,18},{18,... | collective-permute-start | bytes 2359304 | tf_op jit(solution)/shard_map/ppermute | solution.py:222
  7.2 1.3 %copy-start.5 = (s32[1,4]{1,0:T(1,128)S(1)}, s32[1,4]{1,0:T(1,128)}, u32[]{:S(2)}) copy-start(s32[1,4]{1,0:T(1,128)} %kept_ref.2) | copy-start | bytes 52
  7.2 4.2 %collective-permute-start.1 = (bf16[2,128,128]{2,1,0:T(8,128)(2,1)S(1)}, bf16[2,128,128]{2,1,0:T(8,128)(2,1)S(1)}, u32[]{:S(2)}, u32[]{:S(2)}) collective-permute-start(bf16[2,128,128]{2,1,0:T(8,128)(2,1)S(1)} %pad_maximum_fusion), channel_id=1, source_target_pairs={{0,10},{2,8},{4,14},{6,12},{8,2},{10,0},{12,6},{14,4},{16,26},{18,... | collective-permute-start | bytes 196616 | tf_op jit(solution)/shard_map/ppermute | solution.py:222
  9.3 4.8 %collective-permute-start.3 = (bf16[2,128,128]{2,1,0:T(8,128)(2,1)S(1)}, bf16[2,128,128]{2,1,0:T(8,128)(2,1)S(1)}, u32[]{:S(2)}, u32[]{:S(2)}) collective-permute-start(bf16[2,128,128]{2,1,0:T(8,128)(2,1)S(1)} %pad_maximum_fusion), channel_id=1, source_target_pairs={{0,6},{2,4},{4,2},{6,0},{8,14},{10,12},{12,10},{14,8},{16,22},{18,... | collective-permute-start | bytes 196616 | tf_op jit(solution)/shard_map/ppermute | solution.py:222
  11.4 4.1 %collective-permute-start.2 = (bf16[2,128,128]{2,1,0:T(8,128)(2,1)S(1)}, bf16[2,128,128]{2,1,0:T(8,128)(2,1)S(1)}, u32[]{:S(2)}, u32[]{:S(2)}) collective-permute-start(bf16[2,128,128]{2,1,0:T(8,128)(2,1)S(1)} %collective-permute-done.1.refs_0_), channel_id=1, source_target_pairs={{0,6},{2,4},{4,2},{6,0},{8,14},{10,12},{12,10},{14,8},{16,22},{18,... | collective-permute-start | bytes 196616 | tf_op jit(solution)/shard_map/ppermute | solution.py:222
  12.7 10.3 %collective-permute-start.7 = (bf16[4,192,128]{2,1,0:T(8,128)(2,1)S(1)}, bf16[4,192,128]{2,1,0:T(8,128)(2,1)S(1)}, u32[]{:S(2)}, u32[]{:S(2)}) collective-permute-start(bf16[4,192,128]{2,1,0:T(8,128)(2,1)S(1)} %get-tuple-element.45.own_ref), channel_id=1, source_target_pairs={{0,1},{1,0},{2,3},{3,2},{4,5},{5,4},{6,7},{7,6},{8,9},{9,8},{10,11... | collective-permute-start | bytes 589832 | tf_op jit(solution)/shard_map/ppermute | solution.py:259
  16.7 3.1 %collective-permute-start.5 = (f32[1,4,128]{2,0,1:T(1,128)S(1)}, f32[1,4,128]{2,0,1:T(1,128)S(1)}, u32[]{:S(2)}, u32[]{:S(2)}) collective-permute-start(f32[1,4,128]{2,0,1:T(1,128)S(1)} %bitcast.23), channel_id=1, source_target_pairs={{0,6},{2,4},{4,2},{6,0},{8,14},{10,12},{12,10},{14,8},{16,22},{18,... | collective-permute-start | bytes 6152 | tf_op jit(solution)/shard_map/ppermute | solution.py:222
  19.8 3.1 %collective-permute-start.6 = (f32[2,2,128]{2,0,1:T(2,128)S(1)}, f32[2,2,128]{2,0,1:T(2,128)S(1)}, u32[]{:S(2)}, u32[]{:S(2)}) collective-permute-start(f32[2,2,128]{2,0,1:T(2,128)S(1)} %pad_maximum_fusion.3), channel_id=1, source_target_pairs={{0,10},{2,8},{4,14},{6,12},{8,2},{10,0},{12,6},{14,4},{16,26},{18,... | collective-permute-start | bytes 6152 | tf_op jit(solution)/shard_map/ppermute | solution.py:222
  21.3 4.2 %copy-start.7 = (s32[1,4,32]{2,1,0:T(4,128)S(1)}, s32[1,4,32]{2,1,0:T(4,128)}, u32[]{:S(2)}) copy-start(s32[1,4,32]{2,1,0:T(4,128)} %param.14) | copy-start | bytes 1540
  22.9 2.6 %copy-start.6 = (s32[1,4,32,1]{2,3,1,0:T(1,128)S(1)}, s32[1,4,32,1]{2,3,1,0:T(1,128)}, u32[]{:S(2)}) copy-start(s32[1,4,32,1]{2,3,1,0:T(1,128)} %param.13) | copy-start | bytes 1540
  22.9 4.0 %collective-permute-start.8 = (f32[4,1,128]{2,0,1:T(4,128)S(1)}, f32[4,1,128]{2,0,1:T(4,128)S(1)}, u32[]{:S(2)}, u32[]{:S(2)}) collective-permute-start(f32[4,1,128]{2,0,1:T(4,128)S(1)} %fusion.1), channel_id=1, source_target_pairs={{0,18},{2,16},{4,22},{6,20},{8,26},{10,24},{12,30},{14,28},{16,2},... | collective-permute-start | bytes 6152 | tf_op jit(solution)/shard_map/ppermute | solution.py:222

commit v7 on v6

--- a/solution.py
+++ b/solution.py
@@ -189,7 +189,7 @@
 def distill_kernel(mine_ref, back_ref, teach_ref, index_ref, student_ref, distill_ref):
     queries, width = student_ref.shape[1:]
     scorers, lanes = 1 + back_ref.shape[0], back_ref.shape[1]
-    returned = jnp.concatenate([mine_ref[...], back_ref[...]], axis=0)
+    returned = jnp.concatenate([mine_ref[0:1, :], back_ref[...]], axis=0)
     picked = jnp.take_along_axis(
         returned, jnp.broadcast_to(index_ref[1:2, :], (scorers, lanes)), axis=1
     )
@@ -289,7 +289,7 @@
         if n == len(bits) - 2:
             arrived, contrast, index = tie((arrived, contrast, index))
         back = jnp.concatenate([back[:, :half], arrived], axis=0)
-    returned = [mine[:1], back[:, 0]]
+    returned = [mine, back[:, 0]]
     student, distill = distill_loss(returned, teach, index, teacher.shape)
     return (student, distill, contrast)
 

time: 27.8 us -> 27.8 us (level)
  no operation moved by 1% of the time
where the time goes in v7:
time: 27.8 us; the launch traced here: 27.7 us
  starting transfers between devices  15.5 us (56%)
  Pallas kernels  8.7 us (31%)
  waiting for transfers between devices  1.49 us (5%)
  local copies, waits for them, and re-layouts  1.17 us (4%)
  between operations  0.74 us (3%)
    ppermute x8, starting transfers between devices, swap(): lax.ppermute(values, axis, [(i, i ^ bit) for i in range(lax.axis_size(axi...  14 us
    pallas_call x4, Pallas kernels, score(): pl.pallas_call(functools.partial(score_kernel, qlen, len(query_list)), ou...  4.89 us
    ppermute x1, starting transfers between devices, per_device(): lax.ppermute(own_docs, 'blk', [(i, (i + k) % groups) for i in range(group...  1.49 us
    ppermute x8, waiting for transfers between devices, swap(): lax.ppermute(values, axis, [(i, i ^ bit) for i in range(lax.axis_size(axi...  1.49 us
    unnamed x16, local copies, waits for them, and re-layouts  1.16 us
    pallas_call x1, Pallas kernels, contrast_loss(): pl.pallas_call(functools.partial(contrast_kernel, qlen), out_shape=(jax.S...  1.13 us
    pallas_call x1, Pallas kernels, prepare(): pl.pallas_call(prepare_kernel, out_shape=jax.ShapeDtypeStruct(rows.shape,...  1.05 us
    pallas_call x1, Pallas kernels, prepare_docs(): pl.pallas_call(functools.partial(prepare_docs_kernel, teacher.shape[2]),...  0.89 us
  transfers between devices with their start and end apart: 9, of which 5 were waited for; matrix products, arithmetic and copies ran while one was open for 0% of the time, Pallas kernels for 29%

profile of v7, /device:TPU:0, one launch (start us, length us, event | category | flops | bytes accessed | tf_op | source)
XLA Modules:
  0.0 27.7 jit_solution(4378230124197531979)
XLA Ops:
  0.6 0.0 copy-start.2
  0.6 3.5 %collective-permute-start = (bf16[1,128,128]{2,1,0:T(8,128)(2,1)}, bf16[1,128,128]{2,1,0:T(8,128)(2,1)S(1)}, u32[]{:S(2)}, u32[]{:S(2)}) collective-permute-start(bf16[1,128,128]{2,1,0:T(8,128)(2,1)} %bitcast.16), channel_id=1, source_target_pairs={{0,18},{2,16},{4,22},{6,20},{8,26},{10,24},{12,30},{14,28},{16,2},... | collective-permute-start | bytes 98312 | tf_op jit(solution)/shard_map/ppermute | solution.py:222
  4.2 0.0 copy-done.2
  4.2 0.0 copy-start
  4.2 1.1 %copy-done = bf16[1,16,192,128]{3,2,1,0:T(8,128)(2,1)S(1)} copy-done((bf16[1,16,192,128]{3,2,1,0:T(8,128)(2,1)S(1)}, bf16[1,16,192,128]{3,2,1,0:T(8,128)(2,1)}, u32[]{:S(2)}) %copy-start) | copy-done | bytes 786456
  5.3 0.0 copy-start.1
  5.3 0.0 copy-start.3
  5.3 1.1 %shard_map.104.refs_1_.refs_2_ = bf16[16,192,128]{2,1,0:T(8,128)(2,1)S(1)} custom-call(s32[1,16]{1,0:T(1,128)S(1)} %copy-done.2, bf16[16,192,128]{2,1,0:T(8,128)(2,1)S(1)} %bitcast.15), custom_call_target="tpu_custom_call" | custom-call | flops 6291456 | bytes 1572864 | tf_op jit(solution)/shard_map/pallas_call | solution.py:59
  6.4 0.0 copy-start.4
  6.4 0.7 %collective-permute-start.4 = (bf16[16,192,128]{2,1,0:T(8,128)(2,1)S(1)}, bf16[16,192,128]{2,1,0:T(8,128)(2,1)S(1)}, u32[]{:S(2)}, u32[]{:S(2)}) collective-permute-start(bf16[16,192,128]{2,1,0:T(8,128)(2,1)S(1)} %shard_map.104.refs_1_.refs_2_), channel_id=1, source_target_pairs={{0,2},{2,0},{4,6},{6,4},{8,10},{10,8},{12,14},{14,12},{16,18},{18,... | collective-permute-start | bytes 2359304 | tf_op jit(solution)/shard_map/ppermute | solution.py:222
  7.1 0.0 collective-permute-done.refs_1_
  7.1 0.0 copy-done.1
  7.2 0.0 copy-start.5
  7.2 1.3 %collective-permute-start.1 = (bf16[2,128,128]{2,1,0:T(8,128)(2,1)S(1)}, bf16[2,128,128]{2,1,0:T(8,128)(2,1)S(1)}, u32[]{:S(2)}, u32[]{:S(2)}) collective-permute-start(bf16[2,128,128]{2,1,0:T(8,128)(2,1)S(1)} %pad_maximum_fusion), channel_id=1, source_target_pairs={{0,10},{2,8},{4,14},{6,12},{8,2},{10,0},{12,6},{14,4},{16,26},{18,... | collective-permute-start | bytes 196616 | tf_op jit(solution)/shard_map/ppermute | solution.py:222
  8.4 0.0 copy-done.3
  8.4 0.0 copy-done.4
  8.5 0.0 copy-done.5
  8.5 0.9 %shard_map.103 = (bf16[4,192,128]{2,1,0:T(8,128)(2,1)S(1)}, f32[3,128]{1,0:T(4,128)S(1)}) custom-call(s32[1,4]{1,0:T(1,128)S(1)} %copy-done.5, bf16[4,192,128]{2,1,0:T(8,128)(2,1)S(1)} %bitcast.21, f32[1,4,32]{2,1,0:T(4,128)S(1)} %copy-done.4), custom_call_target="tpu_custom_call" | custom-call | flops 15728640000 | bytes 393216 | tf_op jit(solution)/shard_map/pallas_call | solution.py:88
  9.3 1.6 %collective-permute-start.3 = (bf16[2,128,128]{2,1,0:T(8,128)(2,1)S(1)}, bf16[2,128,128]{2,1,0:T(8,128)(2,1)S(1)}, u32[]{:S(2)}, u32[]{:S(2)}) collective-permute-start(bf16[2,128,128]{2,1,0:T(8,128)(2,1)S(1)} %pad_maximum_fusion), channel_id=1, source_target_pairs={{0,6},{2,4},{4,2},{6,0},{8,14},{10,12},{12,10},{14,8},{16,22},{18,... | collective-permute-start | bytes 196616 | tf_op jit(solution)/shard_map/ppermute | solution.py:222
  11.0 0.5 %collective-permute-done.1.refs_0_ = bf16[2,128,128]{2,1,0:T(8,128)(2,1)S(1)} collective-permute-done((bf16[2,128,128]{2,1,0:T(8,128)(2,1)S(1)}, bf16[2,128,128]{2,1,0:T(8,128)(2,1)S(1)}, u32[]{:S(2)}, u32[]{:S(2)}) %collective-permute-start.1) | collective-permute-done | bytes 65568 | tf_op jit(solution)/shard_map/ppermute | solution.py:222
  11.4 1.2 %collective-permute-start.2 = (bf16[2,128,128]{2,1,0:T(8,128)(2,1)S(1)}, bf16[2,128,128]{2,1,0:T(8,128)(2,1)S(1)}, u32[]{:S(2)}, u32[]{:S(2)}) collective-permute-start(bf16[2,128,128]{2,1,0:T(8,128)(2,1)S(1)} %collective-permute-done.1.refs_0_), channel_id=1, source_target_pairs={{0,6},{2,4},{4,2},{6,0},{8,14},{10,12},{12,10},{14,8},{16,22},{18,... | collective-permute-start | bytes 196616 | tf_op jit(solution)/shard_map/ppermute | solution.py:222
  12.7 1.5 %collective-permute-start.7 = (bf16[4,192,128]{2,1,0:T(8,128)(2,1)S(1)}, bf16[4,192,128]{2,1,0:T(8,128)(2,1)S(1)}, u32[]{:S(2)}, u32[]{:S(2)}) collective-permute-start(bf16[4,192,128]{2,1,0:T(8,128)(2,1)S(1)} %get-tuple-element.45.own_ref), channel_id=1, source_target_pairs={{0,1},{1,0},{2,3},{3,2},{4,5},{5,4},{6,7},{7,6},{8,9},{9,8},{10,11... | collective-permute-start | bytes 589832 | tf_op jit(solution)/shard_map/ppermute | solution.py:259
  14.1 0.0 collective-permute-done.3.refs_0_
  14.1 0.0 collective-permute-done.4.refs_2_.refs_3_
  14.1 1.2 %shard_map.105 = f32[2,128]{1,0:T(2,128)S(1)} custom-call(bf16[2,128,128]{2,1,0:T(8,128)(2,1)S(1)} %collective-permute-done.3.refs_0_, bf16[16,192,128]{2,1,0:T(8,128)(2,1)S(1)} %shard_map.104.refs_1_.refs_2_, bf16[16,192,128]{2,1,0:T(8,128)(2,1)S(1)} %collective-permute-done.4.refs_2_.refs_3_), custom_call_target="tpu_custom_call" | custom-call | flops 402653184 | bytes 1572864 | tf_op jit(solution)/shard_map/pallas_call | solution.py:131
  15.4 0.1 collective-permute-done.2.refs_0_
  15.5 1.2 %shard_map.106 = f32[2,128]{1,0:T(2,128)S(1)} custom-call(bf16[2,128,128]{2,1,0:T(8,128)(2,1)S(1)} %collective-permute-done.2.refs_0_, bf16[16,192,128]{2,1,0:T(8,128)(2,1)S(1)} %shard_map.104.refs_1_.refs_2_, bf16[16,192,128]{2,1,0:T(8,128)(2,1)S(1)} %collective-permute-done.4.refs_2_.refs_3_), custom_call_target="tpu_custom_call" | custom-call | flops 402653184 | bytes 1572864 | tf_op jit(solution)/shard_map/pallas_call | solution.py:131
  16.7 1.6 %collective-permute-start.5 = (f32[1,4,128]{2,0,1:T(1,128)S(1)}, f32[1,4,128]{2,0,1:T(1,128)S(1)}, u32[]{:S(2)}, u32[]{:S(2)}) collective-permute-start(f32[1,4,128]{2,0,1:T(1,128)S(1)} %bitcast.23), channel_id=1, source_target_pairs={{0,6},{2,4},{4,2},{6,0},{8,14},{10,12},{12,10},{14,8},{16,22},{18,... | collective-permute-start | bytes 6152 | tf_op jit(solution)/shard_map/ppermute | solution.py:222
  18.4 1.2 %shard_map.107 = f32[2,128]{1,0:T(2,128)S(1)} custom-call(bf16[2,128,128]{2,1,0:T(8,128)(2,1)S(1)} %collective-permute-done.1.refs_0_, bf16[16,192,128]{2,1,0:T(8,128)(2,1)S(1)} %shard_map.104.refs_1_.refs_2_, bf16[16,192,128]{2,1,0:T(8,128)(2,1)S(1)} %collective-permute-done.4.refs_2_.refs_3_), custom_call_target="tpu_custom_call" | custom-call | flops 402653184 | bytes 1572864 | tf_op jit(solution)/shard_map/pallas_call | solution.py:131
  19.6 0.2 collective-permute-done.5
  19.8 1.4 %collective-permute-start.6 = (f32[2,2,128]{2,0,1:T(2,128)S(1)}, f32[2,2,128]{2,0,1:T(2,128)S(1)}, u32[]{:S(2)}, u32[]{:S(2)}) collective-permute-start(f32[2,2,128]{2,0,1:T(2,128)S(1)} %pad_maximum_fusion.3), channel_id=1, source_target_pairs={{0,10},{2,8},{4,14},{6,12},{8,2},{10,0},{12,6},{14,4},{16,26},{18,... | collective-permute-start | bytes 6152 | tf_op jit(solution)/shard_map/ppermute | solution.py:222
  21.3 0.0 copy-start.7
  21.3 1.2 %shard_map.108.mine_ref = f32[2,128]{1,0:T(2,128)S(1)} custom-call(bf16[1,128,128]{2,1,0:T(8,128)(2,1)S(1)} %bitcast.18, bf16[1,128,128]{2,1,0:T(8,128)(2,1)S(1)} %collective-permute-done.refs_1_, bf16[16,192,128]{2,1,0:T(8,128)(2,1)S(1)} %shard_map.104.refs_1_.refs_2_, bf16[16,192,128]{2,1,0:T(8,128)(2,1)S(1)} %collective-permute-done.4.refs_2_.refs_3_), custom_call_target="tpu_custom_call" | custom-call | flops 402653184 | bytes 1572864 | tf_op jit(solution)/shard_map/pallas_call | solution.py:131
  22.5 0.4 %collective-permute-done.6 = f32[2,2,128]{2,0,1:T(2,128)S(1)} collective-permute-done((f32[2,2,128]{2,0,1:T(2,128)S(1)}, f32[2,2,128]{2,0,1:T(2,128)S(1)}, u32[]{:S(2)}, u32[]{:S(2)}) %collective-permute-start.6) | collective-permute-done | bytes 2080 | tf_op jit(solution)/shard_map/ppermute | solution.py:222
  22.9 0.0 copy-start.6
  22.9 0.0 collective-permute-done.7.other_ref
  22.9 2.5 %collective-permute-start.8 = (f32[4,1,128]{2,0,1:T(4,128)S(1)}, f32[4,1,128]{2,0,1:T(4,128)S(1)}, u32[]{:S(2)}, u32[]{:S(2)}) collective-permute-start(f32[4,1,128]{2,0,1:T(4,128)S(1)} %fusion.1), channel_id=1, source_target_pairs={{0,18},{2,16},{4,22},{6,20},{8,26},{10,24},{12,30},{14,28},{16,2},... | collective-permute-start | bytes 6152 | tf_op jit(solution)/shard_map/ppermute | solution.py:222
  25.5 0.0 copy-done.6
  25.5 0.0 copy-done.7
  25.5 1.1 %shard_map.109 = (f32[1,4]{1,0:T(1,128)}, s32[2,128]{1,0:T(2,128)S(1)}) custom-call(bf16[128,128]{1,0:T(8,128)(2,1)S(1)} %bitcast.19, bf16[4,192,128]{2,1,0:T(8,128)(2,1)S(1)} %get-tuple-element.45.own_ref, bf16[4,192,128]{2,1,0:T(8,128)(2,1)S(1)} %collective-permute-done.7.other_ref, s32[4,32]{1,0:T(4,128)S(1)} %get-tuple-element.58.where_ref, ...), custom_call_target="tpu_custom_call" | custom-call | flops 50331648 | bytes 393216 | tf_op jit(solution)/shard_map/pallas_call | solution.py:173
  26.7 0.3 collective-permute-done.8
  26.9 0.7 %shard_map.110 = (f32[1,4,32]{2,1,0:T(4,128)}, f32[1,4]{1,0:T(1,128)}) custom-call(f32[2,128]{1,0:T(2,128)S(1)} %shard_map.108.mine_ref, f32[7,128]{1,0:T(8,128)S(1)} %maximum_bitcast_fusion.back_ref, f32[3,128]{1,0:T(4,128)S(1)} %get-tuple-element.52.teach_ref, s32[2,128]{1,0:T(2,128)S(1)} %get-tuple-element.53.index_ref), custom_call_target="tpu_custom_call" | custom-call | tf_op jit(solution)/shard_map/pallas_call | solution.py:209
  (10 shorter events, 0.1 us)
Async XLA Ops:
  0.6 3.6 %copy-start.2 = (s32[1,16]{1,0:T(1,128)S(1)}, s32[1,16]{1,0:T(1,128)}, u32[]{:S(2)}) copy-start(s32[1,16]{1,0:T(1,128)} %kept_ref.3) | copy-start | bytes 196
  0.6 6.5 %collective-permute-start = (bf16[1,128,128]{2,1,0:T(8,128)(2,1)}, bf16[1,128,128]{2,1,0:T(8,128)(2,1)S(1)}, u32[]{:S(2)}, u32[]{:S(2)}) collective-permute-start(bf16[1,128,128]{2,1,0:T(8,128)(2,1)} %bitcast.16), channel_id=1, source_target_pairs={{0,18},{2,16},{4,22},{6,20},{8,26},{10,24},{12,30},{14,28},{16,2},... | collective-permute-start | bytes 98312 | tf_op jit(solution)/shard_map/ppermute | solution.py:222
  4.2 1.1 %copy-start = (bf16[1,16,192,128]{3,2,1,0:T(8,128)(2,1)S(1)}, bf16[1,16,192,128]{3,2,1,0:T(8,128)(2,1)}, u32[]{:S(2)}) copy-start(bf16[1,16,192,128]{3,2,1,0:T(8,128)(2,1)} %param.9) | copy-start | bytes 2359300
  5.3 1.8 %copy-start.1 = (bf16[1,4,32,128]{3,2,1,0:T(8,128)(2,1)S(1)}, bf16[1,4,32,128]{3,2,1,0:T(8,128)(2,1)}, u32[]{:S(2)}) copy-start(bf16[1,4,32,128]{3,2,1,0:T(8,128)(2,1)} %param.8) | copy-start | bytes 98308
  5.3 3.1 %copy-start.3 = (bf16[1,4,192,128]{3,2,1,0:T(8,128)(2,1)S(1)}, bf16[1,4,192,128]{3,2,1,0:T(8,128)(2,1)}, u32[]{:S(2)}) copy-start(bf16[1,4,192,128]{3,2,1,0:T(8,128)(2,1)} %param.11) | copy-start | bytes 589828
  6.4 2.1 %copy-start.4 = (f32[1,4,32]{2,1,0:T(4,128)S(1)}, f32[1,4,32]{2,1,0:T(4,128)}, u32[]{:S(2)}) copy-start(f32[1,4,32]{2,1,0:T(4,128)} %teacher_ref.1) | copy-start | bytes 1540
  6.4 7.8 %collective-permute-start.4 = (bf16[16,192,128]{2,1,0:T(8,128)(2,1)S(1)}, bf16[16,192,128]{2,1,0:T(8,128)(2,1)S(1)}, u32[]{:S(2)}, u32[]{:S(2)}) collective-permute-start(bf16[16,192,128]{2,1,0:T(8,128)(2,1)S(1)} %shard_map.104.refs_1_.refs_2_), channel_id=1, source_target_pairs={{0,2},{2,0},{4,6},{6,4},{8,10},{10,8},{12,14},{14,12},{16,18},{18,... | collective-permute-start | bytes 2359304 | tf_op jit(solution)/shard_map/ppermute | solution.py:222
  7.2 1.3 %copy-start.5 = (s32[1,4]{1,0:T(1,128)S(1)}, s32[1,4]{1,0:T(1,128)}, u32[]{:S(2)}) copy-start(s32[1,4]{1,0:T(1,128)} %kept_ref.2) | copy-start | bytes 52
  7.2 4.2 %collective-permute-start.1 = (bf16[2,128,128]{2,1,0:T(8,128)(2,1)S(1)}, bf16[2,128,128]{2,1,0:T(8,128)(2,1)S(1)}, u32[]{:S(2)}, u32[]{:S(2)}) collective-permute-start(bf16[2,128,128]{2,1,0:T(8,128)(2,1)S(1)} %pad_maximum_fusion), channel_id=1, source_target_pairs={{0,10},{2,8},{4,14},{6,12},{8,2},{10,0},{12,6},{14,4},{16,26},{18,... | collective-permute-start | bytes 196616 | tf_op jit(solution)/shard_map/ppermute | solution.py:222
  9.3 4.8 %collective-permute-start.3 = (bf16[2,128,128]{2,1,0:T(8,128)(2,1)S(1)}, bf16[2,128,128]{2,1,0:T(8,128)(2,1)S(1)}, u32[]{:S(2)}, u32[]{:S(2)}) collective-permute-start(bf16[2,128,128]{2,1,0:T(8,128)(2,1)S(1)} %pad_maximum_fusion), channel_id=1, source_target_pairs={{0,6},{2,4},{4,2},{6,0},{8,14},{10,12},{12,10},{14,8},{16,22},{18,... | collective-permute-start | bytes 196616 | tf_op jit(solution)/shard_map/ppermute | solution.py:222
  11.4 4.1 %collective-permute-start.2 = (bf16[2,128,128]{2,1,0:T(8,128)(2,1)S(1)}, bf16[2,128,128]{2,1,0:T(8,128)(2,1)S(1)}, u32[]{:S(2)}, u32[]{:S(2)}) collective-permute-start(bf16[2,128,128]{2,1,0:T(8,128)(2,1)S(1)} %collective-permute-done.1.refs_0_), channel_id=1, source_target_pairs={{0,6},{2,4},{4,2},{6,0},{8,14},{10,12},{12,10},{14,8},{16,22},{18,... | collective-permute-start | bytes 196616 | tf_op jit(solution)/shard_map/ppermute | solution.py:222
  12.7 10.3 %collective-permute-start.7 = (bf16[4,192,128]{2,1,0:T(8,128)(2,1)S(1)}, bf16[4,192,128]{2,1,0:T(8,128)(2,1)S(1)}, u32[]{:S(2)}, u32[]{:S(2)}) collective-permute-start(bf16[4,192,128]{2,1,0:T(8,128)(2,1)S(1)} %get-tuple-element.45.own_ref), channel_id=1, source_target_pairs={{0,1},{1,0},{2,3},{3,2},{4,5},{5,4},{6,7},{7,6},{8,9},{9,8},{10,11... | collective-permute-start | bytes 589832 | tf_op jit(solution)/shard_map/ppermute | solution.py:259
  16.7 3.1 %collective-permute-start.5 = (f32[1,4,128]{2,0,1:T(1,128)S(1)}, f32[1,4,128]{2,0,1:T(1,128)S(1)}, u32[]{:S(2)}, u32[]{:S(2)}) collective-permute-start(f32[1,4,128]{2,0,1:T(1,128)S(1)} %bitcast.23), channel_id=1, source_target_pairs={{0,6},{2,4},{4,2},{6,0},{8,14},{10,12},{12,10},{14,8},{16,22},{18,... | collective-permute-start | bytes 6152 | tf_op jit(solution)/shard_map/ppermute | solution.py:222
  19.8 3.1 %collective-permute-start.6 = (f32[2,2,128]{2,0,1:T(2,128)S(1)}, f32[2,2,128]{2,0,1:T(2,128)S(1)}, u32[]{:S(2)}, u32[]{:S(2)}) collective-permute-start(f32[2,2,128]{2,0,1:T(2,128)S(1)} %pad_maximum_fusion.3), channel_id=1, source_target_pairs={{0,10},{2,8},{4,14},{6,12},{8,2},{10,0},{12,6},{14,4},{16,26},{18,... | collective-permute-start | bytes 6152 | tf_op jit(solution)/shard_map/ppermute | solution.py:222
  21.3 4.2 %copy-start.7 = (s32[1,4,32]{2,1,0:T(4,128)S(1)}, s32[1,4,32]{2,1,0:T(4,128)}, u32[]{:S(2)}) copy-start(s32[1,4,32]{2,1,0:T(4,128)} %param.14) | copy-start | bytes 1540
  22.9 2.6 %copy-start.6 = (s32[1,4,32,1]{2,3,1,0:T(1,128)S(1)}, s32[1,4,32,1]{2,3,1,0:T(1,128)}, u32[]{:S(2)}) copy-start(s32[1,4,32,1]{2,3,1,0:T(1,128)} %param.13) | copy-start | bytes 1540
  22.9 4.0 %collective-permute-start.8 = (f32[4,1,128]{2,0,1:T(4,128)S(1)}, f32[4,1,128]{2,0,1:T(4,128)S(1)}, u32[]{:S(2)}, u32[]{:S(2)}) collective-permute-start(f32[4,1,128]{2,0,1:T(4,128)S(1)} %fusion.1), channel_id=1, source_target_pairs={{0,18},{2,16},{4,22},{6,20},{8,26},{10,24},{12,30},{14,28},{16,2},... | collective-permute-start | bytes 6152 | tf_op jit(solution)/shard_map/ppermute | solution.py:222
